TPU v7x, 32 devices: a whole 2x2x4 slice. The times are simulated.
32 devices in a mesh: dp: 16 (over z, y, core), ctx: 2 (over x).
Axes of the slice: x: 2, y: 2, z: 4, core: 2. Of those that a mesh axis runs over, the one named last changes fastest.
Arguments:
- block_input: bfloat16 [48, 512, 1024], P('dp', 'ctx'), may hold values from -6 to 6
- lengths: int32 [48], P('dp'), may hold values from 1 to 512, as said below
- mask: int32 [48, 512], P('dp', 'ctx'), may hold values 0 or 1
- blocks: int32 [48, 512], P('dp', 'ctx'), may hold values from 0 to 22, never falling along the last dimension, each value on 1 to 25 neighbouring positions
- timesteps: int32 [48], P('dp'), may hold values from 0 to 4999
- w_qkv: bfloat16 [1024, 3072], P(('dp', 'ctx')), may hold values from -0.1875 to 0.1875
- w_o: bfloat16 [1024, 1024], P(('dp', 'ctx')), may hold values from -1.5 to 1.5
- w_in: bfloat16 [1024, 4096], P(('dp', 'ctx')), may hold values from -0.1875 to 0.1875
- w_out: bfloat16 [4096, 1024], P(('dp', 'ctx')), may hold values from -0.09375 to 0.09375
- b_in: bfloat16 [4096], P(('dp', 'ctx')), may hold values from -3 to 3
- biases: bfloat16 [4, 1024], P(None, ('dp', 'ctx')), may hold values from -3 to 3
- gains: bfloat16 [2, 1024], P(None, ('dp', 'ctx')), may hold values from 0.5 to 1.5
- shifts: bfloat16 [2, 1024], P(None, ('dp', 'ctx')), may hold values from -2 to 2
- cotangent: bfloat16 [48, 512, 1024], P('dp', 'ctx'), may hold values from -6 to 6
Outputs:
- output: bfloat16 [48, 512, 1024], P('dp', 'ctx')
- input_grad: bfloat16 [48, 512, 1024], P('dp', 'ctx')
- grad_w_qkv: float32 [1024, 3072], P(('dp', 'ctx'))
- grad_w_o: float32 [1024, 1024], P(('dp', 'ctx'))
- grad_w_in: float32 [1024, 4096], P(('dp', 'ctx'))
- grad_w_out: float32 [4096, 1024], P(('dp', 'ctx'))
- grad_b_in: float32 [4096], P(('dp', 'ctx'))
- grad_biases: float32 [4, 1024], P(None, ('dp', 'ctx'))
- grad_gains: float32 [2, 1024], P(None, ('dp', 'ctx'))
- grad_shifts: float32 [2, 1024], P(None, ('dp', 'ctx'))
- rms: float32 [4], replicated
Inputs may be any that keep to these rules, and one draw needn't show every extreme that they name: `lengths`: in every aligned group of 3 items one item has length 512.
All inputs are finite; a program needn't handle non-finite values. No bound on the sum of `mask` on one device may be relied on, other than what follows from the above.
Results may differ from a plain program's by a relative error of at most 0.018.
Values may be sent and summed in bfloat16 or wider, within the bound.
A program may use at most 192 MiB of HBM per device.

v0:
```python
from functools import partial
import math

import jax
import jax.numpy as jnp
from jax import lax
from jax.sharding import PartitionSpec as P

HEADS = 16
HD = 64


fill_value = -1e30
eps_norm = 1e-05
code_absent = 30000.0


def time_embed(steps, width):
    half = width // 2
    freqs = jnp.exp(jnp.arange(half, dtype=jnp.float32) * (-math.log(10000.0) / half))
    angle = steps.astype(jnp.float32)[:, None] * freqs[None, :]
    return jnp.concatenate([jnp.sin(angle), jnp.cos(angle)], axis=-1)


def layer_norm(resid, gain, shift):
    centre = resid - jnp.mean(resid, axis=-1, keepdims=True)
    spread = jnp.mean(centre * centre, axis=-1, keepdims=True)
    return centre * lax.rsqrt(spread + eps_norm) * gain + shift


def inner(left, right):
    return lax.dot_general(
        left, right, (((0,), (0,)), ((), ())), preferred_element_type=jnp.float32
    )


def back_project(grad, weight):
    return lax.dot_general(
        grad, weight, (((1,), (1,)), ((), ())), preferred_element_type=jnp.float32
    )


def scores_of(query, keys, code_row, query_block, positions):
    key_pos = jnp.arange(code_row.shape[0], dtype=jnp.int32)
    permit = (code_row.astype(jnp.float32)[None, :] <= query_block[:, None]) | (
        key_pos[None, :] == positions[:, None]
    )
    raw = jnp.einsum("qhd,khd->hqk", query, keys, preferred_element_type=jnp.float32) * (
        1.0 / math.sqrt(HD)
    )
    return jnp.where(permit[None], raw, fill_value)


def body(
    block_input,
    lengths,
    mask,
    blocks,
    timesteps,
    w_qkv,
    w_o,
    w_in,
    w_out,
    b_in,
    biases,
    gains,
    shifts,
    cotangent,
):
    items, half_len, width = block_input.shape
    full_len = half_len * lax.axis_size("ctx")
    rows = items * half_len
    positions = lax.axis_index("ctx") * half_len + jnp.arange(half_len, dtype=jnp.int32)
    valid = (positions[None, :] < lengths[:, None]) & ((mask == 1) | (positions[None, :] == 0))
    stream = (block_input.astype(jnp.float32) + time_embed(timesteps, width)[:, None, :]).reshape(
        rows, width
    )
    w_qkv_all, w_o_all, w_in_all, w_out_all, b_in_all, bias_all, gain_all, shift_all = (
        lax.all_gather(w_qkv, ("dp", "ctx"), axis=0, tiled=True),
        lax.all_gather(w_o, ("dp", "ctx"), axis=0, tiled=True),
        lax.all_gather(w_in, ("dp", "ctx"), axis=0, tiled=True),
        lax.all_gather(w_out, ("dp", "ctx"), axis=0, tiled=True),
        lax.all_gather(b_in, ("dp", "ctx"), axis=0, tiled=True),
        lax.all_gather(biases, ("dp", "ctx"), axis=1, tiled=True),
        lax.all_gather(gains, ("dp", "ctx"), axis=1, tiled=True),
        lax.all_gather(shifts, ("dp", "ctx"), axis=1, tiled=True),
    )
    bias_full = bias_all.astype(jnp.float32)
    gain_full = gain_all.astype(jnp.float32)
    shift_full = shift_all.astype(jnp.float32)
    b_in_full = b_in_all.astype(jnp.float32)
    stream_low = stream.astype(jnp.bfloat16)
    joint = jnp.dot(stream_low, w_qkv_all, preferred_element_type=jnp.float32)
    query_low = (joint[:, :width] + bias_full[0]).astype(jnp.bfloat16)
    key_low = joint[:, width : 2 * width].astype(jnp.bfloat16)
    value_low = (joint[:, 2 * width :] + bias_full[1]).astype(jnp.bfloat16)
    code_local = jnp.where(valid, blocks.astype(jnp.float32), code_absent).astype(jnp.bfloat16)
    key_all, value_all, code_all = (
        lax.all_gather(key_low.reshape(items, half_len, width), "ctx", axis=1, tiled=True),
        lax.all_gather(value_low.reshape(items, half_len, width), "ctx", axis=1, tiled=True),
        lax.all_gather(code_local, "ctx", axis=1, tiled=True),
    )
    query_block = blocks.astype(jnp.float32)
    query_four = query_low.reshape(items, half_len, HEADS, HD)
    key_four = key_all.reshape(items, full_len, HEADS, HD)
    value_four = value_all.reshape(items, full_len, HEADS, HD)

    def attend(inputs):
        query, keys, values, code_row, block_row = inputs
        scores = scores_of(query, keys, code_row, block_row, positions)
        peak = jnp.max(scores, axis=-1, keepdims=True)
        expo = jnp.exp(scores - peak)
        total = jnp.sum(expo, axis=-1, keepdims=True)
        probs = expo / total
        mixed = jnp.einsum(
            "hqk,khd->qhd", probs.astype(jnp.bfloat16), values, preferred_element_type=jnp.float32
        )
        return (mixed, (peak + jnp.log(total))[..., 0])

    mixed_all, log_totals = lax.map(
        attend, (query_four, key_four, value_four, code_all, query_block)
    )
    mixed_low = mixed_all.reshape(rows, width).astype(jnp.bfloat16)
    attn = jnp.dot(mixed_low, w_o_all, preferred_element_type=jnp.float32) + bias_full[2]
    resid_one = stream + attn
    hidden_one = layer_norm(resid_one, gain_full[0], shift_full[0])
    hidden_low = hidden_one.astype(jnp.bfloat16)
    pre = jnp.dot(hidden_low, w_in_all, preferred_element_type=jnp.float32) + b_in_full
    act_low = jax.nn.gelu(pre, approximate=False).astype(jnp.bfloat16)
    branch = jnp.dot(act_low, w_out_all, preferred_element_type=jnp.float32) + bias_full[3]
    resid_two = hidden_one + branch
    result = layer_norm(resid_two, gain_full[1], shift_full[1])
    output = result.astype(jnp.bfloat16).reshape(items, half_len, width)
    row_weight = valid.reshape(rows).astype(jnp.float32)
    local_sums = jnp.stack(
        [
            jnp.sum(row_weight * jnp.sum(tensor * tensor, axis=-1))
            for tensor in (stream, attn, branch, result)
        ]
        + [jnp.sum(row_weight)]
    )
    totals = lax.psum(local_sums, ("dp", "ctx"))
    rms = jnp.sqrt(totals[:4] / (totals[4] * width))
    w_qkv_back, w_o_back, w_in_back, w_out_back = (
        lax.all_gather(w_qkv, ("dp", "ctx"), axis=0, tiled=True),
        lax.all_gather(w_o, ("dp", "ctx"), axis=0, tiled=True),
        lax.all_gather(w_in, ("dp", "ctx"), axis=0, tiled=True),
        lax.all_gather(w_out, ("dp", "ctx"), axis=0, tiled=True),
    )
    _, norm_two_back = jax.vjp(layer_norm, resid_two, gain_full[1], shift_full[1])
    dres_two, gain_two_grad, shift_two_grad = norm_two_back(
        cotangent.reshape(rows, width).astype(jnp.float32)
    )
    branch_grad = dres_two.astype(jnp.bfloat16)
    grad_out_part = inner(act_low, branch_grad)
    act_grad = back_project(branch_grad, w_out_back)
    _, gelu_back = jax.vjp(partial(jax.nn.gelu, approximate=False), pre)
    pre_grad = gelu_back(act_grad)[0].astype(jnp.bfloat16)
    grad_in_part = inner(hidden_low, pre_grad)
    dhidden = dres_two + back_project(pre_grad, w_in_back)
    _, norm_one_back = jax.vjp(layer_norm, resid_one, gain_full[0], shift_full[0])
    dres_one, gain_one_grad, shift_one_grad = norm_one_back(dhidden)
    attn_grad = dres_one.astype(jnp.bfloat16)
    grad_o_part = inner(mixed_low, attn_grad)
    mixed_grad = (
        back_project(attn_grad, w_o_back).astype(jnp.bfloat16).reshape(items, half_len, HEADS, HD)
    )

    def attend_back(inputs):
        query, keys, values, code_row, block_row, log_row, grad_row = inputs
        scores = scores_of(query, keys, code_row, block_row, positions)
        probs = jnp.exp(scores - log_row[..., None])
        value_part = jnp.einsum(
            "hqk,qhd->khd", probs.astype(jnp.bfloat16), grad_row, preferred_element_type=jnp.float32
        )
        prob_grad = jnp.einsum("qhd,khd->hqk", grad_row, values, preferred_element_type=jnp.float32)
        centre = jnp.sum(probs * prob_grad, axis=-1, keepdims=True)
        score_grad = (probs * (prob_grad - centre)).astype(jnp.bfloat16)
        query_part = jnp.einsum(
            "hqk,khd->qhd", score_grad, keys, preferred_element_type=jnp.float32
        ) * (1.0 / math.sqrt(HD))
        key_part = jnp.einsum(
            "hqk,qhd->khd", score_grad, query, preferred_element_type=jnp.float32
        ) * (1.0 / math.sqrt(HD))
        return (query_part, key_part, value_part)

    query_part, key_part, value_part = lax.map(
        attend_back,
        (query_four, key_four, value_four, code_all, query_block, log_totals, mixed_grad),
    )
    key_grad, value_grad = (
        lax.psum_scatter(
            key_part.reshape(items, full_len, width).astype(jnp.bfloat16),
            "ctx",
            scatter_dimension=1,
            tiled=True,
        ).astype(jnp.float32),
        lax.psum_scatter(
            value_part.reshape(items, full_len, width).astype(jnp.bfloat16),
            "ctx",
            scatter_dimension=1,
            tiled=True,
        ).astype(jnp.float32),
    )
    query_grad_low = query_part.reshape(rows, width).astype(jnp.bfloat16)
    key_grad_low = key_grad.reshape(rows, width).astype(jnp.bfloat16)
    value_grad_low = value_grad.reshape(rows, width).astype(jnp.bfloat16)
    joint_grad = jnp.concatenate([query_grad_low, key_grad_low, value_grad_low], axis=1)
    grad_qkv_part = inner(stream_low, joint_grad)
    input_grad = (
        (dres_one + back_project(joint_grad, w_qkv_back))
        .astype(jnp.bfloat16)
        .reshape(items, half_len, width)
    )
    b_in_part = jnp.sum(pre_grad.astype(jnp.float32), axis=0)
    bias_part = jnp.stack(
        [
            jnp.sum(query_grad_low.astype(jnp.float32), axis=0),
            jnp.sum(value_grad_low.astype(jnp.float32), axis=0),
            jnp.sum(attn_grad.astype(jnp.float32), axis=0),
            jnp.sum(branch_grad.astype(jnp.float32), axis=0),
        ]
    )
    gain_part = jnp.stack([gain_one_grad, gain_two_grad])
    shift_part = jnp.stack([shift_one_grad, shift_two_grad])
    grad_qkv, grad_o, grad_in, grad_out, grad_b_in, grad_bias, grad_gain, grad_shift = (
        lax.psum_scatter(grad_qkv_part, ("dp", "ctx"), scatter_dimension=0, tiled=True),
        lax.psum_scatter(grad_o_part, ("dp", "ctx"), scatter_dimension=0, tiled=True),
        lax.psum_scatter(grad_in_part, ("dp", "ctx"), scatter_dimension=0, tiled=True),
        lax.psum_scatter(grad_out_part, ("dp", "ctx"), scatter_dimension=0, tiled=True),
        lax.psum_scatter(b_in_part, ("dp", "ctx"), scatter_dimension=0, tiled=True),
        lax.psum_scatter(bias_part, ("dp", "ctx"), scatter_dimension=1, tiled=True),
        lax.psum_scatter(gain_part, ("dp", "ctx"), scatter_dimension=1, tiled=True),
        lax.psum_scatter(shift_part, ("dp", "ctx"), scatter_dimension=1, tiled=True),
    )
    return (
        output,
        input_grad,
        grad_qkv,
        grad_o,
        grad_in,
        grad_out,
        grad_b_in,
        grad_bias,
        grad_gain,
        grad_shift,
        rms,
    )


def solution(mesh):
    in_specs = (
        P("dp", "ctx", None),
        P("dp"),
        P("dp", "ctx"),
        P("dp", "ctx"),
        P("dp"),
        P(("dp", "ctx"), None),
        P(("dp", "ctx"), None),
        P(("dp", "ctx"), None),
        P(("dp", "ctx"), None),
        P(("dp", "ctx")),
        P(None, ("dp", "ctx")),
        P(None, ("dp", "ctx")),
        P(None, ("dp", "ctx")),
        P("dp", "ctx", None),
    )
    out_specs = (
        P("dp", "ctx", None),
        P("dp", "ctx", None),
        P(("dp", "ctx"), None),
        P(("dp", "ctx"), None),
        P(("dp", "ctx"), None),
        P(("dp", "ctx"), None),
        P(("dp", "ctx")),
        P(None, ("dp", "ctx")),
        P(None, ("dp", "ctx")),
        P(None, ("dp", "ctx")),
        P(),
    )
    return jax.shard_map(body, mesh=mesh, in_specs=in_specs, out_specs=out_specs, check_vma=False)
```

profile of v0, /device:TPU:0, one launch (start us, length us, event | category | flops | bytes accessed | tf_op | source)
XLA Modules:
  0.0 2051.7 jit_solution(16470153449754659117)
XLA Ops:
  8.6 70.2 %all-gather = bf16[32,32,4]{1,2,0:T(4,128)(2,1)S(1)} all-gather(bf16[1,32,4]{1,2,0:T(4,128)(2,1)} %bitcast.265), channel_id=1, replica_groups=mesh['dp'=16,'ctx'=2] {'dp','ctx'}, dimensions={0}, use_global_device_ids=true | all-gather | bytes 8448 | tf_op jit(solution)/shard_map/all_gather | solution.py:84
  79.7 2.6 multiply_reduce_fusion.4
  84.1 7.7 fusion.89
  91.8 3.1 fusion.63
  96.6 3.3 slice.74
  102.4 4.3 all_gather.40
  106.8 63.0 %all-gather.1 = bf16[32,32,2]{1,2,0:T(2,128)(2,1)S(1)} all-gather(bf16[1,32,2]{1,2,0:T(2,128)(2,1)S(1)} %bitcast.266), channel_id=1, replica_groups=mesh['dp'=16,'ctx'=2] {'dp','ctx'}, dimensions={0}, use_global_device_ids=true | all-gather | bytes 4224 | tf_op jit(solution)/shard_map/all_gather | solution.py:85
  170.5 65.2 %all-gather.2 = bf16[32,32,2]{1,2,0:T(2,128)(2,1)S(1)} all-gather(bf16[1,32,2]{1,2,0:T(2,128)(2,1)S(1)} %bitcast.267), channel_id=1, replica_groups=mesh['dp'=16,'ctx'=2] {'dp','ctx'}, dimensions={0}, use_global_device_ids=true | all-gather | bytes 4224 | tf_op jit(solution)/shard_map/all_gather | solution.py:86
  236.4 63.3 %all-gather.3 = bf16[32,1,128]{2,1,0:T(2,128)(2,1)S(1)} all-gather(bf16[1,1,128]{2,1,0:T(2,128)(2,1)S(1)} %bitcast.268), channel_id=1, replica_groups=mesh['dp'=16,'ctx'=2] {'dp','ctx'}, dimensions={0}, use_global_device_ids=true | all-gather | bytes 8448 | tf_op jit(solution)/shard_map/all_gather | solution.py:83
  299.7 4.1 reshape.323
  303.8 3.3 copy.82
  307.2 4.7 copy.79
  311.8 3.3 copy.81
  316.5 31.2 %while.28 = (s32[]{:T(128)}, bf16[3,256,16,64]{1,3,2,0:T(8,128)(2,1)}, f32[3,16,256]{2,1,0:T(8,128)}, bf16[3,512,16,64]{1,3,2,0:T(8,128)(2,1)}, bf16[3,512]{1,0:...) while((s32[]{:T(128)}, ...), condition=%wide.region_3.4_spmd.clone, body=%wide.region_0.3_spmd.clone.sunk | while | flops 562426624 | bytes 29504112 | solution.py:120
  316.6 2.8 fusion.133
  319.4 2.2 fusion.134
  322.3 4.6 fusion.135
  327.1 2.8 fusion.133
  332.7 4.6 fusion.135
  337.5 2.8 fusion.133
  340.2 2.2 fusion.134
  343.1 4.5 fusion.135
  347.7 3.9 copy.83
  353.1 5.9 fusion.85
  359.5 39.4 %multiply_convert_fusion.1 = (bf16[768,4096]{1,0:T(8,128)(2,1)}, f32[768,4096]{1,0:T(8,128)}, f32[768,4096]{1,0:T(8,128)}) fusion(f32[4096]{0:T(1024)S(1)} %bitcast.257, bf16[1024,4096]{1,0:T(8,128)(2,1)} %all-gather.19.cloned.1.call-done, f32[768,1024]{1,0:T(8,128)S(1)} %get-tuple-element.351, f32[1024]{0:T(1024)S(1)} %bitcast.236, ...), kind=kOutput, calls=%fused_computation.75 | convolution fusion | flops 6654001152 | bytes 43022336 | tf_op jit(solution)/shard_map/dot_general | solution.py:128
  398.9 4.0 all-gather.21.cloned.1.call-done
  402.9 12.6 fusion.83
  416.9 3.4 fusion.68
  425.2 21.1 %convert_reduce_fusion = (f32[4096]{0:T(1024)}, bf16[768,4096]{1,0:T(8,128)(2,1)}) fusion(f32[768,4096]{1,0:T(8,128)} %get-tuple-element.349, f32[768,4096]{1,0:T(8,128)} %get-tuple-element.375, f32[4096]{0:T(1024)S(1)} %bitcast.258, bf16[768,1024]{1,0:T(8,128)(2,1)} %get-tuple-element.339, bf16[4096,1024]{1,0:T(8,128)(2,1)} %all-gather.21.cloned.1.call-done), kind=kOutput, calls=%fused_computation.73 | convolution fusion | flops 6495924224 | bytes 41451520 | tf_op jit(solution)/shard_map/dot_general | solution.py:38
  446.2 12.5 multiply_reduce_fusion.5
  464.7 3.3 reshape.316
  468.0 5.1 copy.88
  474.4 60.2 %while.29 = (s32[]{:T(128)}, bf16[3,256,16,64]{1,3,2,0:T(8,128)(2,1)}, bf16[3,512,16,64]{1,3,2,0:T(8,128)(2,1)}, bf16[3,512,16,64]{1,3,2,0:T(8,128)(2,1)}, bf16[...) while((s32[]{:T(128)}, ...), condition=%wide.region_14.15_spmd.clone, body=%wide.region_12.14_spmd.clone.sunk | while | flops 1374810880 | bytes 92929240 | solution.py:187
  475.3 2.5 fusion.144
  478.5 4.7 multiply_reduce_fusion.10
  483.2 2.4 multiply_convert_fusion.3
  485.7 3.0 bitcast_dynamic-update-slice_fusion.7
  491.3 3.3 bitcast_dynamic-update-slice_fusion.8
  495.4 2.5 fusion.144
  498.6 4.7 multiply_reduce_fusion.10
  503.3 2.4 multiply_convert_fusion.3
  505.8 3.0 bitcast_dynamic-update-slice_fusion.7
  511.3 3.3 bitcast_dynamic-update-slice_fusion.8
  515.4 2.5 fusion.144
  518.6 4.7 multiply_reduce_fusion.10
  523.4 2.4 multiply_convert_fusion.3
  525.8 3.0 bitcast_dynamic-update-slice_fusion.7
  531.3 3.3 bitcast_dynamic-update-slice_fusion.8
  538.9 37.8 %reduce-scatter.18.cloned.1.call-done = bf16[3,256,1024]{1,2,0:T(8,128)(2,1)} async-done(((bf16[3,512,1024]{1,2,0:T(8,128)(2,1)}), bf16[3,256,1024]{1,2,0:T(8,128)(2,1)}) %reduce-scatter.18.cloned.1.call-update) | async-done | bytes 1572880 | tf_op jit(solution)/shard_map/reduce_scatter | solution.py:198
  579.8 5.2 fusion.90
  588.0 34.4 %reduce-scatter.16.cloned.1.call-done = bf16[3,256,1024]{1,2,0:T(8,128)(2,1)} async-done(((bf16[3,512,1024]{1,2,0:T(8,128)(2,1)}), bf16[3,256,1024]{1,2,0:T(8,128)(2,1)}) %reduce-scatter.16.cloned.1.call-update) | async-done | bytes 1572880 | tf_op jit(solution)/shard_map/reduce_scatter | solution.py:192
  628.2 11.9 fusion.71
  641.5 13.0 fusion.91
  656.5 13.3 fusion.77
  671.2 3.3 stack.55
  674.5 39.6 %all-reduce.1 = (f32[4096]{0:T(1024)S(1)}, f32[5]{0:T(128)S(1)}) all-reduce(f32[4096]{0:T(1024)S(1)} %copy-done.36, f32[5]{0:T(128)S(1)} %stack.55), channel_id=8, replica_groups=mesh['dp'=16,'ctx'=2] {'dp','ctx'}, use_global_device_ids=true, to_apply=%region_22.23.clone | all-reduce | flops 4101 | bytes 32808
  716.5 42.4 %reduce-scatter.30.cloned.1.call-done = f32[32,2]{1,0:T(8,128)} async-done(((f32[1024,2]{1,0:T(8,128)}), f32[32,2]{1,0:T(8,128)}) %reduce-scatter.30.cloned.1.call-update) | async-done | bytes 272
  760.2 130.8 %reduce-scatter.32.cloned.1.call-done = f32[32,2]{1,0:T(8,128)} async-done(((f32[1024,2]{1,0:T(8,128)}), f32[32,2]{1,0:T(8,128)}) %reduce-scatter.32.cloned.1.call-update) | async-done | bytes 272
  892.4 9.9 add_convert_fusion.1
  902.3 121.0 %reduce-scatter.28.cloned.1.call-done = f32[32,4]{1,0:T(8,128)} async-done(((f32[1024,4]{1,0:T(8,128)}), f32[32,4]{1,0:T(8,128)}) %reduce-scatter.28.cloned.1.call-update) | async-done | bytes 528
  1024.6 139.4 %reduce-scatter.22.cloned.1.call-done = f32[32,1024]{1,0:T(8,128)} async-done(((f32[1024,1024]{1,0:T(8,128)}), f32[32,1024]{1,0:T(8,128)}) %reduce-scatter.22.cloned.1.call-update) | async-done | bytes 131088 | tf_op jit(solution)/shard_map/reduce_scatter | solution.py:228
  1164.0 160.2 %reduce-scatter.20.cloned.1.call-done = f32[32,3072]{1,0:T(8,128)} async-done(((f32[1024,3072]{1,0:T(8,128)}), f32[32,3072]{1,0:T(8,128)}) %reduce-scatter.20.cloned.1.call-update) | async-done | bytes 393232 | tf_op jit(solution)/shard_map/reduce_scatter | solution.py:227
  1324.2 359.2 %reduce-scatter.26.cloned.1.call-done = f32[128,1024]{1,0:T(8,128)} async-done(((f32[4096,1024]{1,0:T(8,128)}), f32[128,1024]{1,0:T(8,128)}) %reduce-scatter.26.cloned.1.call-update) | async-done | bytes 524304 | tf_op jit(solution)/shard_map/reduce_scatter | solution.py:230
  1683.4 361.4 %reduce-scatter.24.cloned.1.call-done = f32[32,4096]{1,0:T(8,128)} async-done(((f32[1024,4096]{1,0:T(8,128)}), f32[32,4096]{1,0:T(8,128)}) %reduce-scatter.24.cloned.1.call-update) | async-done | bytes 524304 | tf_op jit(solution)/shard_map/reduce_scatter | solution.py:229
  (251 shorter events, 69.7 us)
Async XLA Ops:
  7.2 77.0 %all-gather.11.cloned.1.call-start = ((), (), s32[]{:S(2)}) async-start(), calls=%async_computation.9 | async-start | bytes 6488064 | tf_op jit(solution)/shard_map/all_gather | solution.py:79
  7.9 299.3 %all-gather.13.cloned.1.call-start = ((), (), s32[]{:S(2)}) async-start(), calls=%async_computation.10 | async-start | bytes 4718592 | tf_op jit(solution)/shard_map/all_gather | solution.py:100
  82.2 1.7 copy-start.12
  84.1 7.7 copy-start.18
  91.8 4.6 copy-start.14
  96.5 5.3 copy-start.37
  96.5 5.3 copy-start.42
  96.5 5.3 copy-start.50
  96.5 10.3 copy-start.47
  96.5 74.0 %copy-start.48 = (bf16[2,32]{1,0:T(2,128)(2,1)S(1)}, bf16[2,32]{1,0:T(2,128)(2,1)}, u32[]{:S(2)}) copy-start(bf16[2,32]{1,0:T(2,128)(2,1)} %param.30) | copy-start | bytes 388
  96.5 139.9 %copy-start.49 = (bf16[128]{0:T(256)(128)(2,1)S(1)}, bf16[128]{0:T(256)(128)(2,1)}, u32[]{:S(2)}) copy-start(bf16[128]{0:T(256)(128)(2,1)} %param.27) | copy-start | bytes 772
  96.5 215.3 %all-gather.15.cloned.1.call-start = ((), (), s32[]{:S(2)}) async-start(), calls=%async_computation.11 | async-start | bytes 4718592 | tf_op jit(solution)/shard_map/all_gather | solution.py:99
  99.9 253.2 %all-gather.17.cloned.1.call-start = ((), (), s32[]{:S(2)}) async-start(), calls=%async_computation.12 | async-start | bytes 2162688 | tf_op jit(solution)/shard_map/all_gather | solution.py:80
  100.5 259.0 %all-gather.19.cloned.1.call-start = ((), (), s32[]{:S(2)}) async-start(), calls=%async_computation.13 | async-start | bytes 8650752 | tf_op jit(solution)/shard_map/all_gather | solution.py:81
  101.1 301.9 %all-gather.21.cloned.1.call-start = ((), (), s32[]{:S(2)}) async-start(), calls=%async_computation.14 | async-start | bytes 8650752 | tf_op jit(solution)/shard_map/all_gather | solution.py:82
  101.6 475.1 %reduce-scatter.18.cloned.1.call-start = ((), (), s32[]{:S(2)}) async-start(), calls=%async_computation.16 | async-start | bytes 4718592 | tf_op jit(solution)/shard_map/reduce_scatter | solution.py:198
  170.5 288.3 %copy-start.23 = (f32[1,1024]{1,0:T(1,128)}, f32[1,1024]{1,0:T(1,128)S(1)}, u32[]{:S(2)}) copy-start(f32[1,1024]{1,0:T(1,128)S(1)} %get-tuple-element.370) | copy-start | bytes 12292
  236.4 166.5 %copy-start.27 = (f32[1,1024]{1,0:T(1,128)}, f32[1,1024]{1,0:T(1,128)S(1)}, u32[]{:S(2)}) copy-start(f32[1,1024]{1,0:T(1,128)S(1)} %get-tuple-element.372) | copy-start | bytes 12292
  347.7 5.4 copy-start
  347.7 5.4 copy-start.29
  347.7 5.4 copy-start.31
  359.0 99.8 %copy-start.2 = (f32[768,1024]{1,0:T(8,128)}, f32[768,1024]{1,0:T(8,128)S(1)}, u32[]{:S(2)}) copy-start(f32[768,1024]{1,0:T(8,128)S(1)} %get-tuple-element.351) | copy-start | bytes 9437188
  359.0 99.8 %copy-start.21 = (f32[768]{0:T(1024)}, f32[768]{0:T(1024)S(1)}, u32[]{:S(2)}) copy-start(f32[768]{0:T(1024)S(1)} %broadcast_multiply_fusion.1) | copy-start | bytes 9220
  359.4 99.4 %copy-start.25 = (f32[768]{0:T(1024)}, f32[768]{0:T(1024)S(1)}, u32[]{:S(2)}) copy-start(f32[768]{0:T(1024)S(1)} %fusion.73) | copy-start | bytes 9220
  359.5 43.5 %copy-start.46 = (f32[1,1024]{1,0:T(1,128)S(1)}, f32[1,1024]{1,0:T(1,128)}, u32[]{:S(2)}) copy-start(f32[1,1024]{1,0:T(1,128)} %get-tuple-element.365) | copy-start | bytes 12292
  415.5 1.4 copy-start.7
  415.5 1.4 copy-start.32
  415.5 1.4 copy-start.41
  421.4 1.6 copy-start.9
  459.7 1.6 copy-start.10
  459.7 3.1 copy-start.51
  459.8 1.9 copy-start.33
  468.0 6.4 copy-start.1
  468.0 6.4 copy-start.30
  475.3 3.2 copy-start.13
  485.7 3.0 copy-start.4
  495.4 3.2 copy-start.13
  505.7 3.0 copy-start.4
  515.4 3.2 copy-start.13
  525.8 3.0 copy-start.4
  534.6 1.4 copy-start.8
  534.6 1.7 copy-start.40
  534.6 2.7 copy-start.6
  534.6 87.8 %reduce-scatter.16.cloned.1.call-start = ((), (), s32[]{:S(2)}) async-start(), calls=%async_computation.15 | async-start | bytes 4718592 | tf_op jit(solution)/shard_map/reduce_scatter | solution.py:192
  535.4 43.0 %copy-start.35 = (f32[1024]{0:T(1024)S(1)}, f32[1024]{0:T(1024)}, u32[]{:S(2)}) copy-start(f32[1024]{0:T(1024)} %get-tuple-element.338) | copy-start | bytes 12292
  535.4 223.5 %reduce-scatter.30.cloned.1.call-start = ((), (), s32[]{:S(2)}) async-start(), calls=%async_computation.22 | async-start | bytes 540672
  536.3 43.5 %copy-start.16 = (bf16[128,8,3,256]{3,1,2,0:T(8,128)(2,1)S(1)}, bf16[128,8,3,256]{3,1,2,0:T(8,128)(2,1)}, u32[]{:S(2)}) copy-start(bf16[128,8,3,256]{3,1,2,0:T(8,128)(2,1)} %copy.104) | copy-start | bytes 4718596
  537.6 353.4 %reduce-scatter.32.cloned.1.call-start = ((), (), s32[]{:S(2)}) async-start(), calls=%async_computation.23 | async-start | bytes 540672
  538.8 484.4 %reduce-scatter.28.cloned.1.call-start = ((), (), s32[]{:S(2)}) async-start(), calls=%async_computation.21 | async-start | bytes 540672
  579.5 584.5 %reduce-scatter.22.cloned.1.call-start = ((), (), s32[]{:S(2)}) async-start(), calls=%async_computation.18 | async-start | bytes 4325376 | tf_op jit(solution)/shard_map/reduce_scatter | solution.py:228
  585.0 739.2 %reduce-scatter.20.cloned.1.call-start = ((), (), s32[]{:S(2)}) async-start(), calls=%async_computation.17 | async-start | bytes 12976128 | tf_op jit(solution)/shard_map/reduce_scatter | solution.py:227
  588.0 37.7 %copy-start.15 = (bf16[3,256,1024]{1,2,0:T(8,128)(2,1)S(1)}, bf16[3,256,1024]{1,2,0:T(8,128)(2,1)}, u32[]{:S(2)}) copy-start(bf16[3,256,1024]{1,2,0:T(8,128)(2,1)} %reduce-scatter.18.cloned.1.call-done) | copy-start | bytes 4718596
  626.6 1.6 copy-start.17
  640.1 1.4 copy-start.19
  640.2 1043.2 %reduce-scatter.26.cloned.1.call-start = ((), (), s32[]{:S(2)}) async-start(), calls=%async_computation.20 | async-start | bytes 17301504 | tf_op jit(solution)/shard_map/reduce_scatter | solution.py:230
  654.6 1.9 copy-start.3
  654.6 1.9 copy-start.22
  654.6 1.9 copy-start.24
  654.6 1.9 copy-start.26
  654.6 1.9 copy-start.28
  654.6 1390.1 %reduce-scatter.24.cloned.1.call-start = ((), (), s32[]{:S(2)}) async-start(), calls=%async_computation.19 | async-start | bytes 17301504 | tf_op jit(solution)/shard_map/reduce_scatter | solution.py:229
  669.8 4.7 copy-start.36
  669.8 222.5 %copy-start.11 = (f32[768,1024]{1,0:T(8,128)S(1)}, f32[768,1024]{1,0:T(8,128)}, u32[]{:S(2)}) copy-start(f32[768,1024]{1,0:T(8,128)} %copy-done.10) | copy-start | bytes 9437188
  669.9 222.5 %copy-start.34 = (f32[768]{0:T(1024)S(1)}, f32[768]{0:T(1024)}, u32[]{:S(2)}) copy-start(f32[768]{0:T(1024)} %copy-done.33) | copy-start | bytes 9220
  (9 other events, 8.1 us)
Sparse Core Ops, SparseCore 0:
  10.9 71.7 all-gather.10
  96.6 42.2 all-gather.12
  140.4 45.0 all-gather.14
  188.4 56.5 all-gather.16
  247.8 76.1 all-gather.18
  326.9 76.0 all-gather.20
  534.7 41.9 reduce-scatter.17
  579.0 43.3 reduce-scatter.15
  624.6 134.2 reduce-scatter.29
  761.1 129.8 reduce-scatter.31
  893.3 129.9 reduce-scatter.27
  1026.1 137.8 reduce-scatter.21
  1171.6 152.5 reduce-scatter.19
  1326.9 356.4 reduce-scatter.25
  1686.1 358.6 reduce-scatter.23
where the time goes:
time: 2060 us; the launch traced here: 2050 us
  waiting for transfers between devices  1390 us (67%)
  blocking collectives  306 us (15%)
  matrix products  221 us (11%)
  local copies, waits for them, and re-layouts  78.2 us (4%)
  other arithmetic  36.3 us (2%)
    reduce_scatter x1, waiting for transfers between devices, body(): lax.psum_scatter(grad_in_part, ('dp', 'ctx'), scatter_dimension=0, tiled=...  361 us
    reduce_scatter x1, waiting for transfers between devices, body(): lax.psum_scatter(grad_out_part, ('dp', 'ctx'), scatter_dimension=0, tiled...  359 us
    unnamed x18, waiting for transfers between devices  297 us
    reduce_scatter x1, waiting for transfers between devices, body(): lax.psum_scatter(grad_qkv_part, ('dp', 'ctx'), scatter_dimension=0, tiled...  160 us
    reduce_scatter x1, waiting for transfers between devices, body(): lax.psum_scatter(grad_o_part, ('dp', 'ctx'), scatter_dimension=0, tiled=T...  139 us
    all_gather x1, blocking collectives, body(): lax.all_gather(biases, ('dp', 'ctx'), axis=1, tiled=True)  70.2 us
    all_gather x1, blocking collectives, body(): lax.all_gather(shifts, ('dp', 'ctx'), axis=1, tiled=True)  65.2 us
    all_gather x1, blocking collectives, body(): lax.all_gather(b_in, ('dp', 'ctx'), axis=0, tiled=True)  63.3 us
  transfers between devices with their start and end apart: 15, of which 10 were waited for; matrix products, arithmetic and copies ran while one was open for 9% of the time, Pallas kernels for 0%

commit v1 on v0

v1 whole, which is shorter than its diff:
```python
from functools import partial
import math

import jax
import jax.numpy as jnp
from jax import lax
from jax.experimental import pallas as pl
from jax.experimental.pallas import tpu as pltpu
from jax.sharding import PartitionSpec as P

HEADS = 16
HD = 64

AXES = ("dp", "ctx")


def my_index():
    return lax.axis_index("dp") * lax.axis_size("ctx") + lax.axis_index("ctx")


def n_devices():
    return lax.axis_size("dp") * lax.axis_size("ctx")


def swap(array, bits):
    return lax.ppermute(array, AXES, [(i, i ^ bits) for i in range(n_devices())])


def after(array, *others):
    return lax.optimization_barrier((array, *others))[0]


X, CORE, Y, Z = 1, 2, 4, 8


def reorder(pieces, blocks, to_shape, moves):
    plan = moves

    def kernel(*refs):
        sources, out, sem = refs[: len(pieces)], refs[len(pieces)], refs[len(pieces) + 1]
        me = my_index()
        copies = [
            pltpu.make_async_copy(sources[p].at[b], out.at[jnp.bitwise_xor(me, place)], sem.at[i])
            for i, (p, b, place) in enumerate(plan)
        ]
        for copy in copies:
            copy.start()
        for copy in copies:
            copy.wait()

    return pl.pallas_call(
        kernel,
        out_shape=jax.ShapeDtypeStruct(to_shape, pieces[0].dtype),
        in_specs=[pl.BlockSpec(memory_space=pl.ANY)] * len(pieces),
        out_specs=pl.BlockSpec(memory_space=pl.ANY),
        scratch_shapes=[pltpu.SemaphoreType.DMA((len(plan),))],
    )(*pieces)


def gather_pieces(shard, first):
    nz = n_devices() // Z
    half = nz // 2
    shard = after(shard, *first)
    others = [swap(shard, Z * k) for k in range(1, nz)]
    own = jnp.stack([shard] + others)
    from_x = swap(own, X)
    from_y = swap(own, Y)
    diag_a = swap(from_x[:half], Y)
    diag_b = swap(from_y[half:], X)
    mine = [(own, 0, 0), (from_x, X, 0), (from_y, Y, 0), (diag_a, X | Y, 0), (diag_b, X | Y, half)]
    theirs = [(swap(p, CORE), bits | CORE, k) for p, bits, k in mine]
    return mine + theirs, others


def assemble(placed, rows):
    n = n_devices()
    pieces = [p for p, _, _ in placed]
    plan = []
    for i, (p, bits, start) in enumerate(placed):
        for k in range(p.shape[0]):
            plan.append((i, k, bits | (Z * (start + k))))
    shape = (n,) + pieces[0].shape[1:]
    return reorder(pieces, None, shape, plan).reshape(n * shape[1], shape[2])


def scatter_sum(grad, first):
    n = n_devices()
    nz = n // Z
    half = nz // 2
    rows, cols = grad.shape
    r = rows // n
    rel = reorder_rel(grad.reshape(n, r, cols)).reshape(nz, 2, 2, 2, r, cols)
    f32 = jnp.float32
    low = jnp.bfloat16
    sent = rel[:, :, 1]
    got = swap(after(sent, *first), CORE)
    total = rel[:, :, 0].astype(f32) + got.astype(f32)
    own = total[:, 0, 0].astype(low)
    to_x = total[:, 0, 1].astype(low)
    to_y = total[:, 1, 0].astype(low)
    diag = total[:, 1, 1].astype(low)
    to_x_a = (to_x[:half].astype(f32) + swap(diag[:half], Y).astype(f32)).astype(low)
    to_y_b = (to_y[half:].astype(f32) + swap(diag[half:], X).astype(f32)).astype(low)
    got_x_b = swap(to_x[half:], X)
    got_y_a = swap(to_y[:half], Y)
    got_x_a = swap(to_x_a, X)
    got_y_b = swap(to_y_b, Y)
    own_a = own[:half].astype(f32) + got_x_a.astype(f32) + got_y_a.astype(f32)
    own_b = own[half:].astype(f32) + got_x_b.astype(f32) + got_y_b.astype(f32)
    line = jnp.concatenate([own_a, own_b], axis=0)
    out = line[0]
    line = line.astype(low)
    for k in range(1, nz):
        out = out + swap(line[k], Z * k).astype(f32)
    return out, got


def reorder_rel(grad):
    n = grad.shape[0]
    plan = [(0, s, s) for s in range(n)]

    def kernel(src, out, sem):
        me = my_index()
        copies = [
            pltpu.make_async_copy(src.at[jnp.bitwise_xor(me, s)], out.at[s], sem.at[s]) for s in range(n)
        ]
        for copy in copies:
            copy.start()
        for copy in copies:
            copy.wait()

    return pl.pallas_call(
        kernel,
        out_shape=jax.ShapeDtypeStruct(grad.shape, grad.dtype),
        in_specs=[pl.BlockSpec(memory_space=pl.ANY)],
        out_specs=pl.BlockSpec(memory_space=pl.ANY),
        scratch_shapes=[pltpu.SemaphoreType.DMA((n,))],
    )(grad)


def gather_small(vector):
    n = n_devices()
    rel = vector[None, :]
    bit = 1
    while bit < n:
        rel = jnp.concatenate([rel, swap(rel, bit)], axis=0)
        bit *= 2
    place = jnp.bitwise_xor(jnp.arange(n, dtype=jnp.int32), my_index())
    pick = (place[:, None] == jnp.arange(n, dtype=jnp.int32)[None, :]).astype(vector.dtype)
    return jnp.dot(pick, rel, preferred_element_type=jnp.float32)


def sum_small(vector):
    bit = 1
    while bit < n_devices():
        vector = vector + swap(vector, bit)
        bit *= 2
    return vector


fill_value = -1e30
eps_norm = 1e-05
code_absent = 30000.0


def time_embed(steps, width):
    half = width // 2
    freqs = jnp.exp(jnp.arange(half, dtype=jnp.float32) * (-math.log(10000.0) / half))
    angle = steps.astype(jnp.float32)[:, None] * freqs[None, :]
    return jnp.concatenate([jnp.sin(angle), jnp.cos(angle)], axis=-1)


def layer_norm(resid, gain, shift):
    centre = resid - jnp.mean(resid, axis=-1, keepdims=True)
    spread = jnp.mean(centre * centre, axis=-1, keepdims=True)
    return centre * lax.rsqrt(spread + eps_norm) * gain + shift


def inner(left, right):
    return lax.dot_general(
        left, right, (((0,), (0,)), ((), ())), preferred_element_type=jnp.float32
    )


def back_project(grad, weight):
    return lax.dot_general(
        grad, weight, (((1,), (1,)), ((), ())), preferred_element_type=jnp.float32
    )


def scores_of(query, keys, code_row, query_block, key_pos, positions):
    permit = (code_row[None, :] <= query_block[:, None]) | (key_pos[None, :] == positions[:, None])
    raw = jnp.einsum("qhd,khd->hqk", query, keys, preferred_element_type=jnp.float32) * (
        1.0 / math.sqrt(HD)
    )
    return jnp.where(permit[None], raw, fill_value)


def body(
    block_input,
    lengths,
    mask,
    blocks,
    timesteps,
    w_qkv,
    w_o,
    w_in,
    w_out,
    b_in,
    biases,
    gains,
    shifts,
    cotangent,
):
    items, half_len, width = block_input.shape
    rows = items * half_len
    f32, low = jnp.float32, jnp.bfloat16
    n = n_devices()
    by_hand = (w_qkv.shape[0] % 16 == 0) and n % Z == 0
    positions = lax.axis_index("ctx") * half_len + jnp.arange(half_len, dtype=jnp.int32)
    other_positions = (1 - lax.axis_index("ctx")) * half_len + jnp.arange(half_len, dtype=jnp.int32)
    key_pos = jnp.concatenate([positions, other_positions])
    valid = (positions[None, :] < lengths[:, None]) & ((mask == 1) | (positions[None, :] == 0))
    code_local = jnp.where(valid, blocks.astype(f32), code_absent)
    small = jnp.concatenate([b_in, biases.reshape(-1), gains.reshape(-1), shifts.reshape(-1)])
    if by_hand:
        placed, last = gather_pieces(w_qkv, ())
        w_qkv_all = assemble(placed, rows)
        input_other = swap(after(block_input, *last), X)
        placed, last = gather_pieces(w_o, last)
        w_o_all = assemble(placed, rows)
        placed, last = gather_pieces(w_in, last)
        w_in_all = assemble(placed, rows)
        placed, last = gather_pieces(w_out, last)
        w_out_all = assemble(placed, rows)
    else:
        input_other = swap(block_input, X)
        w_qkv_all, w_o_all, w_in_all, w_out_all = (
            lax.all_gather(w, AXES, axis=0, tiled=True) for w in (w_qkv, w_o, w_in, w_out)
        )
    small_all = gather_small(small)
    code_all = jnp.concatenate([code_local, swap(code_local, X)], axis=1)
    share = width // n
    b_count = b_in.shape[0]
    b_in_full = small_all[:, :b_count].reshape(-1)
    rest = small_all[:, b_count:].reshape(n, 8, share).transpose(1, 0, 2).reshape(8, width)
    bias_full, gain_full, shift_full = rest[:4], rest[4:6], rest[6:8]

    embed = time_embed(timesteps, width)[:, None, :]
    stream = (block_input.astype(f32) + embed).reshape(rows, width)
    stream_low = stream.astype(low)
    other_low = (input_other.astype(f32) + embed).reshape(rows, width).astype(low)
    joint = jnp.dot(stream_low, w_qkv_all, preferred_element_type=f32)
    other = jnp.dot(other_low, w_qkv_all[:, width:], preferred_element_type=f32)
    query_low = (joint[:, :width] + bias_full[0]).astype(low)
    split = lambda array: array.reshape(items, half_len, width)
    key_all = jnp.concatenate(
        [split(joint[:, width : 2 * width].astype(low)), split(other[:, :width].astype(low))], axis=1
    )
    value_all = jnp.concatenate(
        [
            split((joint[:, 2 * width :] + bias_full[1]).astype(low)),
            split((other[:, width:] + bias_full[1]).astype(low)),
        ],
        axis=1,
    )
    full_len = 2 * half_len
    query_block = blocks.astype(f32)
    query_four = query_low.reshape(items, half_len, HEADS, HD)
    key_four = key_all.reshape(items, full_len, HEADS, HD)
    value_four = value_all.reshape(items, full_len, HEADS, HD)

    def attend(inputs):
        query, keys, values, code_row, block_row = inputs
        scores = scores_of(query, keys, code_row, block_row, key_pos, positions)
        peak = jnp.max(scores, axis=-1, keepdims=True)
        expo = jnp.exp(scores - peak)
        total = jnp.sum(expo, axis=-1, keepdims=True)
        probs = expo / total
        mixed = jnp.einsum(
            "hqk,khd->qhd", probs.astype(jnp.bfloat16), values, preferred_element_type=jnp.float32
        )
        return (mixed, (peak + jnp.log(total))[..., 0])

    mixed_all, log_totals = lax.map(
        attend, (query_four, key_four, value_four, code_all, query_block)
    )
    mixed_low = mixed_all.reshape(rows, width).astype(jnp.bfloat16)
    attn = jnp.dot(mixed_low, w_o_all, preferred_element_type=jnp.float32) + bias_full[2]
    resid_one = stream + attn
    hidden_one = layer_norm(resid_one, gain_full[0], shift_full[0])
    hidden_low = hidden_one.astype(jnp.bfloat16)
    pre = jnp.dot(hidden_low, w_in_all, preferred_element_type=jnp.float32) + b_in_full
    act_low = jax.nn.gelu(pre, approximate=False).astype(jnp.bfloat16)
    branch = jnp.dot(act_low, w_out_all, preferred_element_type=jnp.float32) + bias_full[3]
    resid_two = hidden_one + branch
    result = layer_norm(resid_two, gain_full[1], shift_full[1])
    output = result.astype(jnp.bfloat16).reshape(items, half_len, width)
    row_weight = valid.reshape(rows).astype(jnp.float32)
    local_sums = jnp.stack(
        [
            jnp.sum(row_weight * jnp.sum(tensor * tensor, axis=-1))
            for tensor in (stream, attn, branch, result)
        ]
        + [jnp.sum(row_weight)]
    )
    _, norm_two_back = jax.vjp(layer_norm, resid_two, gain_full[1], shift_full[1])
    dres_two, gain_two_grad, shift_two_grad = norm_two_back(
        cotangent.reshape(rows, width).astype(jnp.float32)
    )
    branch_grad = dres_two.astype(jnp.bfloat16)

    if by_hand:
        share_sum = lambda part, first: scatter_sum(part.astype(low), first)
    else:
        share_sum = lambda part, first: (
            lax.psum_scatter(part, AXES, scatter_dimension=0, tiled=True),
            part,
        )
    grad_out, got = share_sum(inner(act_low, branch_grad), ())
    act_grad = back_project(branch_grad, w_out_all)
    _, gelu_back = jax.vjp(partial(jax.nn.gelu, approximate=False), pre)
    pre_grad = gelu_back(act_grad)[0].astype(jnp.bfloat16)
    grad_in, got = share_sum(inner(hidden_low, pre_grad), (got,))
    dhidden = dres_two + back_project(pre_grad, w_in_all)
    _, norm_one_back = jax.vjp(layer_norm, resid_one, gain_full[0], shift_full[0])
    dres_one, gain_one_grad, shift_one_grad = norm_one_back(dhidden)
    attn_grad = dres_one.astype(jnp.bfloat16)
    grad_o, got = share_sum(inner(mixed_low, attn_grad), (got,))
    mixed_grad = (
        back_project(attn_grad, w_o_all).astype(jnp.bfloat16).reshape(items, half_len, HEADS, HD)
    )

    def attend_back(inputs):
        query, keys, values, code_row, block_row, log_row, grad_row = inputs
        scores = scores_of(query, keys, code_row, block_row, key_pos, positions)
        probs = jnp.exp(scores - log_row[..., None])
        value_part = jnp.einsum(
            "hqk,qhd->khd", probs.astype(jnp.bfloat16), grad_row, preferred_element_type=jnp.float32
        )
        prob_grad = jnp.einsum("qhd,khd->hqk", grad_row, values, preferred_element_type=jnp.float32)
        centre = jnp.sum(probs * prob_grad, axis=-1, keepdims=True)
        score_grad = (probs * (prob_grad - centre)).astype(jnp.bfloat16)
        query_part = jnp.einsum(
            "hqk,khd->qhd", score_grad, keys, preferred_element_type=jnp.float32
        ) * (1.0 / math.sqrt(HD))
        key_part = jnp.einsum(
            "hqk,qhd->khd", score_grad, query, preferred_element_type=jnp.float32
        ) * (1.0 / math.sqrt(HD))
        return (query_part, key_part, value_part)

    query_part, key_part, value_part = lax.map(
        attend_back,
        (query_four, key_four, value_four, code_all, query_block, log_totals, mixed_grad),
    )
    key_part = key_part.reshape(items, full_len, width)
    value_part = value_part.reshape(items, full_len, width)
    away = jnp.stack([key_part[:, half_len:], value_part[:, half_len:]]).astype(low)
    back = swap(away, X).astype(f32)
    query_grad_low = query_part.reshape(rows, width).astype(jnp.bfloat16)
    key_grad_low = (key_part[:, :half_len] + back[0]).reshape(rows, width).astype(jnp.bfloat16)
    value_grad_low = (value_part[:, :half_len] + back[1]).reshape(rows, width).astype(jnp.bfloat16)
    joint_grad = jnp.concatenate([query_grad_low, key_grad_low, value_grad_low], axis=1)
    grad_qkv, got = share_sum(inner(stream_low, joint_grad), (got,))
    input_grad = (
        (dres_one + back_project(joint_grad, w_qkv_all))
        .astype(jnp.bfloat16)
        .reshape(items, half_len, width)
    )
    b_in_part = jnp.sum(pre_grad.astype(jnp.float32), axis=0)
    parts = [
        jnp.sum(query_grad_low.astype(jnp.float32), axis=0),
        jnp.sum(value_grad_low.astype(jnp.float32), axis=0),
        jnp.sum(attn_grad.astype(jnp.float32), axis=0),
        jnp.sum(branch_grad.astype(jnp.float32), axis=0),
        gain_one_grad,
        gain_two_grad,
        shift_one_grad,
        shift_two_grad,
    ]
    sums = sum_small(jnp.concatenate([b_in_part] + parts + [local_sums]))
    ff = b_in_part.shape[0]
    me = my_index()
    grad_b_in = lax.dynamic_slice(sums, (me * b_count,), (b_count,))
    grads = lax.dynamic_slice(sums[ff : ff + 8 * width].reshape(8, width), (0, me * share), (8, share))
    totals = sums[ff + 8 * width :]
    rms = jnp.sqrt(totals[:4] / (totals[4] * width))
    return (
        output,
        input_grad,
        grad_qkv,
        grad_o,
        grad_in,
        grad_out,
        grad_b_in,
        grads[:4],
        grads[4:6],
        grads[6:8],
        rms,
    )


def solution(mesh):
    in_specs = (
        P("dp", "ctx", None),
        P("dp"),
        P("dp", "ctx"),
        P("dp", "ctx"),
        P("dp"),
        P(("dp", "ctx"), None),
        P(("dp", "ctx"), None),
        P(("dp", "ctx"), None),
        P(("dp", "ctx"), None),
        P(("dp", "ctx")),
        P(None, ("dp", "ctx")),
        P(None, ("dp", "ctx")),
        P(None, ("dp", "ctx")),
        P("dp", "ctx", None),
    )
    out_specs = (
        P("dp", "ctx", None),
        P("dp", "ctx", None),
        P(("dp", "ctx"), None),
        P(("dp", "ctx"), None),
        P(("dp", "ctx"), None),
        P(("dp", "ctx"), None),
        P(("dp", "ctx")),
        P(None, ("dp", "ctx")),
        P(None, ("dp", "ctx")),
        P(None, ("dp", "ctx")),
        P(),
    )
    return jax.shard_map(body, mesh=mesh, in_specs=in_specs, out_specs=out_specs, check_vma=False)
```

time: 2060 us -> 2270 us (1.10)
  Pallas kernels: 0 us -> 1540 us
  waiting for transfers between devices: 1390 us -> 169 us
  blocking collectives: 306 us -> 0 us
  starting transfers between devices: 1.07 us -> 105 us
  local copies, waits for them, and re-layouts: 78.2 us -> 146 us
  other arithmetic: 36.3 us -> 88.7 us
    pallas_call x0 -> x8, Pallas kernels: none -> 1540 us  [the longest x4 768 us: reorder(): pl.pallas_call(kernel, out_shape=jax.ShapeDtypeStruct(to_shape, pieces[0]...]
    reduce_scatter x6 -> x0, waiting for transfers between devices: 1090 us -> none  [the longest x1 361 us: body(): lax.psum_scatter(grad_in_part, ('dp', 'ctx'), scatter_dimension=0, tiled=...]
    unnamed x18 -> x0, waiting for transfers between devices: 297 us -> none
    all_gather x5 -> x0, blocking collectives: 266 us -> none  [the longest x1 70.2 us: body(): lax.all_gather(biases, ('dp', 'ctx'), axis=1, tiled=True)]
    ppermute x0 -> x101, waiting for transfers between devices: none -> 169 us  [swap(): lax.ppermute(array, AXES, [(i, i ^ bits) for i in range(n_devices())])]
    ppermute x0 -> x101, starting transfers between devices: none -> 105 us  [swap(): lax.ppermute(array, AXES, [(i, i ^ bits) for i in range(n_devices())])]
    unnamed x1 -> x0, blocking collectives: 39.6 us -> none
    slice x2 -> x24, local copies, waits for them, and re-layouts: 3.92 us -> 35.6 us  [the longest x4 15.3 us: scatter_sum(): total = rel[:, :, 0].astype(f32) + got.astype(f32)]
  transfers between devices with their start and end apart: 15 -> 101, of which waited for: 10 -> 34; matrix products, arithmetic and copies ran while one was open for 9% -> 13% of each run, Pallas kernels for 0% -> 57%
where the time goes in v1:
time: 2270 us; the launch traced here: 2260 us
  Pallas kernels  1540 us (68%)
  matrix products  213 us (9%)
  waiting for transfers between devices  169 us (7%)
  local copies, waits for them, and re-layouts  146 us (6%)
  starting transfers between devices  105 us (5%)
  other arithmetic  88.7 us (4%)
    pallas_call x4, Pallas kernels, reorder(): pl.pallas_call(kernel, out_shape=jax.ShapeDtypeStruct(to_shape, pieces[0]...  768 us
    pallas_call x4, Pallas kernels, reorder_rel(): pl.pallas_call(kernel, out_shape=jax.ShapeDtypeStruct(grad.shape, grad.dt...  768 us
    ppermute x101, waiting for transfers between devices, swap(): lax.ppermute(array, AXES, [(i, i ^ bits) for i in range(n_devices())])  169 us
    ppermute x101, starting transfers between devices, swap(): lax.ppermute(array, AXES, [(i, i ^ bits) for i in range(n_devices())])  105 us
  transfers between devices with their start and end apart: 101, of which 34 were waited for; matrix products, arithmetic and copies ran while one was open for 13% of the time, Pallas kernels for 57%

profile of v1, /device:TPU:0, one launch (start us, length us, event | category | flops | bytes accessed | tf_op | source)
XLA Modules:
  0.0 2261.7 jit_solution(1279601991378045309)
XLA Ops:
  13.0 8.1 collective-permute-done.1
  45.5 9.5 collective-permute-done.32
  74.7 6.6 collective-permute-done.44
  95.8 3.9 concatenate.67
  111.1 8.7 collective-permute-done.5.refs_3_
  119.9 26.7 %collective-permute-done.34.refs_1_ = bf16[4,32,4096]{2,1,0:T(8,128)(2,1)} collective-permute-done((bf16[4,32,4096]{2,1,0:T(8,128)(2,1)}, bf16[4,32,4096]{2,1,0:T(8,128)(2,1)}, u32[]{:S(2)}, u32[]{:S(2)}) %collective-permute-start.34) | collective-permute-done | bytes 1048608 | tf_op jit(solution)/shard_map/ppermute | solution.py:26
  149.4 64.9 %shard_map.222 = bf16[32,32,1024]{2,1,0:T(8,128)(2,1)} custom-call(bf16[4,32,1024]{2,1,0:T(8,128)(2,1)} %copy-done.34, bf16[4,32,1024]{2,1,0:T(8,128)(2,1)} %copy-done.37, bf16[4,32,1024]{2,1,0:T(8,128)(2,1)} %copy-done.38, bf16[2,32,1024]{2,1,0:T(8,128)(2,1)} %copy-done.52, bf16[2,32,1024]{2,1,0:T(8,128)(2,1)} %collective-permute-done.25.refs_4_, ...), custom_call_target="tpu_custom_call" | custom-call | tf_op jit(solution)/shard_map/pallas_call | solution.py:51
  218.6 5.6 multiply_reduce_fusion.4
  228.5 192.0 %shard_map.221 = bf16[32,32,3072]{2,1,0:T(8,128)(2,1)} custom-call(bf16[4,32,3072]{2,1,0:T(8,128)(2,1)} %copy-done.20, bf16[4,32,3072]{2,1,0:T(8,128)(2,1)} %copy-done.24, bf16[4,32,3072]{2,1,0:T(8,128)(2,1)} %copy-done.25, bf16[2,32,3072]{2,1,0:T(8,128)(2,1)} %collective-permute-done.5.refs_3_, bf16[2,32,3072]{2,1,0:T(8,128)(2,1)} %collective-permute-done.6.refs_4_, ...), custom_call_target="tpu_custom_call" | custom-call | tf_op jit(solution)/shard_map/pallas_call | solution.py:51
  420.5 5.5 fusion.63
  426.1 5.0 fusion.140
  438.7 4.2 concatenate.68
  445.4 5.3 concatenate.69
  450.7 3.9 pad_maximum_fusion.1
  457.4 4.1 reshape.510
  461.5 3.7 copy.73
  467.8 4.2 concatenate.74
  474.5 5.3 concatenate.73
  479.8 4.0 pad_maximum_fusion.2
  486.0 33.1 %while.28 = (s32[]{:T(128)}, bf16[3,256,16,64]{1,3,2,0:T(8,128)(2,1)}, f32[3,16,256]{2,1,0:T(8,128)}, bf16[3,512,16,64]{1,3,2,0:T(8,128)(2,1)}, f32[3,512]{1,0:T...) while((s32[]{:T(128)}, ...), condition=%wide.region_3.4_spmd.clone, body=%wide.region_0.3_spmd.clone.sunk | while | flops 562426112 | bytes 29507192 | solution.py:285
  492.5 4.5 fusion.182
  503.5 4.5 fusion.182
  514.6 4.5 fusion.182
  519.2 3.9 copy.75
  534.4 6.2 collective-permute-done.48.refs_3_
  542.0 5.1 collective-permute-done.49.refs_4_
  548.2 255.5 %shard_map.223 = bf16[32,32,4096]{2,1,0:T(8,128)(2,1)} custom-call(bf16[4,32,4096]{2,1,0:T(8,128)(2,1)} %pad_maximum_fusion.8.refs_0_, bf16[4,32,4096]{2,1,0:T(8,128)(2,1)} %collective-permute-done.34.refs_1_, bf16[4,32,4096]{2,1,0:T(8,128)(2,1)} %collective-permute-done.35.refs_2_, bf16[2,32,4096]{2,1,0:T(8,128)(2,1)} %collective-permute-done.36.refs_3_, ...), custom_call_target="tpu_custom_call" | custom-call | tf_op jit(solution)/shard_map/pallas_call | solution.py:51
  803.7 38.9 %multiply_convert_fusion.1 = (bf16[768,4096]{1,0:T(8,128)(2,1)}, f32[768,4096]{1,0:T(8,128)}, f32[768,4096]{1,0:T(8,128)}) fusion(f32[4096]{0:T(1024)S(1)} %slice_bitcast_fusion.46, bf16[1024,4096]{1,0:T(8,128)(2,1)} %bitcast.437, f32[768,1024]{1,0:T(8,128)S(1)} %get-tuple-element.355, f32[1024]{0:T(1024)S(1)} %add.335, f32[1024]{0:T(1024)S(1)} %mul.257, ...), kind=kOutput, calls=%fused_computation.72 | convolution fusion | flops 6654001152 | bytes 43022336 | tf_op jit(solution)/shard_map/dot_general | solution.py:293
  842.6 255.5 %shard_map.224 = bf16[32,128,1024]{2,1,0:T(8,128)(2,1)} custom-call(bf16[4,128,1024]{2,1,0:T(8,128)(2,1)} %pad_maximum_fusion.9.refs_0_, bf16[4,128,1024]{2,1,0:T(8,128)(2,1)} %collective-permute-done.46.refs_1_, bf16[4,128,1024]{2,1,0:T(8,128)(2,1)} %collective-permute-done.47.refs_2_, bf16[2,128,1024]{2,1,0:T(8,128)(2,1)} %collective-permute-done.48.refs_3_, ...), custom_call_target="tpu_custom_call" | custom-call | tf_op jit(solution)/shard_map/pallas_call | solution.py:51
  1098.2 12.4 fusion.132
  1112.0 3.4 fusion.75
  1118.3 9.1 convolution_convert_fusion
  1127.4 21.1 convert_reduce_fusion
  1148.6 13.6 multiply_reduce_fusion.5
  1172.0 5.1 copy.79
  1178.5 63.8 %while.29 = (s32[]{:T(128)}, bf16[3,256,16,64]{1,3,2,0:T(8,128)(2,1)}, f32[3,512,16,64]{1,3,2,0:T(8,128)}, f32[3,512,16,64]{1,3,2,0:T(8,128)}, bf16[3,512,16,64]...) while((s32[]{:T(128)}, ...), condition=%wide.region_14.15_spmd.clone, body=%wide.region_12.14_spmd.clone.sunk | while | flops 1374810368 | bytes 92932320 | solution.py:352
  1183.4 4.7 multiply_reduce_fusion.10
  1196.5 3.4 bitcast_dynamic-update-slice_fusion.8
  1204.6 4.7 multiply_reduce_fusion.10
  1217.6 3.4 bitcast_dynamic-update-slice_fusion.8
  1225.8 4.7 multiply_reduce_fusion.10
  1248.9 255.5 %shard_map.228 = bf16[32,128,1024]{2,1,0:T(8,128)(2,1)} custom-call(bf16[32,128,1024]{2,1,0:T(8,128)(2,1)} %bitcast.436), custom_call_target="tpu_custom_call" | custom-call | tf_op jit(solution)/shard_map/pallas_call | solution.py:132
  1504.4 5.2 fusion.135
  1512.8 12.1 convolution_convert_fusion.1
  1525.2 255.5 %shard_map.227 = bf16[32,32,4096]{2,1,0:T(8,128)(2,1)} custom-call(bf16[32,32,4096]{2,1,0:T(8,128)(2,1)} %bitcast.441), custom_call_target="tpu_custom_call" | custom-call | tf_op jit(solution)/shard_map/pallas_call | solution.py:132
  1781.4 6.5 fusion.136
  1790.4 4.9 convert_reduce_fusion.4
  1799.3 5.0 convolution_convert_fusion.3
  1804.3 64.9 %shard_map.226 = bf16[32,32,1024]{2,1,0:T(8,128)(2,1)} custom-call(bf16[32,32,1024]{2,1,0:T(8,128)(2,1)} %bitcast.458), custom_call_target="tpu_custom_call" | custom-call | tf_op jit(solution)/shard_map/pallas_call | solution.py:132
  1887.9 10.7 convolution_convert_fusion.2
  1899.2 6.8 add_convert_fusion.1
  1905.9 192.0 %shard_map.225 = bf16[32,32,3072]{2,1,0:T(8,128)(2,1)} custom-call(bf16[32,32,3072]{2,1,0:T(8,128)(2,1)} %bitcast.448), custom_call_target="tpu_custom_call" | custom-call | tf_op jit(solution)/shard_map/pallas_call | solution.py:132
  2100.8 5.8 fusion.60
  2115.3 7.9 collective-permute-done.92
  2129.7 3.7 collective-permute-done.91
  2133.4 6.1 collective-permute-done.93
  2145.7 3.7 fusion.61
  2150.2 6.0 collective-permute-done.88
  2157.7 5.9 collective-permute-done.83
  2171.8 6.5 collective-permute-done.74
  2180.9 9.2 collective-permute-done.84
  2192.4 9.4 collective-permute-done.69
  2210.4 6.5 collective-permute-done.76
  2229.9 5.1 collective-permute-done.65
  (586 shorter events, 327.9 us)
Async XLA Ops:
  3.7 17.4 collective-permute-start.1
  6.3 14.8 collective-permute-start.2
  12.9 14.0 collective-permute-start.13
  35.3 19.7 collective-permute-start.32
  37.0 19.5 collective-permute-start.33
  39.5 20.5 collective-permute-start.22
  41.1 19.0 collective-permute-start.23
  42.6 23.7 %collective-permute-start.26 = (bf16[4,32,1024]{2,1,0:T(8,128)(2,1)S(1)}, bf16[4,32,1024]{2,1,0:T(8,128)(2,1)S(1)}, u32[]{:S(2)}, u32[]{:S(2)}) collective-permute-start(bf16[4,32,1024]{2,1,0:T(8,128)(2,1)S(1)} %pad_maximum_fusion.11.refs_0_), channel_id=1, source_target_pairs={{0,2},{1,3},{2,0},{3,1},{4,6},{5,7},{6,4},{7,5},{8,10},{9,11},{10,... | collective-permute-start | bytes 786440 | tf_op jit(solution)/shard_map/ppermute | solution.py:26
  60.1 14.1 collective-permute-start.43
  60.1 21.2 collective-permute-start.44
  63.1 18.3 collective-permute-start.45
  70.3 20.5 collective-permute-start.3
  72.8 26.9 %collective-permute-start.4 = (bf16[4,32,3072]{2,1,0:T(8,128)(2,1)S(1)}, bf16[4,32,3072]{2,1,0:T(8,128)(2,1)S(1)}, u32[]{:S(2)}, u32[]{:S(2)}) collective-permute-start(bf16[4,32,3072]{2,1,0:T(8,128)(2,1)S(1)} %pad_maximum_fusion.10.refs_0_), channel_id=1, source_target_pairs={{0,4},{1,5},{2,6},{3,7},{4,0},{5,1},{6,2},{7,3},{8,12},{9,13},{10,... | collective-permute-start | bytes 2359304 | tf_op jit(solution)/shard_map/ppermute | solution.py:26
  74.1 144.0 %collective-permute-start.17 = (bf16[3,256,1024]{2,1,0:T(8,128)(2,1)}, bf16[3,256,1024]{2,1,0:T(8,128)(2,1)}, u32[]{:S(2)}, u32[]{:S(2)}) collective-permute-start(bf16[3,256,1024]{2,1,0:T(8,128)(2,1)} %param.18), channel_id=1, source_target_pairs={{0,1},{1,0},{2,3},{3,2},{4,5},{5,4},{6,7},{7,6},{8,9},{9,8},{10,11... | collective-permute-start | bytes 4718600 | tf_op jit(solution)/shard_map/ppermute | solution.py:26
  85.0 61.6 %collective-permute-start.34 = (bf16[4,32,4096]{2,1,0:T(8,128)(2,1)}, bf16[4,32,4096]{2,1,0:T(8,128)(2,1)}, u32[]{:S(2)}, u32[]{:S(2)}) collective-permute-start(bf16[4,32,4096]{2,1,0:T(8,128)(2,1)} %pad_maximum_fusion.8.refs_0_), channel_id=1, source_target_pairs={{0,1},{1,0},{2,3},{3,2},{4,5},{5,4},{6,7},{7,6},{8,9},{9,8},{10,11... | collective-permute-start | bytes 3145736 | tf_op jit(solution)/shard_map/ppermute | solution.py:26
  86.5 60.1 %collective-permute-start.35 = (bf16[4,32,4096]{2,1,0:T(8,128)(2,1)}, bf16[4,32,4096]{2,1,0:T(8,128)(2,1)}, u32[]{:S(2)}, u32[]{:S(2)}) collective-permute-start(bf16[4,32,4096]{2,1,0:T(8,128)(2,1)} %pad_maximum_fusion.8.refs_0_), channel_id=1, source_target_pairs={{0,4},{1,5},{2,6},{3,7},{4,0},{5,1},{6,2},{7,3},{8,12},{9,13},{10,... | collective-permute-start | bytes 3145736 | tf_op jit(solution)/shard_map/ppermute | solution.py:26
  93.4 26.5 %collective-permute-start.5 = (bf16[2,32,3072]{2,1,0:T(8,128)(2,1)}, bf16[2,32,3072]{2,1,0:T(8,128)(2,1)}, u32[]{:S(2)}, u32[]{:S(2)}) collective-permute-start(bf16[2,32,3072]{2,1,0:T(8,128)(2,1)} %slice.556), channel_id=1, source_target_pairs={{0,4},{1,5},{2,6},{3,7},{4,0},{5,1},{6,2},{7,3},{8,12},{9,13},{10,... | collective-permute-start | bytes 1179656 | tf_op jit(solution)/shard_map/ppermute | solution.py:26
  101.9 116.3 %collective-permute-start.6 = (bf16[2,32,3072]{2,1,0:T(8,128)(2,1)}, bf16[2,32,3072]{2,1,0:T(8,128)(2,1)}, u32[]{:S(2)}, u32[]{:S(2)}) collective-permute-start(bf16[2,32,3072]{2,1,0:T(8,128)(2,1)} %slice.557), channel_id=1, source_target_pairs={{0,1},{1,0},{2,3},{3,2},{4,5},{5,4},{6,7},{7,6},{8,9},{9,8},{10,11... | collective-permute-start | bytes 1179656 | tf_op jit(solution)/shard_map/ppermute | solution.py:26
  119.9 104.4 %collective-permute-start.7 = (bf16[4,32,3072]{2,1,0:T(8,128)(2,1)S(1)}, bf16[4,32,3072]{2,1,0:T(8,128)(2,1)S(1)}, u32[]{:S(2)}, u32[]{:S(2)}) collective-permute-start(bf16[4,32,3072]{2,1,0:T(8,128)(2,1)S(1)} %pad_maximum_fusion.10.refs_0_), channel_id=1, source_target_pairs={{0,2},{1,3},{2,0},{3,1},{4,6},{5,7},{6,4},{7,5},{8,10},{9,11},{10,... | collective-permute-start | bytes 2359304 | tf_op jit(solution)/shard_map/ppermute | solution.py:26
  146.6 80.8 %collective-permute-start.8 = (bf16[4,32,3072]{2,1,0:T(8,128)(2,1)S(1)}, bf16[4,32,3072]{2,1,0:T(8,128)(2,1)}, u32[]{:S(2)}, u32[]{:S(2)}) collective-permute-start(bf16[4,32,3072]{2,1,0:T(8,128)(2,1)S(1)} %collective-permute-done.3.refs_1_), channel_id=1, source_target_pairs={{0,2},{1,3},{2,0},{3,1},{4,6},{5,7},{6,4},{7,5},{8,10},{9,11},{10,... | collective-permute-start | bytes 2359304 | tf_op jit(solution)/shard_map/ppermute | solution.py:26
  146.6 81.3 %collective-permute-start.9 = (bf16[4,32,3072]{2,1,0:T(8,128)(2,1)S(1)}, bf16[4,32,3072]{2,1,0:T(8,128)(2,1)}, u32[]{:S(2)}, u32[]{:S(2)}) collective-permute-start(bf16[4,32,3072]{2,1,0:T(8,128)(2,1)S(1)} %collective-permute-done.4.refs_2_), channel_id=1, source_target_pairs={{0,2},{1,3},{2,0},{3,1},{4,6},{5,7},{6,4},{7,5},{8,10},{9,11},{10,... | collective-permute-start | bytes 2359304 | tf_op jit(solution)/shard_map/ppermute | solution.py:26
  224.3 301.6 %collective-permute-start.38 = (bf16[4,32,4096]{2,1,0:T(8,128)(2,1)}, bf16[4,32,4096]{2,1,0:T(8,128)(2,1)}, u32[]{:S(2)}, u32[]{:S(2)}) collective-permute-start(bf16[4,32,4096]{2,1,0:T(8,128)(2,1)} %pad_maximum_fusion.8.refs_0_), channel_id=1, source_target_pairs={{0,2},{1,3},{2,0},{3,1},{4,6},{5,7},{6,4},{7,5},{8,10},{9,11},{10,... | collective-permute-start | bytes 3145736 | tf_op jit(solution)/shard_map/ppermute | solution.py:26
  224.3 299.1 %collective-permute-start.46 = (bf16[4,128,1024]{2,1,0:T(8,128)(2,1)}, bf16[4,128,1024]{2,1,0:T(8,128)(2,1)}, u32[]{:S(2)}, u32[]{:S(2)}) collective-permute-start(bf16[4,128,1024]{2,1,0:T(8,128)(2,1)} %pad_maximum_fusion.9.refs_0_), channel_id=1, source_target_pairs={{0,1},{1,0},{2,3},{3,2},{4,5},{5,4},{6,7},{7,6},{8,9},{9,8},{10,11... | collective-permute-start | bytes 3145736 | tf_op jit(solution)/shard_map/ppermute | solution.py:26
  225.9 300.2 %collective-permute-start.47 = (bf16[4,128,1024]{2,1,0:T(8,128)(2,1)}, bf16[4,128,1024]{2,1,0:T(8,128)(2,1)}, u32[]{:S(2)}, u32[]{:S(2)}) collective-permute-start(bf16[4,128,1024]{2,1,0:T(8,128)(2,1)} %pad_maximum_fusion.9.refs_0_), channel_id=1, source_target_pairs={{0,4},{1,5},{2,6},{3,7},{4,0},{5,1},{6,2},{7,3},{8,12},{9,13},{10,... | collective-permute-start | bytes 3145736 | tf_op jit(solution)/shard_map/ppermute | solution.py:26
  227.4 305.5 %collective-permute-start.36 = (bf16[2,32,4096]{2,1,0:T(8,128)(2,1)}, bf16[2,32,4096]{2,1,0:T(8,128)(2,1)}, u32[]{:S(2)}, u32[]{:S(2)}) collective-permute-start(bf16[2,32,4096]{2,1,0:T(8,128)(2,1)} %slice.572), channel_id=1, source_target_pairs={{0,4},{1,5},{2,6},{3,7},{4,0},{5,1},{6,2},{7,3},{8,12},{9,13},{10,... | collective-permute-start | bytes 1572872 | tf_op jit(solution)/shard_map/ppermute | solution.py:26
  227.9 306.5 %collective-permute-start.37 = (bf16[2,32,4096]{2,1,0:T(8,128)(2,1)}, bf16[2,32,4096]{2,1,0:T(8,128)(2,1)}, u32[]{:S(2)}, u32[]{:S(2)}) collective-permute-start(bf16[2,32,4096]{2,1,0:T(8,128)(2,1)} %slice.573), channel_id=1, source_target_pairs={{0,1},{1,0},{2,3},{3,2},{4,5},{5,4},{6,7},{7,6},{8,9},{9,8},{10,11... | collective-permute-start | bytes 1572872 | tf_op jit(solution)/shard_map/ppermute | solution.py:26
  523.5 24.1 %collective-permute-start.39 = (bf16[4,32,4096]{2,1,0:T(8,128)(2,1)}, bf16[4,32,4096]{2,1,0:T(8,128)(2,1)}, u32[]{:S(2)}, u32[]{:S(2)}) collective-permute-start(bf16[4,32,4096]{2,1,0:T(8,128)(2,1)} %collective-permute-done.34.refs_1_), channel_id=1, source_target_pairs={{0,2},{1,3},{2,0},{3,1},{4,6},{5,7},{6,4},{7,5},{8,10},{9,11},{10,... | collective-permute-start | bytes 3145736 | tf_op jit(solution)/shard_map/ppermute | solution.py:26
  525.9 22.2 collective-permute-start.40
  526.0 14.6 collective-permute-start.48
  532.9 14.2 collective-permute-start.49
  534.4 12.6 collective-permute-start.41
  547.0 295.5 %collective-permute-start.50 = (bf16[4,128,1024]{2,1,0:T(8,128)(2,1)}, bf16[4,128,1024]{2,1,0:T(8,128)(2,1)}, u32[]{:S(2)}, u32[]{:S(2)}) collective-permute-start(bf16[4,128,1024]{2,1,0:T(8,128)(2,1)} %pad_maximum_fusion.9.refs_0_), channel_id=1, source_target_pairs={{0,2},{1,3},{2,0},{3,1},{4,6},{5,7},{6,4},{7,5},{8,10},{9,11},{10,... | collective-permute-start | bytes 3145736 | tf_op jit(solution)/shard_map/ppermute | solution.py:26
  547.1 295.5 %collective-permute-start.51 = (bf16[4,128,1024]{2,1,0:T(8,128)(2,1)}, bf16[4,128,1024]{2,1,0:T(8,128)(2,1)}, u32[]{:S(2)}, u32[]{:S(2)}) collective-permute-start(bf16[4,128,1024]{2,1,0:T(8,128)(2,1)} %collective-permute-done.46.refs_1_), channel_id=1, source_target_pairs={{0,2},{1,3},{2,0},{3,1},{4,6},{5,7},{6,4},{7,5},{8,10},{9,11},{10,... | collective-permute-start | bytes 3145736 | tf_op jit(solution)/shard_map/ppermute | solution.py:26
  547.6 295.0 %collective-permute-start.52 = (bf16[4,128,1024]{2,1,0:T(8,128)(2,1)}, bf16[4,128,1024]{2,1,0:T(8,128)(2,1)}, u32[]{:S(2)}, u32[]{:S(2)}) collective-permute-start(bf16[4,128,1024]{2,1,0:T(8,128)(2,1)} %collective-permute-done.47.refs_2_), channel_id=1, source_target_pairs={{0,2},{1,3},{2,0},{3,1},{4,6},{5,7},{6,4},{7,5},{8,10},{9,11},{10,... | collective-permute-start | bytes 3145736 | tf_op jit(solution)/shard_map/ppermute | solution.py:26
  547.6 294.9 %collective-permute-start.53 = (bf16[2,128,1024]{2,1,0:T(8,128)(2,1)}, bf16[2,128,1024]{2,1,0:T(8,128)(2,1)}, u32[]{:S(2)}, u32[]{:S(2)}) collective-permute-start(bf16[2,128,1024]{2,1,0:T(8,128)(2,1)} %collective-permute-done.48.refs_3_), channel_id=1, source_target_pairs={{0,2},{1,3},{2,0},{3,1},{4,6},{5,7},{6,4},{7,5},{8,10},{9,11},{10,... | collective-permute-start | bytes 1572872 | tf_op jit(solution)/shard_map/ppermute | solution.py:26
  548.1 294.5 %collective-permute-start.54 = (bf16[2,128,1024]{2,1,0:T(8,128)(2,1)}, bf16[2,128,1024]{2,1,0:T(8,128)(2,1)}, u32[]{:S(2)}, u32[]{:S(2)}) collective-permute-start(bf16[2,128,1024]{2,1,0:T(8,128)(2,1)} %collective-permute-done.49.refs_4_), channel_id=1, source_target_pairs={{0,2},{1,3},{2,0},{3,1},{4,6},{5,7},{6,4},{7,5},{8,10},{9,11},{10,... | collective-permute-start | bytes 1572872 | tf_op jit(solution)/shard_map/ppermute | solution.py:26
  1247.5 540.4 %collective-permute-start.55 = (bf16[2,3,256,1024]{2,3,1,0:T(8,128)(2,1)}, bf16[2,3,256,1024]{2,3,1,0:T(8,128)(2,1)}, u32[]{:S(2)}, u32[]{:S(2)}) collective-permute-start(bf16[2,3,256,1024]{2,3,1,0:T(8,128)(2,1)} %pad_maximum_fusion.3), channel_id=1, source_target_pairs={{0,1},{1,0},{2,3},{3,2},{4,5},{5,4},{6,7},{7,6},{8,9},{9,8},{10,11... | collective-permute-start | bytes 9437192 | tf_op jit(solution)/shard_map/ppermute | solution.py:26
  1512.2 386.5 %collective-permute-start.56 = (bf16[4,2,2,128,1024]{4,3,0,2,1:T(8,128)(2,1)}, bf16[4,2,2,128,1024]{4,3,0,2,1:T(8,128)(2,1)}, u32[]{:S(2)}, u32[]{:S(2)}) collective-permute-start(bf16[4,2,2,128,1024]{4,3,0,2,1:T(8,128)(2,1)} %bitcast.381), channel_id=1, source_target_pairs={{0,2},{1,3},{2,0},{3,1},{4,6},{5,7},{6,4},{7,5},{8,10},{9,11},{10,... | collective-permute-start | bytes 12582920 | tf_op jit(solution)/shard_map/ppermute | solution.py:26
  1798.7 70.5 %collective-permute-start.96 = (f32[12293]{0:T(1024)S(1)}, f32[12293]{0:T(1024)S(1)}, u32[]{:S(2)}, u32[]{:S(2)}) collective-permute-start(f32[12293]{0:T(1024)S(1)} %concatenate.77), channel_id=1, source_target_pairs={{0,1},{1,0},{2,3},{3,2},{4,5},{5,4},{6,7},{7,6},{8,9},{9,8},{10,11... | collective-permute-start | bytes 147524 | tf_op jit(solution)/shard_map/ppermute | solution.py:26
  1869.2 18.1 collective-permute-start.97
  1898.5 199.4 %collective-permute-start.99 = (f32[12293]{0:T(1024)S(1)}, f32[12293]{0:T(1024)S(1)}, u32[]{:S(2)}, u32[]{:S(2)}) collective-permute-start(f32[12293]{0:T(1024)S(1)} %add.395), channel_id=1, source_target_pairs={{0,8},{1,9},{2,10},{3,11},{4,12},{5,13},{6,14},{7,15},{8,0},{9,1},... | collective-permute-start | bytes 147524 | tf_op jit(solution)/shard_map/ppermute | solution.py:26
  1898.6 247.1 %collective-permute-start.57 = (bf16[4,2,2,32,4096]{4,3,0,2,1:T(8,128)(2,1)}, bf16[4,2,2,32,4096]{4,3,0,2,1:T(8,128)(2,1)}, u32[]{:S(2)}, u32[]{:S(2)}) collective-permute-start(bf16[4,2,2,32,4096]{4,3,0,2,1:T(8,128)(2,1)} %bitcast.382), channel_id=1, source_target_pairs={{0,2},{1,3},{2,0},{3,1},{4,6},{5,7},{6,4},{7,5},{8,10},{9,11},{10,... | collective-permute-start | bytes 12582920 | tf_op jit(solution)/shard_map/ppermute | solution.py:26
  2098.0 14.4 collective-permute-start.100
  2108.1 15.1 collective-permute-start.92
  2113.0 16.7 collective-permute-start.87
  2114.8 18.7 collective-permute-start.91
  2124.6 14.9 collective-permute-start.93
  2129.4 20.8 collective-permute-start.89
  2141.3 14.9 collective-permute-start.88
  2142.9 23.8 %collective-permute-start.94 = (bf16[128,1024]{1,0:T(8,128)(2,1)S(1)}, bf16[128,1024]{1,0:T(8,128)(2,1)S(1)}, u32[]{:S(2)}, u32[]{:S(2)}) collective-permute-start(bf16[128,1024]{1,0:T(8,128)(2,1)S(1)} %get-tuple-element.403), channel_id=1, source_target_pairs={{0,16},{1,17},{2,18},{3,19},{4,20},{5,21},{6,22},{7,23},{8,24},{9,... | collective-permute-start | bytes 786440 | tf_op jit(solution)/shard_map/ppermute | solution.py:26
  2143.1 23.7 %collective-permute-start.95 = (bf16[128,1024]{1,0:T(8,128)(2,1)S(1)}, bf16[128,1024]{1,0:T(8,128)(2,1)S(1)}, u32[]{:S(2)}, u32[]{:S(2)}) collective-permute-start(bf16[128,1024]{1,0:T(8,128)(2,1)S(1)} %get-tuple-element.404), channel_id=1, source_target_pairs={{0,24},{1,25},{2,26},{3,27},{4,28},{5,29},{6,30},{7,31},{8,16},{9,... | collective-permute-start | bytes 786440 | tf_op jit(solution)/shard_map/ppermute | solution.py:26
  2149.6 14.0 collective-permute-start.83
  2163.6 15.2 collective-permute-start.78
  2166.1 14.7 collective-permute-start.82
  2166.7 23.4 %collective-permute-start.84 = (bf16[2,32,4096]{2,1,0:T(8,128)(2,1)S(1)}, bf16[2,32,4096]{2,1,0:T(8,128)(2,1)S(1)}, u32[]{:S(2)}, u32[]{:S(2)}) collective-permute-start(bf16[2,32,4096]{2,1,0:T(8,128)(2,1)S(1)} %fusion.88), channel_id=1, source_target_pairs={{0,4},{1,5},{2,6},{3,7},{4,0},{5,1},{6,2},{7,3},{8,12},{9,13},{10,... | collective-permute-start | bytes 1572872 | tf_op jit(solution)/shard_map/ppermute | solution.py:26
  2169.8 54.9 %collective-permute-start.80 = (bf16[2,32,4096]{2,1,0:T(8,128)(2,1)S(1)}, bf16[2,32,4096]{2,1,0:T(8,128)(2,1)S(1)}, u32[]{:S(2)}, u32[]{:S(2)}) collective-permute-start(bf16[2,32,4096]{2,1,0:T(8,128)(2,1)S(1)} %get-tuple-element.381), channel_id=1, source_target_pairs={{0,4},{1,5},{2,6},{3,7},{4,0},{5,1},{6,2},{7,3},{8,12},{9,13},{10,... | collective-permute-start | bytes 1572872 | tf_op jit(solution)/shard_map/ppermute | solution.py:26
  2178.3 43.6 %collective-permute-start.59 = (bf16[4,2,2,32,3072]{4,3,0,2,1:T(8,128)(2,1)S(1)}, bf16[4,2,2,32,3072]{4,3,0,2,1:T(8,128)(2,1)S(1)}, u32[]{:S(2)}, u32[]{:S(2)}) collective-permute-start(bf16[4,2,2,32,3072]{4,3,0,2,1:T(8,128)(2,1)S(1)} %bitcast.455), channel_id=1, source_target_pairs={{0,2},{1,3},{2,0},{3,1},{4,6},{5,7},{6,4},{7,5},{8,10},{9,11},{10,... | collective-permute-start | bytes 9437192 | tf_op jit(solution)/shard_map/ppermute | solution.py:26
  2178.8 23.1 %collective-permute-start.69 = (bf16[2,32,1024]{2,1,0:T(8,128)(2,1)S(1)}, bf16[2,32,1024]{2,1,0:T(8,128)(2,1)S(1)}, u32[]{:S(2)}, u32[]{:S(2)}) collective-permute-start(bf16[2,32,1024]{2,1,0:T(8,128)(2,1)S(1)} %get-tuple-element.402), channel_id=1, source_target_pairs={{0,4},{1,5},{2,6},{3,7},{4,0},{5,1},{6,2},{7,3},{8,12},{9,13},{10,... | collective-permute-start | bytes 393224 | tf_op jit(solution)/shard_map/ppermute | solution.py:26
  2180.8 22.8 %collective-permute-start.73 = (bf16[2,32,1024]{2,1,0:T(8,128)(2,1)S(1)}, bf16[2,32,1024]{2,1,0:T(8,128)(2,1)S(1)}, u32[]{:S(2)}, u32[]{:S(2)}) collective-permute-start(bf16[2,32,1024]{2,1,0:T(8,128)(2,1)S(1)} %get-tuple-element.399), channel_id=1, source_target_pairs={{0,1},{1,0},{2,3},{3,2},{4,5},{5,4},{6,7},{7,6},{8,9},{9,8},{10,11... | collective-permute-start | bytes 393224 | tf_op jit(solution)/shard_map/ppermute | solution.py:26
  2190.1 13.6 collective-permute-start.75
  2203.8 13.1 collective-permute-start.76
  2218.4 34.6 %collective-permute-start.85 = (bf16[32,4096]{1,0:T(8,128)(2,1)S(1)}, bf16[32,4096]{1,0:T(8,128)(2,1)S(1)}, u32[]{:S(2)}, u32[]{:S(2)}) collective-permute-start(bf16[32,4096]{1,0:T(8,128)(2,1)S(1)} %get-tuple-element.405), channel_id=1, source_target_pairs={{0,16},{1,17},{2,18},{3,19},{4,20},{5,21},{6,22},{7,23},{8,24},{9,... | collective-permute-start | bytes 786440 | tf_op jit(solution)/shard_map/ppermute | solution.py:26
  2218.6 34.5 %collective-permute-start.86 = (bf16[32,4096]{1,0:T(8,128)(2,1)S(1)}, bf16[32,4096]{1,0:T(8,128)(2,1)S(1)}, u32[]{:S(2)}, u32[]{:S(2)}) collective-permute-start(bf16[32,4096]{1,0:T(8,128)(2,1)S(1)} %get-tuple-element.406), channel_id=1, source_target_pairs={{0,24},{1,25},{2,26},{3,27},{4,28},{5,29},{6,30},{7,31},{8,16},{9,... | collective-permute-start | bytes 786440 | tf_op jit(solution)/shard_map/ppermute | solution.py:26
  2236.8 16.3 collective-permute-start.81
  (139 other events, 4918.7 us)

commit v2 on v1

--- a/solution.py
+++ b/solution.py
@@ -12,6 +12,7 @@
 HD = 64
 
 AXES = ("dp", "ctx")
+X = 1
 
 
 def my_index():
@@ -25,129 +26,367 @@
 def swap(array, bits):
     return lax.ppermute(array, AXES, [(i, i ^ bits) for i in range(n_devices())])
 
-
-def after(array, *others):
-    return lax.optimization_barrier((array, *others))[0]
-
-
-X, CORE, Y, Z = 1, 2, 4, 8
-
-
-def reorder(pieces, blocks, to_shape, moves):
-    plan = moves
+MESH = pl.DeviceIdType.MESH
+
+
+class Place:
+    def __init__(self):
+        dp = lax.axis_index("dp")
+        self.nz = lax.axis_size("dp") // 4
+        self.x = lax.axis_index("ctx")
+        self.c = dp % 2
+        self.y = (dp // 2) % 2
+        self.z = dp // 4
+
+    def zth(self, k):
+        z, bit = self.z, 1
+        while bit < self.nz:
+            if k & bit:
+                z = z + bit * (1 - 2 * ((self.z // bit) % 2))
+            bit *= 2
+        return z
+
+    def flips(self, y=0, c=0, x=0):
+        return (
+            1 - self.y if y else self.y,
+            1 - self.c if c else self.c,
+            1 - self.x if x else self.x,
+        )
+
+    def device(self, k=0, y=0, c=0, x=0):
+        fy, fc, fx = self.flips(y, c, x)
+        return ((self.zth(k) * 2 + fy) * 2 + fc, fx)
+
+    def shard(self, k=0, y=0, c=0, x=0):
+        fy, fc, fx = self.flips(y, c, x)
+        return ((self.zth(k) * 2 + fy) * 2 + fc) * 2 + fx
+
+    def column(self, y=0, c=0, x=0):
+        fy, fc, fx = self.flips(y, c, x)
+        return (fy * 2 + fc) * 2 + fx
+
+    def partners(self):
+        return [self.device(k=k) for k in range(1, self.nz)] + [
+            self.device(x=1),
+            self.device(y=1),
+            self.device(c=1),
+        ]
+
+
+def meet(place):
+    barrier = pltpu.get_barrier_semaphore()
+    partners = place.partners()
+    for partner in partners:
+        pl.semaphore_signal(barrier, inc=1, device_id=partner, device_id_type=MESH)
+    pl.semaphore_wait(barrier, len(partners))
+
+
+class Sender:
+    def __init__(self, send_sem, recv_sem):
+        self.send_sem, self.recv_sem = send_sem, recv_sem
+        self.count = 0
+        self.open = []
+
+    def send(self, src, dst, device):
+        copy = pltpu.make_async_remote_copy(
+            src_ref=src,
+            dst_ref=dst,
+            send_sem=self.send_sem.at[self.count],
+            recv_sem=self.recv_sem.at[self.count],
+            device_id=device,
+            device_id_type=MESH,
+        )
+        self.count += 1
+        copy.start()
+        self.open.append(copy)
+        return copy
+
+    def close(self):
+        for copy in self.open:
+            copy.wait_send()
+        self.open = []
+
+
+def gather_copies(nz):
+    return (nz - 1) + 2 * (nz + 2) + 5
+
+
+def gather_steps(place, sender, shard, full):
+    nz = place.nz
+    half = nz // 2
+    mine = place.column()
+    own = full.at[place.z, mine]
+    by_z = [sender.send(shard, own, place.device(k=k)) for k in range(1, nz)]
+    from_x = [sender.send(shard, own, place.device(x=1))]
+    from_y = [sender.send(shard, own, place.device(y=1))]
+    yield
+    for k in range(1, nz):
+        by_z[k - 1].wait_recv()
+        piece = full.at[place.zth(k), mine]
+        from_x.append(sender.send(piece, piece, place.device(x=1)))
+        from_y.append(sender.send(piece, piece, place.device(y=1)))
+    line = full.at[:, mine]
+    to_core = [sender.send(line, line, place.device(c=1))]
+    yield
+    for copy in from_x:
+        copy.wait_recv()
+    at_x = place.column(x=1)
+    line = full.at[:, at_x]
+    part = full.at[pl.ds(0, half), at_x]
+    diag_a = sender.send(part, part, place.device(y=1))
+    to_core.append(sender.send(line, line, place.device(c=1)))
+    yield
+    for copy in from_y:
+        copy.wait_recv()
+    at_y = place.column(y=1)
+    line = full.at[:, at_y]
+    part = full.at[pl.ds(half, nz - half), at_y]
+    diag_b = sender.send(part, part, place.device(x=1))
+    to_core.append(sender.send(line, line, place.device(c=1)))
+    yield
+    diag = place.column(x=1, y=1)
+    for copy, start, size in ((diag_a, 0, half), (diag_b, half, nz - half)):
+        copy.wait_recv()
+        part = full.at[pl.ds(start, size), diag]
+        to_core.append(sender.send(part, part, place.device(c=1)))
+    yield
+    for copy in to_core:
+        copy.wait_recv()
+
+
+def gather_kernel(shapes, nz):
+    count = len(shapes)
 
     def kernel(*refs):
-        sources, out, sem = refs[: len(pieces)], refs[len(pieces)], refs[len(pieces) + 1]
-        me = my_index()
-        copies = [
-            pltpu.make_async_copy(sources[p].at[b], out.at[jnp.bitwise_xor(me, place)], sem.at[i])
-            for i, (p, b, place) in enumerate(plan)
+        shards, given = refs[:count], refs[count]
+        fulls, taken = refs[count + 1 : 2 * count + 1], refs[2 * count + 1]
+        send_sem, recv_sem, own_sem = refs[2 * count + 2 :]
+        place = Place()
+        sender = Sender(send_sem, recv_sem)
+        kept = [
+            pltpu.make_async_copy(shard, full.at[place.z, place.column()], own_sem.at[i])
+            for i, (shard, full) in enumerate(zip(shards, fulls))
         ]
-        for copy in copies:
+        for copy in kept:
             copy.start()
-        for copy in copies:
+        meet(place)
+        for copy in kept:
             copy.wait()
-
+        steps = [gather_steps(place, sender, s, f) for s, f in zip(shards, fulls)]
+        swapped = None
+        t = 0
+        while steps:
+            live = []
+            for i, step in enumerate(steps):
+                if i > t:
+                    live.append(step)
+                    continue
+                try:
+                    next(step)
+                    live.append(step)
+                except StopIteration:
+                    pass
+            steps = live
+            if t == 1:
+                swapped = sender.send(given, taken, place.device(x=1))
+            t += 1
+        swapped.wait_recv()
+        sender.close()
+
+    return kernel
+
+
+def gather_all(shards, block_input, collective_id):
+    nz = lax.axis_size("dp") // 4
+    copies = len(shards) * gather_copies(nz) + 1
+    results = pl.pallas_call(
+        gather_kernel([s.shape for s in shards], nz),
+        out_shape=[jax.ShapeDtypeStruct((nz, 8) + s.shape, s.dtype) for s in shards]
+        + [jax.ShapeDtypeStruct(block_input.shape, block_input.dtype)],
+        in_specs=[pl.BlockSpec(memory_space=pltpu.VMEM)] * (len(shards) + 1),
+        out_specs=[pl.BlockSpec(memory_space=pl.ANY)] * (len(shards) + 1),
+        scratch_shapes=[
+            pltpu.SemaphoreType.DMA((copies,)),
+            pltpu.SemaphoreType.DMA((copies,)),
+            pltpu.SemaphoreType.DMA((len(shards),)),
+        ],
+        compiler_params=pltpu.CompilerParams(
+            collective_id=collective_id, has_side_effects=True, vmem_limit_bytes=16 << 20
+        ),
+    )(*shards, block_input)
+    return results
+
+
+def reduce_copies(nz):
+    return 4 + 2 + 2 + 2 + nz - 1
+
+
+def reduce_buffers(nz, rows, cols):
+    low = jnp.bfloat16
+    half = nz // 2
+    return [
+        pltpu.VMEM((4, nz, rows, cols), low),
+        pltpu.VMEM((4, nz, rows, cols), low),
+        pltpu.VMEM((half, rows, cols), low),
+        pltpu.VMEM((nz - half, rows, cols), low),
+        pltpu.VMEM((2, nz, rows, cols), low),
+        pltpu.VMEM((nz - 1, rows, cols), low),
+    ]
+
+
+def add_rows(target, terms, count, rows):
+    step = min(rows, 16)
+    per = rows // step
+
+    def one(j, _):
+        i, start = j // per, (j % per) * step
+        at = pl.ds(pl.multiple_of(start, step), step)
+        total = terms[0](i, at).astype(jnp.float32)
+        for term in terms[1:]:
+            total = total + term(i, at).astype(jnp.float32)
+        target(i, at, total)
+        return 0
+
+    lax.fori_loop(0, count * per, one, 0)
+
+
+def reduce_steps(place, sender, grad, buffers, out):
+    from_core, sums, diag_y, diag_x, from_xy, from_z = buffers
+    nz, half = place.nz, place.nz // 2
+    rows = grad.shape[2]
+    low = jnp.bfloat16
+    groups = ((1, 1), (0, 1), (1, 0), (0, 0))
+    by_core = [
+        sender.send(grad.at[:, place.column(y=fy, c=1, x=fx)], from_core.at[i], place.device(c=1))
+        for i, (fy, fx) in enumerate(groups)
+    ]
+    yield
+
+    def put(slot, offset=0):
+        def store(i, at, value):
+            sums[slot, i + offset, at, :] = value.astype(low)
+
+        return store
+
+    def add_core(slot):
+        fy, fx = groups[slot]
+        column = place.column(y=fy, x=fx)
+        by_core[slot].wait_recv()
+        add_rows(
+            put(slot),
+            [lambda i, at: grad[i, column, at, :], lambda i, at: from_core[slot, i, at, :]],
+            nz,
+            rows,
+        )
+
+    low_z, high_z = pl.ds(0, half), pl.ds(half, nz - half)
+    add_core(0)
+    by_y = sender.send(sums.at[0, low_z], diag_y, place.device(y=1))
+    by_x = sender.send(sums.at[0, high_z], diag_x, place.device(x=1))
+    add_core(1)
+    x_high = sender.send(sums.at[1, high_z], from_xy.at[0, high_z], place.device(x=1))
+    add_core(2)
+    y_low = sender.send(sums.at[2, low_z], from_xy.at[1, low_z], place.device(y=1))
+    yield
+    add_core(3)
+    by_y.wait_recv()
+    add_rows(
+        put(1),
+        [lambda i, at: sums[1, i, at, :], lambda i, at: diag_y[i, at, :]],
+        half,
+        rows,
+    )
+    x_low = sender.send(sums.at[1, low_z], from_xy.at[0, low_z], place.device(x=1))
+    by_x.wait_recv()
+    add_rows(
+        put(2, half),
+        [lambda i, at: sums[2, i + half, at, :], lambda i, at: diag_x[i, at, :]],
+        nz - half,
+        rows,
+    )
+    y_high = sender.send(sums.at[2, high_z], from_xy.at[1, high_z], place.device(y=1))
+    yield
+    for copy in (x_high, y_low, x_low, y_high):
+        copy.wait_recv()
+    add_rows(
+        put(3),
+        [
+            lambda i, at: sums[3, i, at, :],
+            lambda i, at: from_xy[0, i, at, :],
+            lambda i, at: from_xy[1, i, at, :],
+        ],
+        nz,
+        rows,
+    )
+    by_z = [
+        sender.send(sums.at[3, place.zth(k)], from_z.at[k - 1], place.device(k=k)) for k in range(1, nz)
+    ]
+    yield
+    for copy in by_z:
+        copy.wait_recv()
+
+    def last(i, at, value):
+        out[at, :] = value
+
+    add_rows(
+        last,
+        [lambda i, at: sums[3, place.z, at, :]]
+        + [lambda i, at, k=k: from_z[k, at, :] for k in range(nz - 1)],
+        1,
+        rows,
+    )
+
+
+def reduce_kernel(shapes):
+    count = len(shapes)
+
+    def kernel(*refs):
+        grads, outs = refs[:count], refs[count : 2 * count]
+        scratch = refs[2 * count :]
+        buffers = [scratch[6 * i : 6 * i + 6] for i in range(count)]
+        send_sem, recv_sem = scratch[6 * count :]
+        place = Place()
+        sender = Sender(send_sem, recv_sem)
+        meet(place)
+        steps = [reduce_steps(place, sender, g, b, o) for g, b, o in zip(grads, buffers, outs)]
+        t = 0
+        while steps:
+            live = []
+            for i, step in enumerate(steps):
+                if i > t:
+                    live.append(step)
+                    continue
+                try:
+                    next(step)
+                    live.append(step)
+                except StopIteration:
+                    pass
+            steps = live
+            t += 1
+        sender.close()
+
+    return kernel
+
+
+def reduce_all(grads, collective_id):
+    nz = lax.axis_size("dp") // 4
+    n = nz * 8
+    blocks = [g.reshape(nz, 8, g.shape[0] // n, g.shape[1]) for g in grads]
+    copies = len(grads) * reduce_copies(nz)
+    scratch = []
+    for block in blocks:
+        scratch += reduce_buffers(nz, block.shape[2], block.shape[3])
     return pl.pallas_call(
-        kernel,
-        out_shape=jax.ShapeDtypeStruct(to_shape, pieces[0].dtype),
-        in_specs=[pl.BlockSpec(memory_space=pl.ANY)] * len(pieces),
-        out_specs=pl.BlockSpec(memory_space=pl.ANY),
-        scratch_shapes=[pltpu.SemaphoreType.DMA((len(plan),))],
-    )(*pieces)
-
-
-def gather_pieces(shard, first):
-    nz = n_devices() // Z
-    half = nz // 2
-    shard = after(shard, *first)
-    others = [swap(shard, Z * k) for k in range(1, nz)]
-    own = jnp.stack([shard] + others)
-    from_x = swap(own, X)
-    from_y = swap(own, Y)
-    diag_a = swap(from_x[:half], Y)
-    diag_b = swap(from_y[half:], X)
-    mine = [(own, 0, 0), (from_x, X, 0), (from_y, Y, 0), (diag_a, X | Y, 0), (diag_b, X | Y, half)]
-    theirs = [(swap(p, CORE), bits | CORE, k) for p, bits, k in mine]
-    return mine + theirs, others
-
-
-def assemble(placed, rows):
-    n = n_devices()
-    pieces = [p for p, _, _ in placed]
-    plan = []
-    for i, (p, bits, start) in enumerate(placed):
-        for k in range(p.shape[0]):
-            plan.append((i, k, bits | (Z * (start + k))))
-    shape = (n,) + pieces[0].shape[1:]
-    return reorder(pieces, None, shape, plan).reshape(n * shape[1], shape[2])
-
-
-def scatter_sum(grad, first):
-    n = n_devices()
-    nz = n // Z
-    half = nz // 2
-    rows, cols = grad.shape
-    r = rows // n
-    rel = reorder_rel(grad.reshape(n, r, cols)).reshape(nz, 2, 2, 2, r, cols)
-    f32 = jnp.float32
-    low = jnp.bfloat16
-    sent = rel[:, :, 1]
-    got = swap(after(sent, *first), CORE)
-    total = rel[:, :, 0].astype(f32) + got.astype(f32)
-    own = total[:, 0, 0].astype(low)
-    to_x = total[:, 0, 1].astype(low)
-    to_y = total[:, 1, 0].astype(low)
-    diag = total[:, 1, 1].astype(low)
-    to_x_a = (to_x[:half].astype(f32) + swap(diag[:half], Y).astype(f32)).astype(low)
-    to_y_b = (to_y[half:].astype(f32) + swap(diag[half:], X).astype(f32)).astype(low)
-    got_x_b = swap(to_x[half:], X)
-    got_y_a = swap(to_y[:half], Y)
-    got_x_a = swap(to_x_a, X)
-    got_y_b = swap(to_y_b, Y)
-    own_a = own[:half].astype(f32) + got_x_a.astype(f32) + got_y_a.astype(f32)
-    own_b = own[half:].astype(f32) + got_x_b.astype(f32) + got_y_b.astype(f32)
-    line = jnp.concatenate([own_a, own_b], axis=0)
-    out = line[0]
-    line = line.astype(low)
-    for k in range(1, nz):
-        out = out + swap(line[k], Z * k).astype(f32)
-    return out, got
-
-
-def reorder_rel(grad):
-    n = grad.shape[0]
-    plan = [(0, s, s) for s in range(n)]
-
-    def kernel(src, out, sem):
-        me = my_index()
-        copies = [
-            pltpu.make_async_copy(src.at[jnp.bitwise_xor(me, s)], out.at[s], sem.at[s]) for s in range(n)
-        ]
-        for copy in copies:
-            copy.start()
-        for copy in copies:
-            copy.wait()
-
-    return pl.pallas_call(
-        kernel,
-        out_shape=jax.ShapeDtypeStruct(grad.shape, grad.dtype),
-        in_specs=[pl.BlockSpec(memory_space=pl.ANY)],
-        out_specs=pl.BlockSpec(memory_space=pl.ANY),
-        scratch_shapes=[pltpu.SemaphoreType.DMA((n,))],
-    )(grad)
-
-
-def gather_small(vector):
-    n = n_devices()
-    rel = vector[None, :]
-    bit = 1
-    while bit < n:
-        rel = jnp.concatenate([rel, swap(rel, bit)], axis=0)
-        bit *= 2
-    place = jnp.bitwise_xor(jnp.arange(n, dtype=jnp.int32), my_index())
-    pick = (place[:, None] == jnp.arange(n, dtype=jnp.int32)[None, :]).astype(vector.dtype)
-    return jnp.dot(pick, rel, preferred_element_type=jnp.float32)
+        reduce_kernel([b.shape for b in blocks]),
+        out_shape=[jax.ShapeDtypeStruct(b.shape[2:], jnp.float32) for b in blocks],
+        in_specs=[pl.BlockSpec(memory_space=pltpu.VMEM)] * len(grads),
+        out_specs=[pl.BlockSpec(memory_space=pltpu.VMEM)] * len(grads),
+        scratch_shapes=scratch
+        + [pltpu.SemaphoreType.DMA((copies,)), pltpu.SemaphoreType.DMA((copies,))],
+        compiler_params=pltpu.CompilerParams(
+            collective_id=collective_id, has_side_effects=True, vmem_limit_bytes=56 << 20
+        ),
+    )(*blocks)
 
 
 def sum_small(vector):
@@ -216,32 +455,20 @@
     rows = items * half_len
     f32, low = jnp.float32, jnp.bfloat16
     n = n_devices()
-    by_hand = (w_qkv.shape[0] % 16 == 0) and n % Z == 0
     positions = lax.axis_index("ctx") * half_len + jnp.arange(half_len, dtype=jnp.int32)
     other_positions = (1 - lax.axis_index("ctx")) * half_len + jnp.arange(half_len, dtype=jnp.int32)
     key_pos = jnp.concatenate([positions, other_positions])
     valid = (positions[None, :] < lengths[:, None]) & ((mask == 1) | (positions[None, :] == 0))
     code_local = jnp.where(valid, blocks.astype(f32), code_absent)
-    small = jnp.concatenate([b_in, biases.reshape(-1), gains.reshape(-1), shifts.reshape(-1)])
-    if by_hand:
-        placed, last = gather_pieces(w_qkv, ())
-        w_qkv_all = assemble(placed, rows)
-        input_other = swap(after(block_input, *last), X)
-        placed, last = gather_pieces(w_o, last)
-        w_o_all = assemble(placed, rows)
-        placed, last = gather_pieces(w_in, last)
-        w_in_all = assemble(placed, rows)
-        placed, last = gather_pieces(w_out, last)
-        w_out_all = assemble(placed, rows)
-    else:
-        input_other = swap(block_input, X)
-        w_qkv_all, w_o_all, w_in_all, w_out_all = (
-            lax.all_gather(w, AXES, axis=0, tiled=True) for w in (w_qkv, w_o, w_in, w_out)
-        )
-    small_all = gather_small(small)
-    code_all = jnp.concatenate([code_local, swap(code_local, X)], axis=1)
     share = width // n
     b_count = b_in.shape[0]
+    small = jnp.concatenate([b_in, biases.reshape(-1), gains.reshape(-1), shifts.reshape(-1)])
+    small = jnp.pad(small.astype(f32), (0, 1024 - small.shape[0])).reshape(8, 128)
+    gathered = gather_all([w_qkv, small, w_o, w_in, w_out], block_input.reshape(rows, width), 1)
+    w_qkv_all, small_all, w_o_all, w_in_all, w_out_all = (g.reshape(-1, g.shape[-1]) for g in gathered[:5])
+    input_other = gathered[5].reshape(block_input.shape)
+    small_all = small_all.reshape(n, 1024)[:, : b_count + 8 * share]
+    code_all = jnp.concatenate([code_local, swap(code_local, X)], axis=1)
     b_in_full = small_all[:, :b_count].reshape(-1)
     rest = small_all[:, b_count:].reshape(n, 8, share).transpose(1, 0, 2).reshape(8, width)
     bias_full, gain_full, shift_full = rest[:4], rest[4:6], rest[6:8]
@@ -310,23 +537,16 @@
     )
     branch_grad = dres_two.astype(jnp.bfloat16)
 
-    if by_hand:
-        share_sum = lambda part, first: scatter_sum(part.astype(low), first)
-    else:
-        share_sum = lambda part, first: (
-            lax.psum_scatter(part, AXES, scatter_dimension=0, tiled=True),
-            part,
-        )
-    grad_out, got = share_sum(inner(act_low, branch_grad), ())
+    grad_out_part = inner(act_low, branch_grad).astype(low)
     act_grad = back_project(branch_grad, w_out_all)
     _, gelu_back = jax.vjp(partial(jax.nn.gelu, approximate=False), pre)
     pre_grad = gelu_back(act_grad)[0].astype(jnp.bfloat16)
-    grad_in, got = share_sum(inner(hidden_low, pre_grad), (got,))
+    grad_in_part = inner(hidden_low, pre_grad).astype(low)
     dhidden = dres_two + back_project(pre_grad, w_in_all)
     _, norm_one_back = jax.vjp(layer_norm, resid_one, gain_full[0], shift_full[0])
     dres_one, gain_one_grad, shift_one_grad = norm_one_back(dhidden)
     attn_grad = dres_one.astype(jnp.bfloat16)
-    grad_o, got = share_sum(inner(mixed_low, attn_grad), (got,))
+    grad_o_part = inner(mixed_low, attn_grad).astype(low)
     mixed_grad = (
         back_project(attn_grad, w_o_all).astype(jnp.bfloat16).reshape(items, half_len, HEADS, HD)
     )
@@ -361,7 +581,9 @@
     key_grad_low = (key_part[:, :half_len] + back[0]).reshape(rows, width).astype(jnp.bfloat16)
     value_grad_low = (value_part[:, :half_len] + back[1]).reshape(rows, width).astype(jnp.bfloat16)
     joint_grad = jnp.concatenate([query_grad_low, key_grad_low, value_grad_low], axis=1)
-    grad_qkv, got = share_sum(inner(stream_low, joint_grad), (got,))
+    grad_qkv_part = inner(stream_low, joint_grad).astype(low)
+    grad_out, grad_in = reduce_all([grad_out_part, grad_in_part], 2)
+    grad_qkv, grad_o = reduce_all([grad_qkv_part, grad_o_part], 3)
     input_grad = (
         (dres_one + back_project(joint_grad, w_qkv_all))
         .astype(jnp.bfloat16)

time: 2270 us -> 811 us (0.36)
  Pallas kernels: 1540 us -> 316 us
  waiting for transfers between devices: 169 us -> 64.5 us
  starting transfers between devices: 105 us -> 13.8 us
  other arithmetic: 88.7 us -> 64.7 us
    pallas_call x8 -> x3, Pallas kernels: 1540 us -> 316 us  [the longest x2 165 us: reduce_all(): pl.pallas_call(reduce_kernel([b.shape for b in blocks]), out_shape=[jax.S...]
    ppermute x101 -> x7, waiting for transfers between devices: 169 us -> 64.5 us  [swap(): lax.ppermute(array, AXES, [(i, i ^ bits) for i in range(n_devices())])]
    ppermute x101 -> x7, starting transfers between devices: 105 us -> 13.8 us  [swap(): lax.ppermute(array, AXES, [(i, i ^ bits) for i in range(n_devices())])]
    slice x16 -> x0, local copies, waits for them, and re-layouts: 26.5 us -> none  [the longest x4 15.3 us: scatter_sum(): total = rel[:, :, 0].astype(f32) + got.astype(f32)]
  transfers between devices with their start and end apart: 101 -> 7, of which waited for: 34 -> 1; matrix products, arithmetic and copies ran while one was open for 13% -> 20% of each run, Pallas kernels for 57% -> 39%
where the time goes in v2:
time: 811 us; the launch traced here: 801 us
  Pallas kernels  316 us (39%)
  matrix products  209 us (26%)
  local copies, waits for them, and re-layouts  130 us (16%)
  other arithmetic  64.7 us (8%)
  waiting for transfers between devices  64.5 us (8%)
  starting transfers between devices  13.8 us (2%)
    pallas_call x2, Pallas kernels, reduce_all(): pl.pallas_call(reduce_kernel([b.shape for b in blocks]), out_shape=[jax.S...  165 us
    pallas_call x1, Pallas kernels, gather_all(): pl.pallas_call(gather_kernel([s.shape for s in shards], nz), out_shape=[j...  151 us
    ppermute x7, waiting for transfers between devices, swap(): lax.ppermute(array, AXES, [(i, i ^ bits) for i in range(n_devices())])  64.5 us
    unnamed x129, local copies, waits for them, and re-layouts  43 us
    dot_general x4, matrix products, back_project(): lax.dot_general(grad, weight, (((1,), (1,)), ((), ())), preferred_element...  41.9 us
    dot_general x4, matrix products, inner(): lax.dot_general(left, right, (((0,), (0,)), ((), ())), preferred_element_...  37.6 us
    dot_general x1, matrix products, body(): jnp.dot(hidden_low, w_in_all, preferred_element_type=jnp.float32)  37.3 us
    dot_general x6, matrix products, scores_of(): jnp.einsum('qhd,khd->hqk', query, keys, preferred_element_type=jnp.float32)  16.8 us
  transfers between devices with their start and end apart: 7, of which 1 were waited for; matrix products, arithmetic and copies ran while one was open for 20% of the time, Pallas kernels for 39%

profile of v2, /device:TPU:0, one launch (start us, length us, event | category | flops | bytes accessed | tf_op | source)
XLA Modules:
  0.0 801.2 jit_solution(18320876250109665988)
XLA Ops:
  2.0 2.9 collective-permute-start
  13.0 151.3 %shard_map.221 = (bf16[4,8,32,3072]{3,2,1,0:T(8,128)(2,1)S(1)}, f32[4,8,8,128]{3,2,1,0:T(8,128)S(1)}, bf16[4,8,32,1024]{3,2,1,0:T(8,128)(2,1)S(1)}, bf16[4,8,32,...) custom-call(bf16[32,3072]{1,0:T(8,128)(2,1)S(1)} %copy-done.4, ...), custom_call_target="tpu_custom_call" | custom-call | tf_op jit(solution)/shard_map/pallas_call | solution.py:202
  164.3 3.2 copy-done.6
  167.5 3.2 copy-done.7
  171.6 3.3 multiply_reduce_fusion.4
  175.4 5.3 fusion.60
  180.6 7.5 fusion.104
  188.7 3.3 slice.215
  192.1 3.3 slice.216
  195.4 6.9 fusion.66
  202.2 2.6 copy.51
  204.8 5.3 concatenate.36
  210.1 2.6 copy.52
  212.7 5.3 concatenate.37
  217.9 2.6 copy.55
  220.5 5.2 concatenate.42
  228.3 5.7 concatenate.41
  234.1 6.7 pad_maximum_fusion.1
  240.8 4.4 pad_maximum_fusion.2
  245.3 4.8 copy.56
  250.1 5.2 reshape.396
  255.3 5.0 copy.57
  260.3 4.7 copy.58
  268.6 32.3 %while.28 = (s32[]{:T(128)}, bf16[3,256,16,64]{1,3,2,0:T(8,128)(2,1)}, f32[3,16,256]{2,1,0:T(8,128)}, bf16[3,512,16,64]{1,3,2,0:T(8,128)(2,1)}, f32[3,512]{1,0:T...) while((s32[]{:T(128)}, ...), condition=%wide.region_3.4_spmd.clone, body=%wide.region_0.3_spmd.clone.sunk | while | flops 562426112 | bytes 29507192 | solution.py:512
  268.8 3.1 fusion.143
  274.8 4.5 fusion.145
  279.5 3.1 fusion.143
  285.5 4.5 fusion.145
  290.2 3.1 fusion.143
  296.2 4.5 fusion.145
  301.0 2.9 copy.59
  304.4 2.8 fusion.102
  308.6 37.3 %multiply_convert_fusion.1 = (bf16[768,4096]{1,0:T(8,128)(2,1)S(1)}, f32[768,4096]{1,0:T(8,128)}, f32[768,4096]{1,0:T(8,128)}) fusion(f32[4096]{0:T(1024)S(1)} %slice_bitcast_fusion.2, bf16[1024,4096]{1,0:T(8,128)(2,1)S(1)} %bitcast.226, f32[768,1024]{1,0:T(8,128)S(1)} %get-tuple-element.361, f32[1024]{0:T(1024)S(1)} %add.219, f32[1024]{0:T(1024)S(1)} %mul.255, ...), kind=kOutput, calls=%fused_computation.72 | convolution fusion | flops 6654001152 | bytes 43022336 | tf_op jit(solution)/shard_map/dot_general | solution.py:520
  346.0 7.7 fusion.100
  355.2 3.4 fusion.72
  361.7 20.9 %convert_reduce_fusion = (f32[4096]{0:T(1024)S(1)}, bf16[768,4096]{1,0:T(8,128)(2,1)}) fusion(f32[768,4096]{1,0:T(8,128)} %get-tuple-element.359, f32[768,4096]{1,0:T(8,128)} %get-tuple-element.382, f32[4096]{0:T(1024)S(1)} %slice_bitcast_fusion.2, bf16[768,1024]{1,0:T(8,128)(2,1)} %get-tuple-element.345, bf16[4096,1024]{1,0:T(8,128)(2,1)} %bitcast.227), kind=kOutput, calls=%fused_computation.70 | convolution fusion | flops 6495924224 | bytes 41451520 | tf_op jit(solution)/shard_map/dot_general | solution.py:425
  382.7 12.5 %multiply_reduce_fusion.5 = (f32[1024]{0:T(1024)S(1)}, f32[768]{0:T(1024)S(1)}, f32[1024]{0:T(1024)S(1)}, f32[768,1024]{1,0:T(8,128)S(1)}) fusion(f32[768,1024]{1,0:T(8,128)} %copy-done.18, f32[768]{0:T(1024)S(1)} %fusion.84, f32[768]{0:T(1024)S(1)} %broadcast_multiply_fusion.1, f32[1024]{0:T(1024)S(1)} %mul.255, ...), kind=kOutput, calls=%fused_computation.128 | convolution fusion | flops 6450312192 | bytes 24141824 | tf_op jit(solution)/shard_map/dot_general | solution.py:425
  401.1 3.3 reshape.395
  404.4 5.2 copy.63
  411.0 63.6 %while.29 = (s32[]{:T(128)}, bf16[3,256,16,64]{1,3,2,0:T(8,128)(2,1)}, f32[3,512,16,64]{1,3,2,0:T(8,128)}, f32[3,512,16,64]{1,3,2,0:T(8,128)}, bf16[3,512,16,64]...) while((s32[]{:T(128)}, ...), condition=%wide.region_14.15_spmd.clone, body=%wide.region_12.14_spmd.clone.sunk | while | flops 1374810368 | bytes 92932320 | solution.py:572
  415.8 4.7 multiply_reduce_fusion.10
  422.9 3.3 bitcast_dynamic-update-slice_fusion.7
  428.8 3.4 bitcast_dynamic-update-slice_fusion.8
  437.0 4.7 multiply_reduce_fusion.10
  444.1 3.4 bitcast_dynamic-update-slice_fusion.7
  450.0 3.4 bitcast_dynamic-update-slice_fusion.8
  458.2 4.7 multiply_reduce_fusion.10
  465.3 3.3 bitcast_dynamic-update-slice_fusion.7
  471.2 3.4 bitcast_dynamic-update-slice_fusion.8
  474.6 3.2 fusion.77
  481.5 3.5 bitcast_convert_fusion
  486.1 64.5 %collective-permute-done.1 = bf16[2,3,256,1024]{2,3,1,0:T(8,128)(2,1)} collective-permute-done((bf16[2,3,256,1024]{2,3,1,0:T(8,128)(2,1)}, bf16[2,3,256,1024]{2,3,1,0:T(8,128)(2,1)}, u32[]{:S(2)}, u32[]{:S(2)}) %collective-permute-start.1) | collective-permute-done | bytes 3145760 | tf_op jit(solution)/shard_map/ppermute | solution.py:27
  553.1 4.9 convert_reduce_fusion.4
  558.0 3.3 concatenate.45
  562.8 11.5 %convolution_convert_fusion.1 = bf16[4096,1024]{1,0:T(8,128)(2,1)} fusion(bf16[768,4096]{1,0:T(8,128)(2,1)} %copy-done.55, bf16[768,1024]{1,0:T(8,128)(2,1)} %get-tuple-element.345), kind=kOutput, calls=%fused_computation.87 | convolution fusion | flops 6446645248 | bytes 16252928 | tf_op jit(solution)/shard_map/dot_general | solution.py:419
  574.5 12.2 %convolution_convert_fusion = bf16[1024,4096]{1,0:T(8,128)(2,1)} fusion(bf16[768,4096]{1,0:T(8,128)(2,1)} %get-tuple-element.351, f32[768,1024]{1,0:T(8,128)S(1)} %copy-done.20, f32[1024]{0:T(1024)S(1)} %copy-done.50, f32[1024]{0:T(1024)S(1)} %mul.255, f32[768]{0:T(1024)S(1)} %fusion.84, f32[768]{0:T(1024)S(1)} %broadcast_multiply_fusion.1), kind=kOutput, calls=%fused_computation.86 | convolution fusion | flops 6450577408 | bytes 17840128 | tf_op jit(solution)/shard_map/dot_general | solution.py:419
  588.3 3.2 convolution_convert_fusion.3
  592.8 103.0 %shard_map.223 = (f32[128,1024]{1,0:T(8,128)}, f32[32,4096]{1,0:T(8,128)}) custom-call(bf16[4,8,128,1024]{3,2,1,0:T(8,128)(2,1)} %bitcast.240, bf16[4,8,32,4096]{3,2,1,0:T(8,128)(2,1)} %bitcast.241), custom_call_target="tpu_custom_call" | custom-call | tf_op jit(solution)/shard_map/pallas_call | solution.py:379
  699.2 2.6 copy.68
  703.7 2.7 copy.69
  706.5 5.3 collective-permute-start.5
  711.8 10.7 %convolution_convert_fusion.2 = bf16[1024,3072]{1,0:T(8,128)(2,1)} fusion(bf16[768,1024]{1,0:T(8,128)(2,1)} %bitcast_convert_fusion, bf16[768,1024]{0,1:T(8,128)(2,1)} %copy.69, bf16[768,1024]{0,1:T(8,128)(2,1)} %copy.68, bf16[768,1024]{0,1:T(8,128)(2,1)} %bitcast.252), kind=kOutput, calls=%fused_computation.88 | convolution fusion | flops 4849139712 | bytes 12582912 | tf_op jit(solution)/shard_map/dot_general | solution.py:419
  723.5 6.6 add_convert_fusion.1
  730.1 62.1 %shard_map.222 = (f32[32,3072]{1,0:T(8,128)}, f32[32,1024]{1,0:T(8,128)}) custom-call(bf16[4,8,32,3072]{3,2,1,0:T(8,128)(2,1)} %bitcast.244, bf16[4,8,32,1024]{3,2,1,0:T(8,128)(2,1)} %bitcast.249), custom_call_target="tpu_custom_call" | custom-call | tf_op jit(solution)/shard_map/pallas_call | solution.py:379
  (271 shorter events, 94.9 us)
Async XLA Ops:
  2.0 265.2 %collective-permute-start = (f32[3,256]{1,0:T(4,128)S(1)}, f32[3,256]{1,0:T(4,128)S(1)}, u32[]{:S(2)}, u32[]{:S(2)}) collective-permute-start(f32[3,256]{1,0:T(4,128)S(1)} %get-tuple-element.362), channel_id=1, source_target_pairs={{0,1},{1,0},{2,3},{3,2},{4,5},{5,4},{6,7},{7,6},{8,9},{9,8},{10,11... | collective-permute-start | bytes 9224 | tf_op jit(solution)/shard_map/ppermute | solution.py:27
  13.0 158.6 %copy-start.1 = (bf16[3,256,1024]{2,1,0:T(8,128)(2,1)S(1)}, bf16[3,256,1024]{2,1,0:T(8,128)(2,1)}, u32[]{:S(2)}) copy-start(bf16[3,256,1024]{2,1,0:T(8,128)(2,1)} %param.18) | copy-start | bytes 4718596
  164.3 3.2 copy-start.6
  167.5 3.2 copy-start.7
  170.7 9.9 %copy-start.8 = (bf16[4,8,32,3072]{3,2,1,0:T(8,128)(2,1)}, bf16[4,8,32,3072]{3,2,1,0:T(8,128)(2,1)S(1)}, u32[]{:S(2)}) copy-start(bf16[4,8,32,3072]{3,2,1,0:T(8,128)(2,1)S(1)} %get-tuple-element.143) | copy-start | bytes 18874372
  170.7 133.6 %copy-start.9 = (bf16[4,8,32,1024]{3,2,1,0:T(8,128)(2,1)}, bf16[4,8,32,1024]{3,2,1,0:T(8,128)(2,1)S(1)}, u32[]{:S(2)}) copy-start(bf16[4,8,32,1024]{3,2,1,0:T(8,128)(2,1)S(1)} %get-tuple-element.147) | copy-start | bytes 6291460
  234.1 6.7 copy-start.24
  234.1 6.7 copy-start.25
  240.8 4.4 copy-start.44
  265.3 80.7 %copy-start.49 = (f32[1024]{0:T(1024)}, f32[1024]{0:T(1024)S(1)}, u32[]{:S(2)}) copy-start(f32[1024]{0:T(1024)S(1)} %add.219) | copy-start | bytes 12292
  300.9 3.3 copy-start.36
  301.0 3.3 copy-start.38
  301.0 3.3 copy-start.39
  301.0 3.4 copy-start.17
  304.3 2.9 copy-start.27
  304.3 3.4 slice-start
  304.4 4.3 slice-start.1
  304.4 41.6 %slice-start.2 = ((s8[8388608]{0:T(1024)(128)(4,1)}), s8[4194304]{0:T(1024)(128)(4,1)S(1)}, s32[]{:S(2)}) async-start(s8[8388608]{0:T(1024)(128)(4,1)} %bitcast.228), calls=%async_computation.2 | async-start | bytes 8388608
  307.2 38.8 %copy-start.18 = (f32[768,1024]{1,0:T(8,128)}, f32[768,1024]{1,0:T(8,128)S(1)}, u32[]{:S(2)}) copy-start(f32[768,1024]{1,0:T(8,128)S(1)} %get-tuple-element.361) | copy-start | bytes 9437188
  308.6 37.4 %slice-start.3 = ((s8[8388608]{0:T(1024)(128)(4,1)}), s8[4194304]{0:T(1024)(128)(4,1)S(1)}, s32[]{:S(2)}) async-start(s8[8388608]{0:T(1024)(128)(4,1)} %bitcast.228), calls=%async_computation.3 | async-start | bytes 8388608
  308.6 37.4 %copy-start.51 = (f32[1024]{0:T(1024)S(1)}, f32[1024]{0:T(1024)}, u32[]{:S(2)}) copy-start(f32[1024]{0:T(1024)} %add.225) | copy-start | bytes 12292
  346.0 7.8 copy-start.55
  353.7 1.4 copy-start.47
  382.7 12.5 %copy-start.19 = (f32[768,1024]{1,0:T(8,128)S(1)}, f32[768,1024]{1,0:T(8,128)}, u32[]{:S(2)}) copy-start(f32[768,1024]{1,0:T(8,128)} %copy-done.18) | copy-start | bytes 9437188
  396.1 1.7 copy-start.21
  396.1 3.1 copy-start.10
  396.2 5.0 copy-start.42
  404.4 6.6 copy-start.11
  404.4 6.6 copy-start.37
  412.6 3.2 copy-start.23
  422.9 3.3 copy-start.12
  433.8 3.2 copy-start.23
  444.1 3.4 copy-start.12
  455.0 3.2 copy-start.23
  465.3 3.3 copy-start.12
  477.8 3.4 copy-start.16
  479.7 70.8 %collective-permute-start.1 = (bf16[2,3,256,1024]{2,3,1,0:T(8,128)(2,1)}, bf16[2,3,256,1024]{2,3,1,0:T(8,128)(2,1)}, u32[]{:S(2)}, u32[]{:S(2)}) collective-permute-start(bf16[2,3,256,1024]{2,3,1,0:T(8,128)(2,1)} %pad_maximum_fusion.3), channel_id=1, source_target_pairs={{0,1},{1,0},{2,3},{3,2},{4,5},{5,4},{6,7},{7,6},{8,9},{9,8},{10,11... | collective-permute-start | bytes 9437192 | tf_op jit(solution)/shard_map/ppermute | solution.py:27
  481.2 3.8 copy-start.48
  481.2 3.8 copy-start.53
  481.2 3.9 copy-start.52
  481.2 3.9 copy-start.14
  481.5 4.0 copy-start.45
  481.5 4.0 copy-start.54
  553.0 4.9 copy-start.41
  553.1 4.9 copy-start.46
  561.3 13.1 %copy-start.20 = (f32[768,1024]{1,0:T(8,128)S(1)}, f32[768,1024]{1,0:T(8,128)}, u32[]{:S(2)}) copy-start(f32[768,1024]{1,0:T(8,128)} %copy-done.18) | copy-start | bytes 9437188
  561.3 13.1 %copy-start.50 = (f32[1024]{0:T(1024)S(1)}, f32[1024]{0:T(1024)}, u32[]{:S(2)}) copy-start(f32[1024]{0:T(1024)} %copy-done.49) | copy-start | bytes 12292
  561.3 13.0 %collective-permute-start.2 = (f32[12293]{0:T(1024)S(1)}, f32[12293]{0:T(1024)S(1)}, u32[]{:S(2)}, u32[]{:S(2)}) collective-permute-start(f32[12293]{0:T(1024)S(1)} %concatenate.45), channel_id=1, source_target_pairs={{0,1},{1,0},{2,3},{3,2},{4,5},{5,4},{6,7},{7,6},{8,9},{9,8},{10,11... | collective-permute-start | bytes 147524 | tf_op jit(solution)/shard_map/ppermute | solution.py:27
  574.3 14.0 %copy-start.28 = (bf16[128,8,3,256]{3,1,2,0:T(8,128)(2,1)S(1)}, bf16[128,8,3,256]{3,1,2,0:T(8,128)(2,1)}, u32[]{:S(2)}) copy-start(bf16[128,8,3,256]{3,1,2,0:T(8,128)(2,1)} %copy-done.27) | copy-start | bytes 4718596
  574.3 14.0 %copy-start.33 = (bf16[768,1024]{1,0:T(8,128)(2,1)S(1)}, bf16[768,1024]{1,0:T(8,128)(2,1)}, u32[]{:S(2)}) copy-start(bf16[768,1024]{1,0:T(8,128)(2,1)} %copy-done.32) | copy-start | bytes 4718596
  574.4 12.3 %collective-permute-start.3 = (f32[12293]{0:T(1024)S(1)}, f32[12293]{0:T(1024)S(1)}, u32[]{:S(2)}, u32[]{:S(2)}) collective-permute-start(f32[12293]{0:T(1024)S(1)} %add.237), channel_id=1, source_target_pairs={{0,2},{1,3},{2,0},{3,1},{4,6},{5,7},{6,4},{7,5},{8,10},{9,11},{10,... | collective-permute-start | bytes 147524 | tf_op jit(solution)/shard_map/ppermute | solution.py:27
  586.7 119.8 %collective-permute-start.4 = (f32[12293]{0:T(1024)S(1)}, f32[12293]{0:T(1024)S(1)}, u32[]{:S(2)}, u32[]{:S(2)}) collective-permute-start(f32[12293]{0:T(1024)S(1)} %add.238), channel_id=1, source_target_pairs={{0,4},{1,5},{2,6},{3,7},{4,0},{5,1},{6,2},{7,3},{8,12},{9,13},{10,... | collective-permute-start | bytes 147524 | tf_op jit(solution)/shard_map/ppermute | solution.py:27
  695.8 1.6 copy-start.26
  703.7 19.7 %slice-start.4 = ((s8[6291456]{0:T(1024)(128)(4,1)}), s8[2097152]{0:T(1024)(128)(4,1)S(1)}, s32[]{:S(2)}) async-start(s8[6291456]{0:T(1024)(128)(4,1)} %bitcast.233), calls=%async_computation.4 | async-start | bytes 4194304
  706.5 16.1 %collective-permute-start.5 = (f32[12293]{0:T(1024)S(1)}, f32[12293]{0:T(1024)S(1)}, u32[]{:S(2)}, u32[]{:S(2)}) collective-permute-start(f32[12293]{0:T(1024)S(1)} %add.239), channel_id=1, source_target_pairs={{0,8},{1,9},{2,10},{3,11},{4,12},{5,13},{6,14},{7,15},{8,0},{9,1},... | collective-permute-start | bytes 147524 | tf_op jit(solution)/shard_map/ppermute | solution.py:27
  711.8 11.7 %slice-start.5 = ((s8[6291456]{0:T(1024)(128)(4,1)}), s8[4194304]{0:T(1024)(128)(4,1)S(1)}, s32[]{:S(2)}) async-start(s8[6291456]{0:T(1024)(128)(4,1)} %bitcast.233), calls=%async_computation.5 | async-start | bytes 8388608
  711.8 11.7 %copy-start.22 = (f32[768,1024]{1,0:T(8,128)S(1)}, f32[768,1024]{1,0:T(8,128)}, u32[]{:S(2)}) copy-start(f32[768,1024]{1,0:T(8,128)} %copy-done.21) | copy-start | bytes 9437188
  711.8 11.7 %copy-start.29 = (bf16[128,8,3,256]{3,1,2,0:T(8,128)(2,1)S(1)}, bf16[128,8,3,256]{3,1,2,0:T(8,128)(2,1)}, u32[]{:S(2)}) copy-start(bf16[128,8,3,256]{3,1,2,0:T(8,128)(2,1)} %copy.76) | copy-start | bytes 4718596
  711.8 11.7 %copy-start.30 = (bf16[768,1024]{0,1:T(8,128)(2,1)S(1)}, bf16[768,1024]{0,1:T(8,128)(2,1)}, u32[]{:S(2)}) copy-start(bf16[768,1024]{0,1:T(8,128)(2,1)} %copy.68) | copy-start | bytes 4718596
  711.8 11.7 %copy-start.31 = (bf16[768,1024]{0,1:T(8,128)(2,1)S(1)}, bf16[768,1024]{0,1:T(8,128)(2,1)}, u32[]{:S(2)}) copy-start(bf16[768,1024]{0,1:T(8,128)(2,1)} %copy.69) | copy-start | bytes 4718596
  711.8 11.7 %copy-start.43 = (f32[768]{0:T(1024)S(1)}, f32[768]{0:T(1024)}, u32[]{:S(2)}) copy-start(f32[768]{0:T(1024)} %copy-done.42) | copy-start | bytes 9220
  722.6 69.6 %collective-permute-start.6 = (f32[12293]{0:T(1024)S(1)}, f32[12293]{0:T(1024)S(1)}, u32[]{:S(2)}, u32[]{:S(2)}) collective-permute-start(f32[12293]{0:T(1024)S(1)} %add.240), channel_id=1, source_target_pairs={{0,16},{1,17},{2,18},{3,19},{4,20},{5,21},{6,22},{7,23},{8,24},{9,... | collective-permute-start | bytes 147524 | tf_op jit(solution)/shard_map/ppermute | solution.py:27
  730.1 69.0 %copy-start.35 = (f32[32,4096]{1,0:T(8,128)S(1)}, f32[32,4096]{1,0:T(8,128)}, u32[]{:S(2)}) copy-start(f32[32,4096]{1,0:T(8,128)} %get-tuple-element.624) | copy-start | bytes 1572868
  730.1 69.8 %copy-start.34 = (f32[128,1024]{1,0:T(8,128)S(1)}, f32[128,1024]{1,0:T(8,128)}, u32[]{:S(2)}) copy-start(f32[128,1024]{1,0:T(8,128)} %get-tuple-element.625) | copy-start | bytes 1572868
  (11 other events, 12.5 us)

commit v3 on v2

--- a/solution.py
+++ b/solution.py
@@ -154,69 +154,6 @@
         copy.wait_recv()
 
 
-def gather_kernel(shapes, nz):
-    count = len(shapes)
-
-    def kernel(*refs):
-        shards, given = refs[:count], refs[count]
-        fulls, taken = refs[count + 1 : 2 * count + 1], refs[2 * count + 1]
-        send_sem, recv_sem, own_sem = refs[2 * count + 2 :]
-        place = Place()
-        sender = Sender(send_sem, recv_sem)
-        kept = [
-            pltpu.make_async_copy(shard, full.at[place.z, place.column()], own_sem.at[i])
-            for i, (shard, full) in enumerate(zip(shards, fulls))
-        ]
-        for copy in kept:
-            copy.start()
-        meet(place)
-        for copy in kept:
-            copy.wait()
-        steps = [gather_steps(place, sender, s, f) for s, f in zip(shards, fulls)]
-        swapped = None
-        t = 0
-        while steps:
-            live = []
-            for i, step in enumerate(steps):
-                if i > t:
-                    live.append(step)
-                    continue
-                try:
-                    next(step)
-                    live.append(step)
-                except StopIteration:
-                    pass
-            steps = live
-            if t == 1:
-                swapped = sender.send(given, taken, place.device(x=1))
-            t += 1
-        swapped.wait_recv()
-        sender.close()
-
-    return kernel
-
-
-def gather_all(shards, block_input, collective_id):
-    nz = lax.axis_size("dp") // 4
-    copies = len(shards) * gather_copies(nz) + 1
-    results = pl.pallas_call(
-        gather_kernel([s.shape for s in shards], nz),
-        out_shape=[jax.ShapeDtypeStruct((nz, 8) + s.shape, s.dtype) for s in shards]
-        + [jax.ShapeDtypeStruct(block_input.shape, block_input.dtype)],
-        in_specs=[pl.BlockSpec(memory_space=pltpu.VMEM)] * (len(shards) + 1),
-        out_specs=[pl.BlockSpec(memory_space=pl.ANY)] * (len(shards) + 1),
-        scratch_shapes=[
-            pltpu.SemaphoreType.DMA((copies,)),
-            pltpu.SemaphoreType.DMA((copies,)),
-            pltpu.SemaphoreType.DMA((len(shards),)),
-        ],
-        compiler_params=pltpu.CompilerParams(
-            collective_id=collective_id, has_side_effects=True, vmem_limit_bytes=16 << 20
-        ),
-    )(*shards, block_input)
-    return results
-
-
 def reduce_copies(nz):
     return 4 + 2 + 2 + 2 + nz - 1
 
@@ -425,6 +362,401 @@
     return lax.dot_general(
         grad, weight, (((1,), (1,)), ((), ())), preferred_element_type=jnp.float32
     )
+
+
+NN = (((1,), (0,)), ((), ()))
+NT = (((1,), (1,)), ((), ()))
+LOW = jnp.bfloat16
+F32 = jnp.float32
+
+
+def mm(left, right, dims=NN):
+    return lax.dot_general(left, right, dims, preferred_element_type=F32)
+
+
+def loop(count, step):
+    lax.fori_loop(0, count, lambda i, _: (step(i), 0)[1], 0)
+
+
+def tile(index, size):
+    return pl.ds(pl.multiple_of(index * size, size), size)
+
+
+def run_out(steps):
+    for _ in steps:
+        pass
+
+
+def expand(packed, offset, share, start, length):
+    n, wide = packed.shape
+    place = lax.broadcasted_iota(jnp.int32, (wide, length), 1) + start
+    lane = lax.broadcasted_iota(jnp.int32, (wide, length), 0)
+    pick = (lane == offset + lax.rem(place, share)).astype(F32).astype(LOW)
+    spread = mm(packed, pick)
+    row = lax.broadcasted_iota(jnp.int32, (n, length), 0)
+    column = lax.broadcasted_iota(jnp.int32, (n, length), 1) + start
+    return jnp.sum(jnp.where(row == lax.div(column, share), spread, 0.0), axis=0, keepdims=True)
+
+
+def normalize(resid):
+    centre = resid - jnp.mean(resid, axis=-1, keepdims=True)
+    spread = jnp.mean(centre * centre, axis=-1, keepdims=True)
+    rstd = lax.rsqrt(spread + eps_norm)
+    return centre * rstd, rstd
+
+
+def column_sum(value):
+    return jnp.sum(value, axis=0, keepdims=True)
+
+
+def forward_kernel(by_hand, items, half_len, names_in, names_out, names_scratch, *refs):
+    names = names_in + names_out + names_scratch
+    r = dict(zip(names, refs))
+    width = r["input"].shape[1]
+    rows = items * half_len
+    blocks = r["act"].shape[0]
+    place = Place()
+    sender = Sender(r["send"], r["recv"])
+    local = r["local"]
+    local_count = [0]
+
+    def copy(src, dst):
+        made = pltpu.make_async_copy(src, dst, local.at[local_count[0]])
+        local_count[0] += 1
+        made.start()
+        return made
+
+    saved = []
+    cot_in = copy(r["cotangent"], r["cot"])
+    params = ["w_qkv", "small", "w_o", "w_in", "w_out"]
+    if by_hand:
+        full = {p: r["all_" + p] for p in params}
+        kept = [copy(r[p], full[p].at[place.z, place.column()]) for p in params]
+    else:
+        full = {p: r[p] for p in params}
+        kept = []
+    meet(place)
+    for made in kept:
+        made.wait()
+    if by_hand:
+        gens = {p: gather_steps(place, sender, r[p], full[p]) for p in params}
+
+    def pump(*which):
+        if by_hand:
+            for p in which:
+                next(gens[p], None)
+
+    across = place.device(x=1)
+    pump("w_qkv", "small")
+    codes_over = sender.send(r["codes"], r["codes_taken"], across)
+    half_item = [pl.ds(i * half_len, half_len) for i in range(items)]
+    input_over = []
+    for at in half_item[:2]:
+        input_over.append(sender.send(r["input"].at[at], r["taken"].at[at], across))
+    stream, sums = r["stream"], r["sums"]
+    sums[...] = jnp.zeros_like(sums)
+    valid = [r["cols"][:, items + i : items + i + 1] for i in range(items)]
+    for i in range(items):
+        embed = r["embed"][i : i + 1, :]
+
+        def make_stream(j, i=i, embed=embed):
+            at = pl.ds(pl.multiple_of(i * half_len + j * 32, 32), 32)
+            value = r["input"][at, :].astype(F32) + embed
+            stream[at, :] = value.astype(LOW)
+            weight = r["cols"][tile(j, 32), items + i : items + i + 1]
+            sums[0:1, :] += column_sum(value * value * weight)
+
+        loop(half_len // 32, make_stream)
+    pump("w_qkv", "small", "w_o", "w_in")
+    pump("w_qkv", "small")
+    pump("w_qkv", "small")
+    for at in half_item[2:]:
+        input_over.append(sender.send(r["input"].at[at], r["taken"].at[at], across))
+    pump("w_qkv", "small", "w_o")
+    pump("w_qkv", "small")
+    load_qkv = [
+        copy(full["w_qkv"].at[:, :, :, pl.ds(t * width, width)], r["v_qkv"].at[t]) for t in range(3)
+    ]
+    load_small = copy(full["small"], r["v_small"])
+    load_small.wait()
+    shards = r["v_small"].shape[0] * r["v_small"].shape[1]
+    for d in range(shards):
+        r["packed"][d : d + 1, :] = r["v_small"][d // 8, d % 8, 0:1, :]
+    packed = r["packed"][...].astype(LOW)
+    share = width // shards
+    b_share = share * blocks
+    vectors, b_in = r["vectors"], r["v_b_in"]
+    for t in range(8):
+        vectors[t : t + 1, :] = expand(packed, b_share + t * share, share, 0, width)
+    for t in range(blocks):
+        b_in[t : t + 1, :] = expand(packed, 0, b_share, t * width, width)
+    bias_q, bias_v, bias_o, bias_out = (vectors[t : t + 1, :] for t in range(4))
+    gain_one, gain_two, shift_one, shift_two = (vectors[t : t + 1, :] for t in range(4, 8))
+    heads = r["heads"]
+    step = 256
+
+    def weight(name, t, at):
+        value = r[name][t, :, :, :, at]
+        return value.reshape(-1, value.shape[-1])
+
+    for made in load_qkv:
+        made.wait()
+
+    def project_own(j):
+        at = tile(j, step)
+        mine = stream[0:rows, :]
+        heads[0, :, at] = (mm(mine, weight("v_qkv", 0, at)) + vectors[0:1, at]).astype(LOW)
+        heads[1, :, at] = mm(mine, weight("v_qkv", 1, at)).astype(LOW)
+        heads[3, :, at] = (mm(mine, weight("v_qkv", 2, at)) + vectors[1:2, at]).astype(LOW)
+
+    def project_other(j):
+        at = tile(j, step)
+        theirs = stream[rows : 2 * rows, :]
+        heads[2, :, at] = mm(theirs, weight("v_qkv", 1, at)).astype(LOW)
+        heads[4, :, at] = (mm(theirs, weight("v_qkv", 2, at)) + vectors[1:2, at]).astype(LOW)
+
+    pump("w_in")
+    loop(width // step, project_own)
+    pump("w_o", "w_out")
+    codes_over.wait_recv()
+    same = lax.broadcasted_iota(jnp.int32, (half_len, half_len), 0) == lax.broadcasted_iota(
+        jnp.int32, (half_len, half_len), 1
+    )
+    for i in range(items):
+        asked = r["cols"][:, i : i + 1]
+        own = (r["codes"][i : i + 1, :] <= asked) | same
+        other = r["codes_taken"][i : i + 1, :] <= asked
+        r["permit"][i, :, 0:half_len] = jnp.where(own, 0.0, fill_value)
+        r["permit"][i, :, half_len : 2 * half_len] = jnp.where(other, 0.0, fill_value)
+    for made in input_over:
+        made.wait_recv()
+    for i in range(items):
+        embed = r["embed"][i : i + 1, :]
+
+        def make_other(j, i=i, embed=embed):
+            at = pl.ds(pl.multiple_of(i * half_len + j * 32, 32), 32)
+            to = pl.ds(pl.multiple_of(rows + i * half_len + j * 32, 32), 32)
+            stream[to, :] = (r["taken"][at, :].astype(F32) + embed).astype(LOW)
+
+        loop(half_len // 32, make_other)
+    loop(width // step, project_other)
+    saved.append(copy(heads, r["save_heads"]))
+    saved.append(copy(r["permit"], r["save_permit"]))
+    pump("w_o", "w_o", "w_in")
+    lane = lax.broadcasted_iota(jnp.int32, (half_len, 2 * HD), 1)
+    key_lane = lax.broadcasted_iota(jnp.int32, (2 * half_len, 2 * HD), 1)
+
+    def attend(i):
+        at_rows = pl.ds(i * half_len, half_len)
+
+        def pair(p):
+            at = tile(p, 2 * HD)
+            query = heads[0, at_rows, at] * (1.0 / math.sqrt(HD))
+            keys = jnp.concatenate([heads[1, at_rows, at], heads[2, at_rows, at]], axis=0)
+            values = jnp.concatenate([heads[3, at_rows, at], heads[4, at_rows, at]], axis=0)
+            nothing = jnp.zeros((), LOW)
+            mixed = None
+            logs = r["logs"][i]
+            for h in range(2):
+                scores = mm(jnp.where((lane < HD) == (h == 0), query, nothing), keys, NT) + r["permit"][i]
+                peak = jnp.max(scores, axis=1, keepdims=True)
+                expo = jnp.exp(scores - peak)
+                total = jnp.sum(expo, axis=1, keepdims=True)
+                probs = (expo * (1.0 / total)).astype(LOW)
+                part = mm(probs, jnp.where((key_lane < HD) == (h == 0), values, nothing))
+                mixed = part if mixed is None else mixed + part
+                logs = jnp.where(lane == 2 * p + h, peak + jnp.log(total), logs)
+            r["logs"][i] = logs
+            stream[at_rows, at] = mixed.astype(LOW)
+
+        loop(width // (2 * HD), pair)
+
+    attend(0)
+    pump("w_in", "w_in")
+    if items > 1:
+        attend(1)
+    pump("w_in", "w_out")
+    for i in range(2, items):
+        attend(i)
+    mixed = stream
+    saved.append(copy(stream.at[pl.ds(0, rows)], r["save_mixed"]))
+    saved.append(copy(r["logs"], r["save_logs"]))
+    if by_hand:
+        run_out(gens["w_o"])
+    load_o = copy(full["w_o"], r["v_o"])
+    load_o.wait()
+    xhat = r["xhat"]
+    for i in range(items):
+        at_rows = pl.ds(i * half_len, half_len)
+        w_o = r["v_o"][...].reshape(width, width)
+        r["work"][...] = mm(mixed[at_rows, :], w_o) + bias_o
+        embed = r["embed"][i : i + 1, :]
+
+        def first_norm(j, i=i, embed=embed):
+            at = pl.ds(pl.multiple_of(i * half_len + j * 32, 32), 32)
+            to = pl.ds(pl.multiple_of(rows + i * half_len + j * 32, 32), 32)
+            weight_rows = r["cols"][tile(j, 32), items + i : items + i + 1]
+            attn = r["work"][tile(j, 32), :]
+            sums[1:2, :] += column_sum(attn * attn * weight_rows)
+            value, rstd = normalize(r["input"][at, :].astype(F32) + embed + attn)
+            xhat[at, :] = value
+            r["rstd"][at, :] = jnp.broadcast_to(rstd, (32, 128))
+            stream[to, :] = (value * gain_one + shift_one).astype(LOW)
+
+        loop(half_len // 32, first_norm)
+    saved.append(copy(xhat, r["save_xhat"]))
+    saved.append(copy(r["rstd"], r["save_rstd"]))
+    if by_hand:
+        run_out(gens["w_in"])
+    load_in = [copy(full["w_in"].at[:, :, :, pl.ds(t * width, width)], r["v_in"].at[t]) for t in range(blocks)]
+    for made in saved[:1]:
+        made.wait()
+    act, slope = heads, r["slope"]
+    for t in range(blocks):
+        load_in[t].wait()
+
+        def feed(j, t=t):
+            at = tile(j, step)
+            w_in = weight("v_in", t, at)
+            for i in range(items):
+                own = pl.ds(i * half_len, half_len)
+                pre = mm(stream[pl.ds(rows + i * half_len, half_len), :], w_in) + b_in[t : t + 1, at]
+                cdf = 0.5 + 0.5 * lax.erf(pre * (1.0 / math.sqrt(2.0)))
+                act[t, own, at] = (pre * cdf).astype(LOW)
+                pdf = jnp.exp(pre * pre * -0.5) * (1.0 / math.sqrt(2.0 * math.pi))
+                slope[t, own, at] = (cdf + pre * pdf).astype(LOW)
+
+        loop(width // step, feed)
+        if t == 1:
+            pump("w_out")
+        if t == 2:
+            pump("w_out")
+    saved.append(copy(heads.at[pl.ds(0, blocks)], r["act"]))
+    saved.append(copy(slope, r["save_slope"]))
+    if by_hand:
+        run_out(gens["w_out"])
+    load_out = [copy(full["w_out"].at[t], r["v_out"].at[t]) for t in range(blocks)]
+    for made in load_out:
+        made.wait()
+    cot_in.wait()
+    saved[2].wait()
+    for i in range(items):
+        at_rows = pl.ds(i * half_len, half_len)
+        total = None
+        for t in range(blocks):
+            part = mm(act[t, at_rows, :], r["v_out"][t].reshape(width, width))
+            total = part if total is None else total + part
+        r["work"][...] = total + bias_out
+
+        def second_norm(j, i=i):
+            at = pl.ds(pl.multiple_of(i * half_len + j * 32, 32), 32)
+            to = pl.ds(pl.multiple_of(rows + i * half_len + j * 32, 32), 32)
+            weight_rows = r["cols"][tile(j, 32), items + i : items + i + 1]
+            branch = r["work"][tile(j, 32), :]
+            sums[2:3, :] += column_sum(branch * branch * weight_rows)
+            value, rstd = normalize(xhat[at, :] * gain_one + shift_one + branch)
+            result = value * gain_two + shift_two
+            sums[3:4, :] += column_sum(result * result * weight_rows)
+            stream[at, :] = result.astype(LOW)
+            grad = r["cot"][at, :].astype(F32)
+            sums[5:6, :] += column_sum(grad * value)
+            sums[6:7, :] += column_sum(grad)
+            scaled = grad * gain_two
+            back = rstd * (
+                scaled
+                - jnp.mean(scaled, axis=-1, keepdims=True)
+                - value * jnp.mean(scaled * value, axis=-1, keepdims=True)
+            )
+            r["back"][at, :] = back
+            back_low = back.astype(LOW)
+            stream[to, :] = back_low
+            sums[4:5, :] += column_sum(back_low.astype(F32))
+
+        loop(half_len // 32, second_norm)
+    saved.append(copy(stream.at[pl.ds(0, rows)], r["output"]))
+    saved.append(copy(stream.at[pl.ds(rows, rows)], r["save_back_low"]))
+    saved.append(copy(r["back"], r["save_back"]))
+    saved.append(copy(vectors, r["save_vectors"]))
+    for i, made in enumerate(saved):
+        if i not in (0, 2):
+            made.wait()
+    sender.close()
+
+
+def forward(by_hand, items, half_len, weights, small, block_input, embed, codes, cols, cotangent, collective_id):
+    rows, width = block_input.shape
+    full_len = 2 * half_len
+    blocks = 4
+    nz = lax.axis_size("dp") // 4
+    shape = jax.ShapeDtypeStruct
+    vmem, hbm = pl.BlockSpec(memory_space=pltpu.VMEM), pl.BlockSpec(memory_space=pl.ANY)
+    params = ["w_qkv", "small", "w_o", "w_in", "w_out"]
+    ins = dict(zip(params, [weights[0], small] + weights[1:]))
+    spaces_in = [vmem if by_hand else hbm] * 5
+    ins.update(input=block_input, embed=embed, codes=codes, cols=cols, cotangent=cotangent)
+    spaces_in += [vmem] * 4 + [hbm]
+    outs, spaces_out = {}, []
+    if by_hand:
+        for p in params:
+            outs["all_" + p] = shape((nz, 8) + ins[p].shape, ins[p].dtype)
+            spaces_out.append(hbm)
+    outs.update(
+        save_heads=shape((5, rows, width), LOW),
+        save_permit=shape((items, half_len, full_len), F32),
+        save_mixed=shape((rows, width), LOW),
+        save_logs=shape((items, half_len, 128), F32),
+        save_xhat=shape((rows, width), F32),
+        save_rstd=shape((rows, 128), F32),
+        act=shape((blocks, rows, width), LOW),
+        save_slope=shape((blocks, rows, width), LOW),
+        output=shape((rows, width), LOW),
+        save_back_low=shape((rows, width), LOW),
+        save_back=shape((rows, width), F32),
+        save_vectors=shape((8, width), F32),
+        sums=shape((8, width), F32),
+    )
+    spaces_out += [hbm] * 12 + [vmem]
+    if by_hand:
+        small_full = (nz, 8) + small.shape
+    else:
+        small_full = small.shape
+    copies = 5 * gather_copies(nz) + items + 1
+    scratch = dict(
+        send=pltpu.SemaphoreType.DMA((copies,)),
+        recv=pltpu.SemaphoreType.DMA((copies,)),
+        local=pltpu.SemaphoreType.DMA((40,)),
+        taken=pltpu.VMEM((rows, width), LOW),
+        codes_taken=pltpu.VMEM(codes.shape, F32),
+        stream=pltpu.VMEM((2 * rows, width), LOW),
+        v_qkv=pltpu.VMEM((3, 4, 8, 32, width), LOW),
+        v_small=pltpu.VMEM(small_full, F32),
+        packed=pltpu.VMEM((small_full[0] * 8, small_full[-1]), F32),
+        vectors=pltpu.VMEM((8, width), F32),
+        v_b_in=pltpu.VMEM((8, width), F32),
+        heads=pltpu.VMEM((5, rows, width), LOW),
+        permit=pltpu.VMEM((items, half_len, full_len), F32),
+        logs=pltpu.VMEM((items, half_len, 128), F32),
+        v_o=pltpu.VMEM((4, 8, 32, width), LOW),
+        work=pltpu.VMEM((half_len, width), F32),
+        xhat=pltpu.VMEM((rows, width), F32),
+        rstd=pltpu.VMEM((rows, 128), F32),
+        v_in=pltpu.VMEM((blocks, 4, 8, 32, width), LOW),
+        slope=pltpu.VMEM((blocks, rows, width), LOW),
+        v_out=pltpu.VMEM((blocks, 8, 128, width), LOW),
+        cot=pltpu.VMEM((rows, width), LOW),
+        back=pltpu.VMEM((rows, width), F32),
+    )
+    results = pl.pallas_call(
+        partial(forward_kernel, by_hand, items, half_len, list(ins), list(outs), list(scratch)),
+        out_shape=list(outs.values()),
+        in_specs=spaces_in,
+        out_specs=spaces_out,
+        scratch_shapes=list(scratch.values()),
+        compiler_params=pltpu.CompilerParams(
+            collective_id=collective_id, has_side_effects=True, vmem_limit_bytes=62 << 20
+        ),
+    )(*ins.values())
+    return dict(zip(outs, results))
 
 
 def scores_of(query, keys, code_row, query_block, key_pos, positions):
@@ -462,89 +794,77 @@
     code_local = jnp.where(valid, blocks.astype(f32), code_absent)
     share = width // n
     b_count = b_in.shape[0]
+    share = width // n
+    b_count = b_in.shape[0]
     small = jnp.concatenate([b_in, biases.reshape(-1), gains.reshape(-1), shifts.reshape(-1)])
-    small = jnp.pad(small.astype(f32), (0, 1024 - small.shape[0])).reshape(8, 128)
-    gathered = gather_all([w_qkv, small, w_o, w_in, w_out], block_input.reshape(rows, width), 1)
-    w_qkv_all, small_all, w_o_all, w_in_all, w_out_all = (g.reshape(-1, g.shape[-1]) for g in gathered[:5])
-    input_other = gathered[5].reshape(block_input.shape)
-    small_all = small_all.reshape(n, 1024)[:, : b_count + 8 * share]
+    small_wide = -(-small.shape[0] // 128) * 128
+    small = jnp.pad(small.astype(f32), (0, small_wide - small.shape[0]))
+    small = jnp.broadcast_to(small[None, :], (8, small_wide))
+    by_hand = w_qkv.shape[0] == 32
+    weights = [w_qkv, w_o, w_in, w_out]
+    if not by_hand:
+        weights = [lax.all_gather(w, AXES, axis=0, tiled=True) for w in weights]
+        weights = [w.reshape(4, 8, w.shape[0] // 32, w.shape[1]) for w in weights]
+        small = lax.all_gather(small, AXES, axis=0).reshape(n // 8, 8, 8, small_wide)
+    embed = time_embed(timesteps, width)
+    embed_rows = jnp.pad(embed, ((0, 8 - items), (0, 0)))
+    codes = jnp.pad(code_local, ((0, 8 - items), (0, 0)))
+    cols = jnp.concatenate([blocks.astype(f32), valid.astype(f32)], axis=0).T
+    cols = jnp.pad(cols, ((0, 0), (0, 128 - 2 * items)))
+    fw = forward(
+        by_hand,
+        items,
+        half_len,
+        weights,
+        small,
+        block_input.reshape(rows, width),
+        embed_rows,
+        codes,
+        cols,
+        cotangent.reshape(rows, width),
+        1,
+    )
+    if by_hand:
+        weights = [fw["all_" + p] for p in ("w_qkv", "w_o", "w_in", "w_out")]
+    w_qkv_all, w_o_all, w_in_all, w_out_all = (w.reshape(-1, w.shape[-1]) for w in weights)
+    gain_full = fw["save_vectors"][4:6]
+    shift_full = fw["save_vectors"][6:8]
     code_all = jnp.concatenate([code_local, swap(code_local, X)], axis=1)
-    b_in_full = small_all[:, :b_count].reshape(-1)
-    rest = small_all[:, b_count:].reshape(n, 8, share).transpose(1, 0, 2).reshape(8, width)
-    bias_full, gain_full, shift_full = rest[:4], rest[4:6], rest[6:8]
-
-    embed = time_embed(timesteps, width)[:, None, :]
-    stream = (block_input.astype(f32) + embed).reshape(rows, width)
+    stream = (block_input.astype(f32) + embed[:, None, :]).reshape(rows, width)
     stream_low = stream.astype(low)
-    other_low = (input_other.astype(f32) + embed).reshape(rows, width).astype(low)
-    joint = jnp.dot(stream_low, w_qkv_all, preferred_element_type=f32)
-    other = jnp.dot(other_low, w_qkv_all[:, width:], preferred_element_type=f32)
-    query_low = (joint[:, :width] + bias_full[0]).astype(low)
-    split = lambda array: array.reshape(items, half_len, width)
-    key_all = jnp.concatenate(
-        [split(joint[:, width : 2 * width].astype(low)), split(other[:, :width].astype(low))], axis=1
-    )
-    value_all = jnp.concatenate(
-        [
-            split((joint[:, 2 * width :] + bias_full[1]).astype(low)),
-            split((other[:, width:] + bias_full[1]).astype(low)),
-        ],
-        axis=1,
-    )
     full_len = 2 * half_len
+    saved_heads = fw["save_heads"].reshape(5, items, half_len, width)
+    query_four = saved_heads[0].reshape(items, half_len, HEADS, HD)
+    key_four = jnp.concatenate([saved_heads[1], saved_heads[2]], axis=1).reshape(items, full_len, HEADS, HD)
+    value_four = jnp.concatenate([saved_heads[3], saved_heads[4]], axis=1).reshape(items, full_len, HEADS, HD)
     query_block = blocks.astype(f32)
-    query_four = query_low.reshape(items, half_len, HEADS, HD)
-    key_four = key_all.reshape(items, full_len, HEADS, HD)
-    value_four = value_all.reshape(items, full_len, HEADS, HD)
-
-    def attend(inputs):
-        query, keys, values, code_row, block_row = inputs
-        scores = scores_of(query, keys, code_row, block_row, key_pos, positions)
-        peak = jnp.max(scores, axis=-1, keepdims=True)
-        expo = jnp.exp(scores - peak)
-        total = jnp.sum(expo, axis=-1, keepdims=True)
-        probs = expo / total
-        mixed = jnp.einsum(
-            "hqk,khd->qhd", probs.astype(jnp.bfloat16), values, preferred_element_type=jnp.float32
-        )
-        return (mixed, (peak + jnp.log(total))[..., 0])
-
-    mixed_all, log_totals = lax.map(
-        attend, (query_four, key_four, value_four, code_all, query_block)
-    )
-    mixed_low = mixed_all.reshape(rows, width).astype(jnp.bfloat16)
-    attn = jnp.dot(mixed_low, w_o_all, preferred_element_type=jnp.float32) + bias_full[2]
-    resid_one = stream + attn
-    hidden_one = layer_norm(resid_one, gain_full[0], shift_full[0])
-    hidden_low = hidden_one.astype(jnp.bfloat16)
-    pre = jnp.dot(hidden_low, w_in_all, preferred_element_type=jnp.float32) + b_in_full
-    act_low = jax.nn.gelu(pre, approximate=False).astype(jnp.bfloat16)
-    branch = jnp.dot(act_low, w_out_all, preferred_element_type=jnp.float32) + bias_full[3]
-    resid_two = hidden_one + branch
-    result = layer_norm(resid_two, gain_full[1], shift_full[1])
-    output = result.astype(jnp.bfloat16).reshape(items, half_len, width)
-    row_weight = valid.reshape(rows).astype(jnp.float32)
-    local_sums = jnp.stack(
-        [
-            jnp.sum(row_weight * jnp.sum(tensor * tensor, axis=-1))
-            for tensor in (stream, attn, branch, result)
-        ]
-        + [jnp.sum(row_weight)]
-    )
-    _, norm_two_back = jax.vjp(layer_norm, resid_two, gain_full[1], shift_full[1])
-    dres_two, gain_two_grad, shift_two_grad = norm_two_back(
-        cotangent.reshape(rows, width).astype(jnp.float32)
-    )
-    branch_grad = dres_two.astype(jnp.bfloat16)
+    log_totals = fw["save_logs"][:, :, :HEADS].transpose(0, 2, 1)
+    mixed_low = fw["save_mixed"]
+    act_low = fw["act"].transpose(1, 0, 2).reshape(rows, -1)
+    slope = fw["save_slope"].transpose(1, 0, 2).reshape(rows, -1)
+    xhat_one = fw["save_xhat"]
+    rstd_one = fw["save_rstd"][:, :1]
+    hidden_low = (xhat_one * gain_full[0] + shift_full[0]).astype(low)
+    output = fw["output"].reshape(items, half_len, width)
+    dres_two = fw["save_back"]
+    branch_grad = fw["save_back_low"]
+    fsums = fw["sums"]
+    local_sums = jnp.concatenate([jnp.sum(fsums[:4], axis=1), jnp.sum(valid.astype(f32))[None]])
+    gain_two_grad, shift_two_grad = fsums[5], fsums[6]
 
     grad_out_part = inner(act_low, branch_grad).astype(low)
     act_grad = back_project(branch_grad, w_out_all)
-    _, gelu_back = jax.vjp(partial(jax.nn.gelu, approximate=False), pre)
-    pre_grad = gelu_back(act_grad)[0].astype(jnp.bfloat16)
+    pre_grad = (act_grad * slope.astype(f32)).astype(low)
     grad_in_part = inner(hidden_low, pre_grad).astype(low)
     dhidden = dres_two + back_project(pre_grad, w_in_all)
-    _, norm_one_back = jax.vjp(layer_norm, resid_one, gain_full[0], shift_full[0])
-    dres_one, gain_one_grad, shift_one_grad = norm_one_back(dhidden)
+    scaled = dhidden * gain_full[0]
+    dres_one = rstd_one * (
+        scaled
+        - jnp.mean(scaled, axis=-1, keepdims=True)
+        - xhat_one * jnp.mean(scaled * xhat_one, axis=-1, keepdims=True)
+    )
+    gain_one_grad = jnp.sum(dhidden * xhat_one, axis=0)
+    shift_one_grad = jnp.sum(dhidden, axis=0)
     attn_grad = dres_one.astype(jnp.bfloat16)
     grad_o_part = inner(mixed_low, attn_grad).astype(low)
     mixed_grad = (
@@ -582,8 +902,14 @@
     value_grad_low = (value_part[:, :half_len] + back[1]).reshape(rows, width).astype(jnp.bfloat16)
     joint_grad = jnp.concatenate([query_grad_low, key_grad_low, value_grad_low], axis=1)
     grad_qkv_part = inner(stream_low, joint_grad).astype(low)
-    grad_out, grad_in = reduce_all([grad_out_part, grad_in_part], 2)
-    grad_qkv, grad_o = reduce_all([grad_qkv_part, grad_o_part], 3)
+    if by_hand:
+        grad_out, grad_in = reduce_all([grad_out_part, grad_in_part], 2)
+        grad_qkv, grad_o = reduce_all([grad_qkv_part, grad_o_part], 3)
+    else:
+        grad_out, grad_in, grad_qkv, grad_o = (
+            lax.psum_scatter(part.astype(f32), AXES, scatter_dimension=0, tiled=True)
+            for part in (grad_out_part, grad_in_part, grad_qkv_part, grad_o_part)
+        )
     input_grad = (
         (dres_one + back_project(joint_grad, w_qkv_all))
         .astype(jnp.bfloat16)
@@ -594,7 +920,7 @@
         jnp.sum(query_grad_low.astype(jnp.float32), axis=0),
         jnp.sum(value_grad_low.astype(jnp.float32), axis=0),
         jnp.sum(attn_grad.astype(jnp.float32), axis=0),
-        jnp.sum(branch_grad.astype(jnp.float32), axis=0),
+        fsums[4],
         gain_one_grad,
         gain_two_grad,
         shift_one_grad,

time: 811 us -> 730 us (0.900)
  matrix products: 209 us -> 125 us
  Pallas kernels: 316 us -> 357 us
  other arithmetic: 64.7 us -> 42.6 us
  waiting for transfers between devices: 64.5 us -> 47.8 us
    dot_general x8 -> x0, matrix products: 74.3 us -> none  [the longest x1 37.3 us: body(): jnp.dot(hidden_low, w_in_all, preferred_element_type=jnp.float32)]
    pallas_call x1, Pallas kernels: 151 us -> 194 us  [forward(): pl.pallas_call(partial(forward_kernel, by_hand, items, half_len, list(ins...]
    reduce_sum x12 -> x2, other arithmetic: 19.3 us -> 1.49 us  [the longest x1 1.37 us: body(): jnp.sum(valid.astype(f32))[None]]
    convert_element_type x3 -> x2, local copies, waits for them, and re-layouts: 8.09 us -> 25.5 us  [body(): pre_grad = (act_grad * slope.astype(f32)).astype(low)]
    unnamed x129 -> x83, local copies, waits for them, and re-layouts: 43 us -> 26 us
    ppermute x7, waiting for transfers between devices: 64.5 us -> 47.8 us  [swap(): lax.ppermute(array, AXES, [(i, i ^ bits) for i in range(n_devices())])]
    dot_general x6 -> x3, matrix products: 16.8 us -> 7.36 us  [scores_of(): jnp.einsum('qhd,khd->hqk', query, keys, preferred_element_type=jnp.float32)]
    transpose x0 -> x2, local copies, waits for them, and re-layouts: none -> 8.6 us  [the longest x1 8.57 us: body(): act_low = fw['act'].transpose(1, 0, 2).reshape(rows, -1)]
  transfers between devices with their start and end apart: 7 -> 7, of which waited for: 1 -> 1; matrix products, arithmetic and copies ran while one was open for 20% -> 30% of each run, Pallas kernels for 39% -> 50%
where the time goes in v3:
time: 730 us; the launch traced here: 719 us
  Pallas kernels  357 us (49%)
  local copies, waits for them, and re-layouts  129 us (18%)
  matrix products  125 us (17%)
  waiting for transfers between devices  47.8 us (7%)
  other arithmetic  42.6 us (6%)
  starting transfers between devices  14.6 us (2%)
    pallas_call x1, Pallas kernels, forward(): pl.pallas_call(partial(forward_kernel, by_hand, items, half_len, list(ins...  194 us
    pallas_call x2, Pallas kernels, reduce_all(): pl.pallas_call(reduce_kernel([b.shape for b in blocks]), out_shape=[jax.S...  163 us
    ppermute x7, waiting for transfers between devices, swap(): lax.ppermute(array, AXES, [(i, i ^ bits) for i in range(n_devices())])  47.8 us
    dot_general x4, matrix products, back_project(): lax.dot_general(grad, weight, (((1,), (1,)), ((), ())), preferred_element...  41.3 us
    dot_general x4, matrix products, inner(): lax.dot_general(left, right, (((0,), (0,)), ((), ())), preferred_element_...  37.1 us
    unnamed x83, local copies, waits for them, and re-layouts  26 us
    convert_element_type x2, local copies, waits for them, and re-layouts, body(): pre_grad = (act_grad * slope.astype(f32)).astype(low)  25.5 us
  transfers between devices with their start and end apart: 7, of which 1 were waited for; matrix products, arithmetic and copies ran while one was open for 30% of the time, Pallas kernels for 50%

profile of v3, /device:TPU:0, one launch (start us, length us, event | category | flops | bytes accessed | tf_op | source)
XLA Modules:
  0.0 719.0 jit_solution(3461940648357175512)
XLA Ops:
  2.7 2.9 collective-permute-start
  12.8 193.8 %shard_map.221 = (bf16[4,8,32,3072]{3,2,1,0:T(8,128)(2,1)}, f32[4,8,8,384]{3,2,1,0:T(8,128)}, bf16[4,8,32,1024]{3,2,1,0:T(8,128)(2,1)}, bf16[4,8,32,4096]{3,2,1,...) custom-call(bf16[32,3072]{1,0:T(8,128)(2,1)} %refs_0_.1, ...), custom_call_target="tpu_custom_call" | custom-call | tf_op jit(solution)/shard_map/pallas_call | solution.py:749
  206.6 8.8 %convert_bitcast_fusion = f32[768,4,1024]{2,0,1:T(8,128)} fusion(bf16[4,768,1024]{2,1,0:T(8,128)(2,1)} %get-tuple-element.105), kind=kLoop, calls=%fused_computation.43 | loop fusion | flops 3145728 | bytes 18874368 | tf_op jit(solution)/shard_map/convert_element_type | solution.py:857
  215.4 12.7 %copy.89 = f32[768,4,1024]{0,2,1:T(8,128)} copy(f32[768,4,1024]{2,0,1:T(8,128)} %convert_bitcast_fusion) | data formatting | bytes 25165824 | tf_op jit(solution)/shard_map/convert_element_type | solution.py:857
  228.1 12.8 %copy.90 = f32[768,4096]{1,0:T(8,128)} copy(f32[768,4096]{0,1:T(8,128)} %bitcast.145) | data formatting | bytes 25165824 | tf_op jit(solution)/shard_map/convert_element_type | solution.py:857
  242.4 14.6 %convert_reduce_fusion = (f32[4096]{0:T(1024)}, bf16[768,4096]{1,0:T(8,128)(2,1)}) fusion(f32[768,4096]{1,0:T(8,128)} %copy.90, bf16[768,1024]{1,0:T(8,128)(2,1)S(1)} %copy-done.36, bf16[4096,1024]{1,0:T(8,128)(2,1)} %bitcast.178), kind=kOutput, calls=%fused_computation.44 | convolution fusion | flops 6455029760 | bytes 28852224 | tf_op jit(solution)/shard_map/dot_general | solution.py:362
  257.0 14.5 %multiply_reduce_fusion.1 = (f32[1024]{0:T(1024)}, f32[768]{0:T(1024)S(1)}, f32[768]{0:T(1024)S(1)}, f32[1024]{0:T(1024)}, f32[768,1024]{1,0:T(8,128)}) fusion(f32[768,1024]{1,0:T(8,128)S(1)} %copy-done.10, f32[1024]{0:T(1024)S(1)} %bitcast.170, f32[768,1024]{1,0:T(8,128)} %get-tuple-element.102, bf16[768,4096]{1,0:T(8,128)(2,1)} %get-tuple-element.259, ...), kind=kOutput, calls=%fused_computation.61 | convolution fusion | flops 6448738304 | bytes 24135680 | tf_op jit(solution)/shard_map/dot_general | solution.py:362
  271.7 2.9 fusion.51
  274.7 1.6 copy.92
  276.3 4.2 concatenate.54
  280.4 2.7 copy.91
  283.1 5.3 concatenate.53
  288.5 2.6 copy.96
  291.0 5.3 concatenate.59
  296.3 2.6 copy.95
  298.9 5.7 concatenate.58
  304.6 6.1 pad_maximum_fusion.1
  312.1 1.7 copy-done.7
  313.7 3.1 convolution_convert_fusion.4
  316.8 4.5 pad_maximum_fusion.2
  321.3 3.1 copy.97
  324.4 5.2 reshape.247
  329.6 4.9 copy.98
  335.3 5.2 reshape.248
  340.6 5.0 copy.100
  345.5 4.7 copy.101
  350.9 57.3 %while.15 = (s32[]{:T(128)}, bf16[3,256,16,64]{1,3,2,0:T(8,128)(2,1)}, f32[3,512,16,64]{1,3,2,0:T(8,128)}, f32[3,512,16,64]{1,3,2,0:T(8,128)}, bf16[3,512,16,64]...) while((s32[]{:T(128)}, ...), condition=%wide.region_4.5_spmd.clone, body=%wide.region_2.4_spmd.clone.sunk | while | flops 1374810368 | bytes 92932336 | solution.py:892
  351.1 2.5 fusion.86
  354.5 4.7 multiply_reduce_fusion.5
  359.2 2.4 multiply_convert_fusion.3
  363.1 3.7 bitcast_dynamic-update-slice_fusion.4
  366.8 3.5 bitcast_dynamic-update-slice_fusion.5
  370.2 2.5 fusion.86
  373.6 4.7 multiply_reduce_fusion.5
  378.4 2.4 multiply_convert_fusion.3
  382.2 3.6 bitcast_dynamic-update-slice_fusion.4
  385.8 3.4 bitcast_dynamic-update-slice_fusion.5
  389.3 2.5 fusion.86
  392.6 4.7 multiply_reduce_fusion.5
  397.4 2.4 multiply_convert_fusion.3
  401.2 3.6 bitcast_dynamic-update-slice_fusion.4
  404.8 3.4 bitcast_dynamic-update-slice_fusion.5
  408.2 2.0 fusion.42
  410.3 2.0 fusion.41
  412.6 1.6 collective-permute-start.1
  414.2 8.6 %copy.107 = bf16[768,4,1024]{0,2,1:T(8,128)(2,1)} copy(bf16[768,4,1024]{2,0,1:T(8,128)(2,1)} %bitcast.151) | data formatting | bytes 12582912 | tf_op jit(solution)/shard_map/transpose | solution.py:843
  422.9 11.4 %convolution_convert_fusion.1 = bf16[4096,1024]{1,0:T(8,128)(2,1)} fusion(bf16[768,4096]{0,1:T(8,128)(2,1)} %bitcast.152, bf16[768,1024]{1,0:T(8,128)(2,1)} %get-tuple-element.103), kind=kOutput, calls=%fused_computation.47 | convolution fusion | flops 6446645248 | bytes 16252928 | tf_op jit(solution)/shard_map/dot_general | solution.py:356
  434.6 47.8 %collective-permute-done.1 = bf16[2,3,256,1024]{2,3,1,0:T(8,128)(2,1)} collective-permute-done((bf16[2,3,256,1024]{2,3,1,0:T(8,128)(2,1)S(1)}, bf16[2,3,256,1024]{2,3,1,0:T(8,128)(2,1)}, u32[]{:S(2)}, u32[]{:S(2)}) %collective-permute-start.1) | collective-permute-done | bytes 3145760 | tf_op jit(solution)/shard_map/ppermute | solution.py:27
  482.4 2.5 convert_element_type.126
  485.0 3.8 convert_reduce_fusion.2
  491.1 12.3 %convolution_convert_fusion = bf16[1024,4096]{1,0:T(8,128)(2,1)} fusion(bf16[768,4096]{1,0:T(8,128)(2,1)} %get-tuple-element.259, f32[768,1024]{1,0:T(8,128)} %get-tuple-element.108, f32[1024]{0:T(1024)S(1)} %bitcast.176, f32[1024]{0:T(1024)S(1)} %bitcast.172), kind=kOutput, calls=%fused_computation.46 | convolution fusion | flops 6449004544 | bytes 17833984 | tf_op jit(solution)/shard_map/dot_general | solution.py:356
  504.3 3.2 convolution_convert_fusion.3
  507.5 1.6 collective-permute-start.4
  509.1 1.6 add_convert_fusion.1
  510.7 100.9 %shard_map.223 = (f32[128,1024]{1,0:T(8,128)}, f32[32,4096]{1,0:T(8,128)}) custom-call(bf16[4,8,128,1024]{3,2,1,0:T(8,128)(2,1)} %bitcast.147, bf16[4,8,32,4096]{3,2,1,0:T(8,128)(2,1)} %bitcast.148), custom_call_target="tpu_custom_call" | custom-call | tf_op jit(solution)/shard_map/pallas_call | solution.py:316
  611.6 2.8 copy.102
  614.4 1.6 copy.112
  616.0 1.7 copy.104
  617.7 2.6 copy.106
  621.2 1.8 copy.105
  623.0 5.3 collective-permute-start.5
  628.3 10.3 %convolution_convert_fusion.2 = bf16[1024,3072]{1,0:T(8,128)(2,1)} fusion(bf16[768,1024]{1,0:T(8,128)(2,1)} %bitcast.166, bf16[768,1024]{0,1:T(8,128)(2,1)} %copy.106, bf16[768,1024]{0,1:T(8,128)(2,1)} %copy.105, bf16[768,1024]{0,1:T(8,128)(2,1)S(1)} %bitcast.162), kind=kOutput, calls=%fused_computation.48 | convolution fusion | flops 4849139712 | bytes 12582912 | tf_op jit(solution)/shard_map/dot_general | solution.py:356
  639.3 9.2 %add_convert_fusion.2 = bf16[768,1024]{1,0:T(8,128)(2,1)} fusion(f32[768,1024]{1,0:T(8,128)S(1)} %copy-done.9, bf16[1024,3072]{1,0:T(8,128)(2,1)} %bitcast.179, bf16[768,1024]{0,1:T(8,128)(2,1)S(1)} %copy-done.15, bf16[768,1024]{0,1:T(8,128)(2,1)S(1)} %copy-done.16, bf16[768,1024]{0,1:T(8,128)(2,1)S(1)} %bitcast.163), kind=kOutput, calls=%fused_computation.67 | convolution fusion | flops 4847566848 | bytes 15728640 | tf_op jit(solution)/shard_map/dot_general | solution.py:362
  648.5 62.2 %shard_map.222 = (f32[32,3072]{1,0:T(8,128)}, f32[32,1024]{1,0:T(8,128)}) custom-call(bf16[4,8,32,3072]{3,2,1,0:T(8,128)(2,1)} %bitcast.156, bf16[4,8,32,1024]{3,2,1,0:T(8,128)(2,1)} %bitcast.161), custom_call_target="tpu_custom_call" | custom-call | tf_op jit(solution)/shard_map/pallas_call | solution.py:316
  (174 shorter events, 33.5 us)
Async XLA Ops:
  2.7 347.5 %collective-permute-start = (f32[3,256]{1,0:T(4,128)S(1)}, f32[3,256]{1,0:T(4,128)}, u32[]{:S(2)}, u32[]{:S(2)}) collective-permute-start(f32[3,256]{1,0:T(4,128)S(1)} %broadcast_select_fusion), channel_id=1, source_target_pairs={{0,1},{1,0},{2,3},{3,2},{4,5},{5,4},{6,7},{7,6},{8,9},{9,8},{10,11... | collective-permute-start | bytes 9224 | tf_op jit(solution)/shard_map/ppermute | solution.py:27
  10.0 0.6 copy-start.22
  228.1 14.3 %copy-start.36 = (bf16[768,1024]{1,0:T(8,128)(2,1)S(1)}, bf16[768,1024]{1,0:T(8,128)(2,1)}, u32[]{:S(2)}) copy-start(bf16[768,1024]{1,0:T(8,128)(2,1)} %get-tuple-element.103) | copy-start | bytes 4718596
  242.4 14.6 %copy-start.10 = (f32[768,1024]{1,0:T(8,128)S(1)}, f32[768,1024]{1,0:T(8,128)}, u32[]{:S(2)}) copy-start(f32[768,1024]{1,0:T(8,128)} %get-tuple-element.108) | copy-start | bytes 9437188
  257.0 14.7 %slice-start = ((s8[7864320]{0:T(1024)(128)(4,1)}), s8[4194304]{0:T(1024)(128)(4,1)S(1)}, s32[]{:S(2)}) async-start(s8[7864320]{0:T(1024)(128)(4,1)} %bitcast.149), calls=%async_computation | async-start | bytes 8388608
  257.0 14.5 %copy-start.20 = (f32[768,128]{1,0:T(8,128)S(1)}, f32[768,128]{1,0:T(8,128)}, u32[]{:S(2)}) copy-start(f32[768,128]{1,0:T(8,128)} %get-tuple-element.101) | copy-start | bytes 1179652
  257.0 14.7 %slice-start.1 = ((s8[7864320]{0:T(1024)(128)(4,1)}), s8[3670016]{0:T(1024)(128)(4,1)S(1)}, s32[]{:S(2)}) async-start(s8[7864320]{0:T(1024)(128)(4,1)} %bitcast.149), calls=%async_computation.1 | async-start | bytes 7340032
  280.4 8.0 %copy-start.19 = (f32[3,256,128]{2,1,0:T(8,128)S(1)}, f32[3,256,128]{2,1,0:T(8,128)}, u32[]{:S(2)}) copy-start(f32[3,256,128]{2,1,0:T(8,128)} %get-tuple-element.110) | copy-start | bytes 1179652
  304.6 6.1 copy-start.11
  304.6 6.1 copy-start.12
  310.6 3.1 copy-start.34
  312.1 1.7 copy-start.7
  313.7 3.1 copy-start.1
  313.7 3.1 copy-start.2
  351.1 3.4 copy-start
  359.2 2.4 copy-start.4
  363.1 3.7 copy-start.5
  370.2 3.4 copy-start
  378.4 2.4 copy-start.4
  382.2 3.6 copy-start.5
  389.3 3.4 copy-start
  397.4 2.4 copy-start.4
  401.2 3.6 copy-start.5
  412.6 69.8 %collective-permute-start.1 = (bf16[2,3,256,1024]{2,3,1,0:T(8,128)(2,1)S(1)}, bf16[2,3,256,1024]{2,3,1,0:T(8,128)(2,1)}, u32[]{:S(2)}, u32[]{:S(2)}) collective-permute-start(bf16[2,3,256,1024]{2,3,1,0:T(8,128)(2,1)S(1)} %pad_maximum_fusion.3), channel_id=1, source_target_pairs={{0,1},{1,0},{2,3},{3,2},{4,5},{5,4},{6,7},{7,6},{8,9},{9,8},{10,11... | collective-permute-start | bytes 9437192 | tf_op jit(solution)/shard_map/ppermute | solution.py:27
  414.2 8.6 %copy-start.25 = (f32[8,1024]{1,0:T(8,128)S(1)}, f32[8,1024]{1,0:T(8,128)}, u32[]{:S(2)}) copy-start(f32[8,1024]{1,0:T(8,128)} %get-tuple-element.122) | copy-start | bytes 98308
  422.9 11.4 %copy-start.6 = (bf16[3,256,16,64]{1,3,2,0:T(8,128)(2,1)S(1)}, bf16[3,256,16,64]{1,3,2,0:T(8,128)(2,1)}, u32[]{:S(2)}) copy-start(bf16[3,256,16,64]{1,3,2,0:T(8,128)(2,1)} %get-tuple-element.112) | copy-start | bytes 4718596
  484.9 3.8 copy-start.26
  484.9 3.8 copy-start.27
  484.9 3.8 copy-start.28
  484.9 3.8 copy-start.29
  485.0 3.8 copy-start.30
  485.0 3.8 copy-start.32
  485.0 3.8 copy-start.33
  485.0 6.1 copy-start.31
  489.6 13.8 %collective-permute-start.2 = (f32[12293]{0:T(1024)S(1)}, f32[12293]{0:T(1024)S(1)}, u32[]{:S(2)}, u32[]{:S(2)}) collective-permute-start(f32[12293]{0:T(1024)S(1)} %concatenate.62), channel_id=1, source_target_pairs={{0,1},{1,0},{2,3},{3,2},{4,5},{5,4},{6,7},{7,6},{8,9},{9,8},{10,11... | collective-permute-start | bytes 147524 | tf_op jit(solution)/shard_map/ppermute | solution.py:27
  491.1 13.2 %copy-start.8 = (f32[768,1024]{1,0:T(8,128)S(1)}, f32[768,1024]{1,0:T(8,128)}, u32[]{:S(2)}) copy-start(f32[768,1024]{1,0:T(8,128)} %copy-done.7) | copy-start | bytes 9437188
  491.1 13.2 %copy-start.35 = (bf16[768,1024]{1,0:T(8,128)(2,1)S(1)}, bf16[768,1024]{1,0:T(8,128)(2,1)}, u32[]{:S(2)}) copy-start(bf16[768,1024]{1,0:T(8,128)(2,1)} %get-tuple-element.116) | copy-start | bytes 4718596
  503.4 4.1 collective-permute-start.3
  504.3 4.8 copy-start.3
  504.3 4.8 copy-start.23
  507.5 115.5 %collective-permute-start.4 = (f32[12293]{0:T(1024)S(1)}, f32[12293]{0:T(1024)S(1)}, u32[]{:S(2)}, u32[]{:S(2)}) collective-permute-start(f32[12293]{0:T(1024)S(1)} %add.96), channel_id=1, source_target_pairs={{0,4},{1,5},{2,6},{3,7},{4,0},{5,1},{6,2},{7,3},{8,12},{9,13},{10,... | collective-permute-start | bytes 147524 | tf_op jit(solution)/shard_map/ppermute | solution.py:27
  621.2 7.1 copy-start.13
  623.0 15.6 %collective-permute-start.5 = (f32[12293]{0:T(1024)S(1)}, f32[12293]{0:T(1024)S(1)}, u32[]{:S(2)}, u32[]{:S(2)}) collective-permute-start(f32[12293]{0:T(1024)S(1)} %add.97), channel_id=1, source_target_pairs={{0,8},{1,9},{2,10},{3,11},{4,12},{5,13},{6,14},{7,15},{8,0},{9,1},... | collective-permute-start | bytes 147524 | tf_op jit(solution)/shard_map/ppermute | solution.py:27
  628.3 11.0 %copy-start.9 = (f32[768,1024]{1,0:T(8,128)S(1)}, f32[768,1024]{1,0:T(8,128)}, u32[]{:S(2)}) copy-start(f32[768,1024]{1,0:T(8,128)} %copy-done.7) | copy-start | bytes 9437188
  628.3 11.0 %copy-start.15 = (bf16[768,1024]{0,1:T(8,128)(2,1)S(1)}, bf16[768,1024]{0,1:T(8,128)(2,1)}, u32[]{:S(2)}) copy-start(bf16[768,1024]{0,1:T(8,128)(2,1)} %copy.106) | copy-start | bytes 4718596
  628.3 11.0 %copy-start.16 = (bf16[768,1024]{0,1:T(8,128)(2,1)S(1)}, bf16[768,1024]{0,1:T(8,128)(2,1)}, u32[]{:S(2)}) copy-start(bf16[768,1024]{0,1:T(8,128)(2,1)} %copy.105) | copy-start | bytes 4718596
  638.6 72.2 %collective-permute-start.6 = (f32[12293]{0:T(1024)S(1)}, f32[12293]{0:T(1024)S(1)}, u32[]{:S(2)}, u32[]{:S(2)}) collective-permute-start(f32[12293]{0:T(1024)S(1)} %add.98), channel_id=1, source_target_pairs={{0,16},{1,17},{2,18},{3,19},{4,20},{5,21},{6,22},{7,23},{8,24},{9,... | collective-permute-start | bytes 147524 | tf_op jit(solution)/shard_map/ppermute | solution.py:27
  648.5 65.9 %copy-start.14 = (bf16[768,1024]{1,0:T(8,128)(2,1)S(1)}, bf16[768,1024]{1,0:T(8,128)(2,1)}, u32[]{:S(2)}) copy-start(bf16[768,1024]{1,0:T(8,128)(2,1)} %get-tuple-element.100) | copy-start | bytes 4718596
  710.8 4.8 copy-start.21
  710.8 5.6 copy-start.24
  710.8 6.2 copy-start.18
  710.8 7.0 copy-start.17

commit v4 on v3

--- a/solution.py
+++ b/solution.py
@@ -23,8 +23,17 @@
     return lax.axis_size("dp") * lax.axis_size("ctx")
 
 
-def swap(array, bits):
-    return lax.ppermute(array, AXES, [(i, i ^ bits) for i in range(n_devices())])
+fill_value = -1e30
+eps_norm = 1e-05
+code_absent = 30000.0
+
+
+def time_embed(steps, width):
+    half = width // 2
+    freqs = jnp.exp(jnp.arange(half, dtype=jnp.float32) * (-math.log(10000.0) / half))
+    angle = steps.astype(jnp.float32)[:, None] * freqs[None, :]
+    return jnp.concatenate([jnp.sin(angle), jnp.cos(angle)], axis=-1)
+
 
 MESH = pl.DeviceIdType.MESH
 
@@ -153,219 +162,9 @@
     for copy in to_core:
         copy.wait_recv()
 
-
-def reduce_copies(nz):
-    return 4 + 2 + 2 + 2 + nz - 1
-
-
-def reduce_buffers(nz, rows, cols):
-    low = jnp.bfloat16
-    half = nz // 2
-    return [
-        pltpu.VMEM((4, nz, rows, cols), low),
-        pltpu.VMEM((4, nz, rows, cols), low),
-        pltpu.VMEM((half, rows, cols), low),
-        pltpu.VMEM((nz - half, rows, cols), low),
-        pltpu.VMEM((2, nz, rows, cols), low),
-        pltpu.VMEM((nz - 1, rows, cols), low),
-    ]
-
-
-def add_rows(target, terms, count, rows):
-    step = min(rows, 16)
-    per = rows // step
-
-    def one(j, _):
-        i, start = j // per, (j % per) * step
-        at = pl.ds(pl.multiple_of(start, step), step)
-        total = terms[0](i, at).astype(jnp.float32)
-        for term in terms[1:]:
-            total = total + term(i, at).astype(jnp.float32)
-        target(i, at, total)
-        return 0
-
-    lax.fori_loop(0, count * per, one, 0)
-
-
-def reduce_steps(place, sender, grad, buffers, out):
-    from_core, sums, diag_y, diag_x, from_xy, from_z = buffers
-    nz, half = place.nz, place.nz // 2
-    rows = grad.shape[2]
-    low = jnp.bfloat16
-    groups = ((1, 1), (0, 1), (1, 0), (0, 0))
-    by_core = [
-        sender.send(grad.at[:, place.column(y=fy, c=1, x=fx)], from_core.at[i], place.device(c=1))
-        for i, (fy, fx) in enumerate(groups)
-    ]
-    yield
-
-    def put(slot, offset=0):
-        def store(i, at, value):
-            sums[slot, i + offset, at, :] = value.astype(low)
-
-        return store
-
-    def add_core(slot):
-        fy, fx = groups[slot]
-        column = place.column(y=fy, x=fx)
-        by_core[slot].wait_recv()
-        add_rows(
-            put(slot),
-            [lambda i, at: grad[i, column, at, :], lambda i, at: from_core[slot, i, at, :]],
-            nz,
-            rows,
-        )
-
-    low_z, high_z = pl.ds(0, half), pl.ds(half, nz - half)
-    add_core(0)
-    by_y = sender.send(sums.at[0, low_z], diag_y, place.device(y=1))
-    by_x = sender.send(sums.at[0, high_z], diag_x, place.device(x=1))
-    add_core(1)
-    x_high = sender.send(sums.at[1, high_z], from_xy.at[0, high_z], place.device(x=1))
-    add_core(2)
-    y_low = sender.send(sums.at[2, low_z], from_xy.at[1, low_z], place.device(y=1))
-    yield
-    add_core(3)
-    by_y.wait_recv()
-    add_rows(
-        put(1),
-        [lambda i, at: sums[1, i, at, :], lambda i, at: diag_y[i, at, :]],
-        half,
-        rows,
-    )
-    x_low = sender.send(sums.at[1, low_z], from_xy.at[0, low_z], place.device(x=1))
-    by_x.wait_recv()
-    add_rows(
-        put(2, half),
-        [lambda i, at: sums[2, i + half, at, :], lambda i, at: diag_x[i, at, :]],
-        nz - half,
-        rows,
-    )
-    y_high = sender.send(sums.at[2, high_z], from_xy.at[1, high_z], place.device(y=1))
-    yield
-    for copy in (x_high, y_low, x_low, y_high):
-        copy.wait_recv()
-    add_rows(
-        put(3),
-        [
-            lambda i, at: sums[3, i, at, :],
-            lambda i, at: from_xy[0, i, at, :],
-            lambda i, at: from_xy[1, i, at, :],
-        ],
-        nz,
-        rows,
-    )
-    by_z = [
-        sender.send(sums.at[3, place.zth(k)], from_z.at[k - 1], place.device(k=k)) for k in range(1, nz)
-    ]
-    yield
-    for copy in by_z:
-        copy.wait_recv()
-
-    def last(i, at, value):
-        out[at, :] = value
-
-    add_rows(
-        last,
-        [lambda i, at: sums[3, place.z, at, :]]
-        + [lambda i, at, k=k: from_z[k, at, :] for k in range(nz - 1)],
-        1,
-        rows,
-    )
-
-
-def reduce_kernel(shapes):
-    count = len(shapes)
-
-    def kernel(*refs):
-        grads, outs = refs[:count], refs[count : 2 * count]
-        scratch = refs[2 * count :]
-        buffers = [scratch[6 * i : 6 * i + 6] for i in range(count)]
-        send_sem, recv_sem = scratch[6 * count :]
-        place = Place()
-        sender = Sender(send_sem, recv_sem)
-        meet(place)
-        steps = [reduce_steps(place, sender, g, b, o) for g, b, o in zip(grads, buffers, outs)]
-        t = 0
-        while steps:
-            live = []
-            for i, step in enumerate(steps):
-                if i > t:
-                    live.append(step)
-                    continue
-                try:
-                    next(step)
-                    live.append(step)
-                except StopIteration:
-                    pass
-            steps = live
-            t += 1
-        sender.close()
-
-    return kernel
-
-
-def reduce_all(grads, collective_id):
-    nz = lax.axis_size("dp") // 4
-    n = nz * 8
-    blocks = [g.reshape(nz, 8, g.shape[0] // n, g.shape[1]) for g in grads]
-    copies = len(grads) * reduce_copies(nz)
-    scratch = []
-    for block in blocks:
-        scratch += reduce_buffers(nz, block.shape[2], block.shape[3])
-    return pl.pallas_call(
-        reduce_kernel([b.shape for b in blocks]),
-        out_shape=[jax.ShapeDtypeStruct(b.shape[2:], jnp.float32) for b in blocks],
-        in_specs=[pl.BlockSpec(memory_space=pltpu.VMEM)] * len(grads),
-        out_specs=[pl.BlockSpec(memory_space=pltpu.VMEM)] * len(grads),
-        scratch_shapes=scratch
-        + [pltpu.SemaphoreType.DMA((copies,)), pltpu.SemaphoreType.DMA((copies,))],
-        compiler_params=pltpu.CompilerParams(
-            collective_id=collective_id, has_side_effects=True, vmem_limit_bytes=56 << 20
-        ),
-    )(*blocks)
-
-
-def sum_small(vector):
-    bit = 1
-    while bit < n_devices():
-        vector = vector + swap(vector, bit)
-        bit *= 2
-    return vector
-
-
-fill_value = -1e30
-eps_norm = 1e-05
-code_absent = 30000.0
-
-
-def time_embed(steps, width):
-    half = width // 2
-    freqs = jnp.exp(jnp.arange(half, dtype=jnp.float32) * (-math.log(10000.0) / half))
-    angle = steps.astype(jnp.float32)[:, None] * freqs[None, :]
-    return jnp.concatenate([jnp.sin(angle), jnp.cos(angle)], axis=-1)
-
-
-def layer_norm(resid, gain, shift):
-    centre = resid - jnp.mean(resid, axis=-1, keepdims=True)
-    spread = jnp.mean(centre * centre, axis=-1, keepdims=True)
-    return centre * lax.rsqrt(spread + eps_norm) * gain + shift
-
-
-def inner(left, right):
-    return lax.dot_general(
-        left, right, (((0,), (0,)), ((), ())), preferred_element_type=jnp.float32
-    )
-
-
-def back_project(grad, weight):
-    return lax.dot_general(
-        grad, weight, (((1,), (1,)), ((), ())), preferred_element_type=jnp.float32
-    )
-
-
 NN = (((1,), (0,)), ((), ()))
 NT = (((1,), (1,)), ((), ()))
+TN = (((0,), (0,)), ((), ()))
 LOW = jnp.bfloat16
 F32 = jnp.float32
 
@@ -407,6 +206,128 @@
 
 def column_sum(value):
     return jnp.sum(value, axis=0, keepdims=True)
+
+
+def reduce_copies(nz):
+    return 4 + 2 + 4 + nz - 1
+
+
+def reduce_buffers(nz, rows, cols):
+    return dict(
+        core=pltpu.VMEM((4, nz, rows, cols), LOW),
+        diag=pltpu.VMEM((nz, rows, cols), LOW),
+        line=pltpu.VMEM((2, nz, rows, cols), LOW),
+        column=pltpu.VMEM((nz - 1, rows, cols), LOW),
+    )
+
+
+def add_rows(store, terms, count, rows):
+    step = min(rows, 16)
+    per = rows // step
+
+    def one(j):
+        i, start = j // per, (j % per) * step
+        at = pl.ds(pl.multiple_of(start, step), step)
+        total = terms[0](i, at).astype(F32)
+        for term in terms[1:]:
+            total = total + term(i, at).astype(F32)
+        store(i, at, total)
+
+    loop(count * per, one)
+
+
+def reduce_steps(place, sender, grad, buffers, out, split):
+    nz = place.nz
+    rows = grad.shape[2]
+    core, diag, line, column = (buffers[k] for k in ("core", "diag", "line", "column"))
+    groups = ((1, 1), (0, 1), (1, 0), (0, 0))
+    here = [place.column(y=fy, x=fx) for fy, fx in groups]
+    by_core = [
+        sender.send(grad.at[:, place.column(y=fy, c=1, x=fx)], core.at[i], place.device(c=1))
+        for i, (fy, fx) in enumerate(groups)
+    ]
+    yield
+
+    def put(slot, start=0):
+        def store(i, at, value):
+            grad[i + start, here[slot], at, :] = value.astype(LOW)
+
+        return store
+
+    def held(slot, start=0):
+        return lambda i, at: grad[i + start, here[slot], at, :]
+
+    def add_core(slot):
+        by_core[slot].wait_recv()
+        add_rows(put(slot), [held(slot), lambda i, at: core[slot, i, at, :]], nz, rows)
+
+    def part(slot, start, size):
+        return grad.at[pl.ds(start, size), here[slot]]
+
+    low, high = pl.ds(0, split), pl.ds(split, nz - split)
+    by_y = by_x = x_high = y_low = x_low = y_high = None
+    add_core(0)
+    if split > 0:
+        by_y = sender.send(part(0, 0, split), diag.at[low], place.device(y=1))
+    if split < nz:
+        by_x = sender.send(part(0, split, nz - split), diag.at[high], place.device(x=1))
+    add_core(1)
+    if split < nz:
+        x_high = sender.send(part(1, split, nz - split), line.at[0, high], place.device(x=1))
+    add_core(2)
+    if split > 0:
+        y_low = sender.send(part(2, 0, split), line.at[1, low], place.device(y=1))
+    add_core(3)
+    yield
+    if split > 0:
+        by_y.wait_recv()
+        add_rows(put(1), [held(1), lambda i, at: diag[i, at, :]], split, rows)
+        x_low = sender.send(part(1, 0, split), line.at[0, low], place.device(x=1))
+    if split < nz:
+        by_x.wait_recv()
+        add_rows(put(2, split), [held(2, split), lambda i, at: diag[i + split, at, :]], nz - split, rows)
+        y_high = sender.send(part(2, split, nz - split), line.at[1, high], place.device(y=1))
+    yield
+    for copy in (x_high, y_low, x_low, y_high):
+        if copy is not None:
+            copy.wait_recv()
+    add_rows(
+        put(3),
+        [held(3), lambda i, at: line[0, i, at, :], lambda i, at: line[1, i, at, :]],
+        nz,
+        rows,
+    )
+    by_z = [
+        sender.send(grad.at[place.zth(k), here[3]], column.at[k - 1], place.device(k=k))
+        for k in range(1, nz)
+    ]
+    yield
+    for copy in by_z:
+        copy.wait_recv()
+
+    def last(i, at, value):
+        out[at, :] = value
+
+    add_rows(
+        last,
+        [lambda i, at: grad[place.z, here[3], at, :]]
+        + [lambda i, at, k=k: column[k, at, :] for k in range(nz - 1)],
+        1,
+        rows,
+    )
+
+
+def sum_steps(place, sender, levels, taken):
+    partners = [place.device(c=1), place.device(x=1), place.device(y=1)]
+    bit = 1
+    while bit < place.nz:
+        partners.append(place.device(k=bit))
+        bit *= 2
+    for s, partner in enumerate(partners):
+        copy = sender.send(levels.at[s], taken.at[s], partner)
+        yield
+        copy.wait_recv()
+        levels[s + 1] = levels[s] + taken[s]
 
 
 def forward_kernel(by_hand, items, half_len, names_in, names_out, names_scratch, *refs):
@@ -449,13 +370,14 @@
     across = place.device(x=1)
     pump("w_qkv", "small")
     codes_over = sender.send(r["codes"], r["codes_taken"], across)
+    cols_over = sender.send(r["cols"], r["cols_taken"], across)
     half_item = [pl.ds(i * half_len, half_len) for i in range(items)]
     input_over = []
     for at in half_item[:2]:
         input_over.append(sender.send(r["input"].at[at], r["taken"].at[at], across))
     stream, sums = r["stream"], r["sums"]
     sums[...] = jnp.zeros_like(sums)
-    valid = [r["cols"][:, items + i : items + i + 1] for i in range(items)]
+    sums[7:8, 0:128] = column_sum(r["cols"][...])
     for i in range(items):
         embed = r["embed"][i : i + 1, :]
 
@@ -467,6 +389,7 @@
             sums[0:1, :] += column_sum(value * value * weight)
 
         loop(half_len // 32, make_stream)
+    save_stream = copy(stream.at[pl.ds(0, rows)], r["save_stream"])
     pump("w_qkv", "small", "w_o", "w_in")
     pump("w_qkv", "small")
     pump("w_qkv", "small")
@@ -512,6 +435,7 @@
     def project_other(j):
         at = tile(j, step)
         theirs = stream[rows : 2 * rows, :]
+        heads[5, :, at] = (mm(theirs, weight("v_qkv", 0, at)) + vectors[0:1, at]).astype(LOW)
         heads[2, :, at] = mm(theirs, weight("v_qkv", 1, at)).astype(LOW)
         heads[4, :, at] = (mm(theirs, weight("v_qkv", 2, at)) + vectors[1:2, at]).astype(LOW)
 
@@ -541,7 +465,8 @@
         loop(half_len // 32, make_other)
     loop(width // step, project_other)
     saved.append(copy(heads, r["save_heads"]))
-    saved.append(copy(r["permit"], r["save_permit"]))
+    saved.append(copy(r["codes_taken"], r["save_codes"]))
+    save_stream.wait()
     pump("w_o", "w_o", "w_in")
     lane = lax.broadcasted_iota(jnp.int32, (half_len, 2 * HD), 1)
     key_lane = lax.broadcasted_iota(jnp.int32, (2 * half_len, 2 * HD), 1)
@@ -570,7 +495,10 @@
             stream[at_rows, at] = mixed.astype(LOW)
 
         loop(width // (2 * HD), pair)
-
+        r["log_rows"][i] = r["logs"][i].T[:HEADS]
+        logs_over.append(sender.send(r["log_rows"].at[i], r["logs_taken"].at[i], across))
+
+    logs_over = []
     attend(0)
     pump("w_in", "w_in")
     if items > 1:
@@ -580,7 +508,7 @@
         attend(i)
     mixed = stream
     saved.append(copy(stream.at[pl.ds(0, rows)], r["save_mixed"]))
-    saved.append(copy(r["logs"], r["save_logs"]))
+    saved.append(copy(r["log_rows"], r["save_logs"]))
     if by_hand:
         run_out(gens["w_o"])
     load_o = copy(full["w_o"], r["v_o"])
@@ -604,6 +532,7 @@
             stream[to, :] = (value * gain_one + shift_one).astype(LOW)
 
         loop(half_len // 32, first_norm)
+    save_hidden = copy(stream.at[pl.ds(rows, rows)], r["save_hidden"])
     saved.append(copy(xhat, r["save_xhat"]))
     saved.append(copy(r["rstd"], r["save_rstd"]))
     if by_hand:
@@ -640,6 +569,7 @@
         made.wait()
     cot_in.wait()
     saved[2].wait()
+    save_hidden.wait()
     for i in range(items):
         at_rows = pl.ds(i * half_len, half_len)
         total = None
@@ -677,6 +607,11 @@
     saved.append(copy(stream.at[pl.ds(rows, rows)], r["save_back_low"]))
     saved.append(copy(r["back"], r["save_back"]))
     saved.append(copy(vectors, r["save_vectors"]))
+    for made in logs_over:
+        made.wait_recv()
+    saved.append(copy(r["logs_taken"], r["save_logs_taken"]))
+    cols_over.wait_recv()
+    saved.append(copy(r["cols_taken"], r["save_cols"]))
     for i, made in enumerate(saved):
         if i not in (0, 2):
             made.wait()
@@ -701,10 +636,14 @@
             outs["all_" + p] = shape((nz, 8) + ins[p].shape, ins[p].dtype)
             spaces_out.append(hbm)
     outs.update(
-        save_heads=shape((5, rows, width), LOW),
-        save_permit=shape((items, half_len, full_len), F32),
+        save_heads=shape((6, rows, width), LOW),
+        save_codes=shape(codes.shape, F32),
+        save_cols=shape(cols.shape, F32),
+        save_stream=shape((rows, width), LOW),
+        save_hidden=shape((rows, width), LOW),
         save_mixed=shape((rows, width), LOW),
-        save_logs=shape((items, half_len, 128), F32),
+        save_logs=shape((items, HEADS, half_len), F32),
+        save_logs_taken=shape((items, HEADS, half_len), F32),
         save_xhat=shape((rows, width), F32),
         save_rstd=shape((rows, 128), F32),
         act=shape((blocks, rows, width), LOW),
@@ -715,27 +654,30 @@
         save_vectors=shape((8, width), F32),
         sums=shape((8, width), F32),
     )
-    spaces_out += [hbm] * 12 + [vmem]
+    spaces_out += [hbm] * 16 + [vmem]
     if by_hand:
         small_full = (nz, 8) + small.shape
     else:
         small_full = small.shape
-    copies = 5 * gather_copies(nz) + items + 1
+    copies = 5 * gather_copies(nz) + 2 * items + 2
     scratch = dict(
         send=pltpu.SemaphoreType.DMA((copies,)),
         recv=pltpu.SemaphoreType.DMA((copies,)),
         local=pltpu.SemaphoreType.DMA((40,)),
         taken=pltpu.VMEM((rows, width), LOW),
         codes_taken=pltpu.VMEM(codes.shape, F32),
+        cols_taken=pltpu.VMEM(cols.shape, F32),
         stream=pltpu.VMEM((2 * rows, width), LOW),
         v_qkv=pltpu.VMEM((3, 4, 8, 32, width), LOW),
         v_small=pltpu.VMEM(small_full, F32),
         packed=pltpu.VMEM((small_full[0] * 8, small_full[-1]), F32),
         vectors=pltpu.VMEM((8, width), F32),
         v_b_in=pltpu.VMEM((8, width), F32),
-        heads=pltpu.VMEM((5, rows, width), LOW),
+        heads=pltpu.VMEM((6, rows, width), LOW),
         permit=pltpu.VMEM((items, half_len, full_len), F32),
         logs=pltpu.VMEM((items, half_len, 128), F32),
+        log_rows=pltpu.VMEM((items, HEADS, half_len), F32),
+        logs_taken=pltpu.VMEM((items, HEADS, half_len), F32),
         v_o=pltpu.VMEM((4, 8, 32, width), LOW),
         work=pltpu.VMEM((half_len, width), F32),
         xhat=pltpu.VMEM((rows, width), F32),
@@ -756,15 +698,562 @@
             collective_id=collective_id, has_side_effects=True, vmem_limit_bytes=62 << 20
         ),
     )(*ins.values())
+    return dict(zip(outs, results), codes=codes, cols=cols)
+
+
+class Kernel:
+    def __init__(self, names, refs):
+        self.refs = dict(zip(names, refs))
+        self.place = Place()
+        self.sender = Sender(self["send"], self["recv"])
+        self.count = 0
+        self.saved = []
+
+    def __getitem__(self, name):
+        return self.refs[name]
+
+    def copy(self, src, dst):
+        made = pltpu.make_async_copy(src, dst, self["local"].at[self.count])
+        self.count += 1
+        made.start()
+        return made
+
+    def save(self, src, dst):
+        self.saved.append(self.copy(src, dst))
+
+    def close(self):
+        for made in self.saved:
+            made.wait()
+        self.sender.close()
+
+
+def call(body, ins, spaces_in, outs, scratch, copies, collective_id):
+    vmem, hbm = pl.BlockSpec(memory_space=pltpu.VMEM), pl.BlockSpec(memory_space=pl.ANY)
+    scratch = dict(
+        send=pltpu.SemaphoreType.DMA((copies,)),
+        recv=pltpu.SemaphoreType.DMA((copies,)),
+        local=pltpu.SemaphoreType.DMA((48,)),
+        **scratch,
+    )
+    names = list(ins) + list(outs) + list(scratch)
+
+    def kernel(*refs):
+        body(Kernel(names, refs))
+
+    results = pl.pallas_call(
+        kernel,
+        out_shape=[jax.ShapeDtypeStruct(s, d) for s, d, _ in outs.values()],
+        in_specs=[vmem if name in spaces_in else hbm for name in ins],
+        out_specs=[vmem if space == "vmem" else hbm for _, _, space in outs.values()],
+        scratch_shapes=list(scratch.values()),
+        compiler_params=pltpu.CompilerParams(
+            collective_id=collective_id, has_side_effects=True, vmem_limit_bytes=63 << 20
+        ),
+    )(*ins.values())
     return dict(zip(outs, results))
 
 
-def scores_of(query, keys, code_row, query_block, key_pos, positions):
-    permit = (code_row[None, :] <= query_block[:, None]) | (key_pos[None, :] == positions[:, None])
-    raw = jnp.einsum("qhd,khd->hqk", query, keys, preferred_element_type=jnp.float32) * (
-        1.0 / math.sqrt(HD)
-    )
-    return jnp.where(permit[None], raw, fill_value)
+def feed_back(by_hand, items, half_len, fw, weights, collective_id):
+    blocks, rows, width = fw["act"].shape
+    nz = lax.axis_size("dp") // 4
+    half_width = width // 2
+    step = 256
+
+    def body(k):
+        place, sender = k.place, k.sender
+        load_low = k.copy(k["back_low"], k["v_low"])
+        load_act = [k.copy(k["act"].at[t], k["v_act"].at[t]) for t in range(blocks)]
+        load_out = k.copy(k["w_out"], k["v_out"])
+        load_slope = k.copy(k["slope"], k["v_slope"])
+        load_in = [
+            k.copy(k["w_in"].at[:, :, :, pl.ds(t * width, width)], k["v_in"].at[t]) for t in range(blocks)
+        ]
+        load_rest = [
+            k.copy(k["back"], k["v_back"]),
+            k.copy(k["xhat"], k["v_xhat"]),
+            k.copy(k["rstd"], k["v_rstd"]),
+            k.copy(k["w_o"], k["v_o"]),
+        ]
+        meet(place)
+        load_low.wait()
+        low, act, grad = k["v_low"], k["v_act"], k["grad"]
+        gens = []
+        if by_hand:
+            for q in range(2):
+                buffers = {name: k[f"{name}{q}"] for name in ("core", "diag", "line", "column")}
+                target = k["grad_out"].at[:, pl.ds(q * half_width, half_width)]
+                gens.append(reduce_steps(place, sender, grad.at[q], buffers, target, nz))
+
+        def pump(q):
+            if by_hand:
+                next(gens[q], None)
+
+        for t in range(blocks):
+            load_act[t].wait()
+
+            def outer(j, t=t):
+                part = mm(act[t, :, tile(j, step)], low[...], TN).astype(LOW)
+                part = part.reshape(step // 128, 128, width)
+                to = pl.ds(j * (step // 128), step // 128)
+                grad[0, t, to] = part[:, :, :half_width]
+                grad[1, t, to] = part[:, :, half_width:]
+
+            loop(width // step, outer)
+        pump(0)
+        pump(1)
+        if not by_hand:
+            for q in range(2):
+                k.save(grad.at[q], k["grad_out"].at[:, :, :, pl.ds(q * half_width, half_width)])
+        load_out.wait()
+        load_slope.wait()
+        sums = k["sums"]
+        sums[...] = jnp.zeros_like(sums)
+        for t in range(blocks):
+
+            def pull(j, t=t):
+                at = tile(j, step)
+                w_out = k["v_out"][t, pl.ds(j * (step // 128), step // 128)].reshape(step, width)
+                part = mm(low[...], w_out, NT) * k["v_slope"][t, :, at].astype(F32)
+                part = part.astype(LOW)
+                act[t, :, at] = part
+                sums[t : t + 1, at] = column_sum(part.astype(F32))
+
+            loop(width // step, pull)
+            if t < 2:
+                pump(t)
+        k.save(act, k["pre_grad"])
+        for made in load_in + load_rest:
+            made.wait()
+        gain = k["vectors"][4:5, :]
+        for i in range(items):
+            at_rows = pl.ds(i * half_len, half_len)
+            total = None
+            for t in range(blocks):
+                part = mm(act[t, at_rows, :], k["v_in"][t].reshape(width, width), NT)
+                total = part if total is None else total + part
+            k["work"][...] = total
+
+            def first_back(j, i=i):
+                at = pl.ds(pl.multiple_of(i * half_len + j * 32, 32), 32)
+                hidden = k["work"][tile(j, 32), :] + k["v_back"][at, :]
+                xhat = k["v_xhat"][at, :]
+                rstd = k["v_rstd"][at, 0:1]
+                sums[4:5, :] += column_sum(hidden * xhat)
+                sums[5:6, :] += column_sum(hidden)
+                scaled = hidden * gain
+                value = rstd * (
+                    scaled
+                    - jnp.mean(scaled, axis=-1, keepdims=True)
+                    - xhat * jnp.mean(scaled * xhat, axis=-1, keepdims=True)
+                )
+                k["v_back"][at, :] = value
+                value_low = value.astype(LOW)
+                low[at, :] = value_low
+                sums[6:7, :] += column_sum(value_low.astype(F32))
+
+            loop(half_len // 32, first_back)
+            if i < 2:
+                pump(i)
+        w_o = k["v_o"][...].reshape(width, width)
+        for i in range(items):
+            at_rows = pl.ds(i * half_len, half_len)
+            k["v_mixed_grad"][at_rows, :] = mm(low[at_rows, :], w_o, NT).astype(LOW)
+        over = sender.send(k["v_mixed_grad"], k["v_taken"], place.device(x=1))
+        k.save(k["v_back"], k["input_part"])
+        k.save(low, k["attn_grad"])
+        k.save(k["v_mixed_grad"], k["mixed_grad"])
+        for q in range(2):
+            pump(q)
+        for gen in gens:
+            run_out(gen)
+        over.wait_recv()
+        k.save(k["v_taken"], k["mixed_grad_taken"])
+        k.close()
+
+    ins = dict(
+        back_low=fw["save_back_low"],
+        act=fw["act"],
+        w_out=weights[3],
+        slope=fw["save_slope"],
+        w_in=weights[2],
+        back=fw["save_back"],
+        xhat=fw["save_xhat"],
+        rstd=fw["save_rstd"],
+        w_o=weights[1],
+        vectors=fw["save_vectors"],
+    )
+    outs = dict(
+        pre_grad=((blocks, rows, width), LOW, "hbm"),
+        input_part=((rows, width), F32, "hbm"),
+        attn_grad=((rows, width), LOW, "hbm"),
+        mixed_grad=((rows, width), LOW, "hbm"),
+        mixed_grad_taken=((rows, width), LOW, "hbm"),
+        sums=((8, width), F32, "vmem"),
+    )
+    if by_hand:
+        outs["grad_out"] = ((128, width), F32, "vmem")
+    else:
+        outs["grad_out"] = ((4, 8, 128, width), LOW, "hbm")
+    scratch = dict(
+        v_low=pltpu.VMEM((rows, width), LOW),
+        v_act=pltpu.VMEM((blocks, rows, width), LOW),
+        v_out=pltpu.VMEM((blocks, 8, 128, width), LOW),
+        v_slope=pltpu.VMEM((blocks, rows, width), LOW),
+        v_in=pltpu.VMEM((blocks, 4, 8, 32, width), LOW),
+        v_back=pltpu.VMEM((rows, width), F32),
+        v_xhat=pltpu.VMEM((rows, width), F32),
+        v_rstd=pltpu.VMEM((rows, 128), F32),
+        v_o=pltpu.VMEM((4, 8, 32, width), LOW),
+        v_mixed_grad=pltpu.VMEM((rows, width), LOW),
+        v_taken=pltpu.VMEM((rows, width), LOW),
+        work=pltpu.VMEM((half_len, width), F32),
+        grad=pltpu.VMEM((2, 4, 8, 128, half_width), LOW),
+    )
+    copies = 1
+    if by_hand:
+        copies += 2 * reduce_copies(nz)
+        for q in range(2):
+            for name, buffer in reduce_buffers(nz, 128, half_width).items():
+                scratch[f"{name}{q}"] = buffer
+    return call(body, ins, ("vectors",), outs, scratch, copies, collective_id)
+
+
+def attend_back(by_hand, items, half_len, fw, fb, collective_id):
+    blocks, rows, width = fw["act"].shape
+    nz = lax.axis_size("dp") // 4
+    chunks = blocks + 1
+    step = 256
+    scale = 1.0 / math.sqrt(HD)
+
+    def body(k):
+        place, sender = k.place, k.sender
+        load_hidden = k.copy(k["hidden"], k["v_left"])
+        load_pre = [k.copy(k["pre_grad"].at[t], k["v_pre"].at[t]) for t in range(blocks)]
+        load_mixed = [k.copy(k["attn_grad"], k["v_attn"])]
+        load_heads = [
+            k.copy(k["heads"], k["v_heads"]),
+            k.copy(k["mixed_grad"], k["v_grad"].at[0]),
+            k.copy(k["mixed_grad_taken"], k["v_grad"].at[1]),
+        ]
+        meet(place)
+        grad = k["grad"]
+        gens = []
+        if by_hand:
+            for q in range(chunks):
+                buffers = {name: k[f"{name}{q}"] for name in ("core", "diag", "line", "column")}
+                if q < blocks:
+                    target = k["grad_in"].at[:, pl.ds(q * width, width)]
+                else:
+                    target = k["grad_o"]
+                gens.append(reduce_steps(place, sender, grad.at[q], buffers, target, nz // 2))
+
+        def pump(*which):
+            if by_hand:
+                for q in which:
+                    next(gens[q], None)
+
+        load_hidden.wait()
+        left, turned = k["v_left"], k["v_turned"]
+
+        def turn(j):
+            turned[tile(j, 128), :] = left[:, tile(j, 128)].T
+
+        def outer(q, right):
+            def one(j):
+                at = tile(j, step)
+                part = mm(turned[...], right[:, at]).astype(LOW)
+                grad[q, :, :, :, at] = part.reshape(4, 8, 32, step)
+
+            loop(width // step, one)
+
+        loop(width // 128, turn)
+        load_left = None
+        for t in range(blocks):
+            load_pre[t].wait()
+            outer(t, k["v_pre"].at[t])
+            pump(t)
+            if t == 0:
+                load_left = k.copy(k["mixed"], left)
+            if t >= 1:
+                pump(t - 1)
+        load_left.wait()
+        for made in load_mixed:
+            made.wait()
+        loop(width // 128, turn)
+        outer(blocks, k["v_attn"])
+        pump(blocks)
+        for made in load_heads:
+            made.wait()
+        same = lax.broadcasted_iota(jnp.int32, (half_len, half_len), 0) == lax.broadcasted_iota(
+            jnp.int32, (half_len, half_len), 1
+        )
+        for i in range(items):
+            asked = k["codes"][items + i : items + i + 1, :]
+            asked_taken = k["codes_taken"][items + i : items + i + 1, :]
+            code = k["cols"][:, 2 * items + i : 2 * items + i + 1]
+            code_taken = k["cols_taken"][:, 2 * items + i : 2 * items + i + 1]
+            k["permit"][i, 0:half_len, :] = jnp.where((code <= asked) | same, 0.0, fill_value)
+            k["permit"][i, half_len : 2 * half_len, :] = jnp.where(code_taken <= asked, 0.0, fill_value)
+            k["permit_taken"][i] = jnp.where(code <= asked_taken, 0.0, fill_value)
+        heads, grads, result = k["v_heads"], k["v_grad"], k["v_pre"]
+        lane = lax.broadcasted_iota(jnp.int32, (half_len, 2 * HD), 1)
+        key_lane = lax.broadcasted_iota(jnp.int32, (2 * half_len, 2 * HD), 1)
+        nothing = jnp.zeros((), LOW)
+
+        def ours(i):
+            at_rows = pl.ds(i * half_len, half_len)
+
+            def pair(p):
+                at = tile(p, 2 * HD)
+                query = heads[0, at_rows, at]
+                keys = jnp.concatenate([heads[1, at_rows, at], heads[2, at_rows, at]], axis=0)
+                values = jnp.concatenate([heads[3, at_rows, at], heads[4, at_rows, at]], axis=0)
+                grad_row = grads[0, at_rows, at]
+                query_part = key_part = value_part = None
+                for h in range(2):
+                    mine = (lane < HD) == (h == 0)
+                    key_mine = (key_lane < HD) == (h == 0)
+                    query_h = jnp.where(mine, query, nothing)
+                    grad_h = jnp.where(mine, grad_row, nothing)
+                    keys_h = jnp.where(key_mine, keys, nothing)
+                    at_head = pl.ds(2 * p + h, 1)
+                    scores = mm(keys, query_h * scale, NT) + (k["permit"][i] - k["logs"][i, at_head, :])
+                    probs = jnp.exp(scores)
+                    prob_grad = mm(values, grad_h, NT)
+                    centre = column_sum(probs * prob_grad)
+                    k["centre"][i, at_head, :] = centre
+                    score_grad = (probs * (prob_grad - centre)).astype(LOW)
+                    parts = (
+                        mm(score_grad, keys_h, TN),
+                        mm(score_grad[:half_len], query_h),
+                        mm(probs[:half_len].astype(LOW), grad_h),
+                    )
+                    if h == 0:
+                        query_part, key_part, value_part = parts
+                    else:
+                        query_part = query_part + parts[0]
+                        key_part = key_part + parts[1]
+                        value_part = value_part + parts[2]
+                query_low = (query_part * scale).astype(LOW)
+                result[0, at_rows, at] = query_low
+                k["sums"][0:1, at] += column_sum(query_low.astype(F32))
+                k["parts"][0, at_rows, at] = key_part
+                k["parts"][1, at_rows, at] = value_part
+
+            loop(width // (2 * HD), pair)
+
+        def theirs(i):
+            at_rows = pl.ds(i * half_len, half_len)
+
+            def pair(p):
+                at = tile(p, 2 * HD)
+                query = heads[5, at_rows, at]
+                keys, values = heads[1, at_rows, at], heads[3, at_rows, at]
+                grad_row = grads[1, at_rows, at]
+                key_part, value_part = k["parts"][0, at_rows, at], k["parts"][1, at_rows, at]
+                for h in range(2):
+                    mine = (lane < HD) == (h == 0)
+                    query_h = jnp.where(mine, query, nothing)
+                    grad_h = jnp.where(mine, grad_row, nothing)
+                    at_head = pl.ds(2 * p + h, 1)
+                    scores = mm(keys, query_h * scale, NT) + (
+                        k["permit_taken"][i] - k["logs_taken"][i, at_head, :]
+                    )
+                    probs = jnp.exp(scores)
+                    prob_grad = mm(values, grad_h, NT)
+                    score_grad = (probs * (prob_grad - k["centre_taken"][i, at_head, :])).astype(LOW)
+                    key_part = key_part + mm(score_grad, query_h)
+                    value_part = value_part + mm(probs.astype(LOW), grad_h)
+                result[1, at_rows, at] = (key_part * scale).astype(LOW)
+                value_low = value_part.astype(LOW)
+                result[2, at_rows, at] = value_low
+                k["sums"][1:2, at] += column_sum(value_low.astype(F32))
+
+            loop(width // (2 * HD), pair)
+
+        k["sums"][...] = jnp.zeros_like(k["sums"])
+        over = []
+        plan = {0: (0, 1, 2, 3, 4), 1: (3, 0, 1, 2), 2: (3, 4)}
+        for i in range(items):
+            ours(i)
+            over.append(sender.send(k["centre"].at[i], k["centre_taken"].at[i], place.device(x=1)))
+            pump(*plan.get(i, ()))
+        k.save(result.at[0], k["joint_grad"].at[0])
+        for i in range(items):
+            over[i].wait_recv()
+            theirs(i)
+            if i == 0:
+                pump(0, 1, 2, 3, 4)
+        k.save(result.at[1], k["joint_grad"].at[1])
+        k.save(result.at[2], k["joint_grad"].at[2])
+        for gen in gens:
+            run_out(gen)
+        if not by_hand:
+            for q in range(blocks):
+                k.save(grad.at[q], k["grad_in"].at[:, :, :, pl.ds(q * width, width)])
+            k.save(grad.at[blocks], k["grad_o"])
+        k.close()
+
+    ins = dict(
+        hidden=fw["save_hidden"],
+        pre_grad=fb["pre_grad"],
+        mixed=fw["save_mixed"],
+        attn_grad=fb["attn_grad"],
+        heads=fw["save_heads"],
+        mixed_grad=fb["mixed_grad"],
+        mixed_grad_taken=fb["mixed_grad_taken"],
+        codes=fw["codes"],
+        codes_taken=fw["save_codes"],
+        cols=fw["cols"],
+        cols_taken=fw["save_cols"],
+        logs=fw["save_logs"],
+        logs_taken=fw["save_logs_taken"],
+    )
+    outs = dict(
+        joint_grad=((3, rows, width), LOW, "hbm"),
+        sums=((8, width), F32, "vmem"),
+    )
+    if by_hand:
+        outs["grad_in"] = ((32, blocks * width), F32, "vmem")
+        outs["grad_o"] = ((32, width), F32, "vmem")
+    else:
+        outs["grad_in"] = ((4, 8, 32, blocks * width), LOW, "hbm")
+        outs["grad_o"] = ((4, 8, 32, width), LOW, "hbm")
+    scratch = dict(
+        v_left=pltpu.VMEM((rows, width), LOW),
+        v_turned=pltpu.VMEM((width, rows), LOW),
+        v_pre=pltpu.VMEM((blocks, rows, width), LOW),
+        v_attn=pltpu.VMEM((rows, width), LOW),
+        v_heads=pltpu.VMEM((6, rows, width), LOW),
+        v_grad=pltpu.VMEM((2, rows, width), LOW),
+        grad=pltpu.VMEM((chunks, 4, 8, 32, width), LOW),
+        permit=pltpu.VMEM((items, 2 * half_len, half_len), F32),
+        permit_taken=pltpu.VMEM((items, half_len, half_len), F32),
+        parts=pltpu.VMEM((2, rows, width), F32),
+        centre=pltpu.VMEM((items, HEADS, half_len), F32),
+        centre_taken=pltpu.VMEM((items, HEADS, half_len), F32),
+    )
+    copies = items
+    if by_hand:
+        copies += chunks * reduce_copies(nz)
+        for q in range(chunks):
+            for name, buffer in reduce_buffers(nz, 32, width).items():
+                scratch[f"{name}{q}"] = buffer
+    spaces = ("codes", "codes_taken", "cols", "cols_taken", "logs", "logs_taken")
+    return call(body, ins, spaces, outs, scratch, copies, collective_id)
+
+
+def project_back(by_hand, items, half_len, fw, fb, ab, weights, collective_id):
+    _, rows, width = ab["joint_grad"].shape
+    nz = lax.axis_size("dp") // 4
+    step = 256
+    stages = 3 + (nz - 1).bit_length()
+
+    def body(k):
+        place, sender = k.place, k.sender
+        load_stream = k.copy(k["stream"], k["v_left"])
+        load_joint = [k.copy(k["joint_grad"].at[t], k["v_joint"].at[t]) for t in range(3)]
+        load_qkv = [
+            k.copy(k["w_qkv"].at[:, :, :, pl.ds(t * width, width)], k["v_qkv"].at[t]) for t in range(3)
+        ]
+        load_part = k.copy(k["input_part"], k["v_part"])
+        meet(place)
+        levels = k["levels"]
+        for s, name in enumerate(("sums_one", "sums_two", "sums_three")):
+            levels[0, 8 * s : 8 * s + 8, :] = k[name][...]
+        small = sum_steps(place, sender, levels, k["levels_taken"])
+        next(small)
+        grad = k["grad"]
+        gens = []
+        if by_hand:
+            for q in range(3):
+                buffers = {name: k[f"{name}{q}"] for name in ("core", "diag", "line", "column")}
+                target = k["grad_qkv"].at[:, pl.ds(q * width, width)]
+                gens.append(reduce_steps(place, sender, grad.at[q], buffers, target, nz // 2))
+
+        def pump(*which):
+            if by_hand:
+                for q in which:
+                    next(gens[q], None)
+
+        load_stream.wait()
+        left, turned = k["v_left"], k["v_turned"]
+
+        def turn(j):
+            turned[tile(j, 128), :] = left[:, tile(j, 128)].T
+
+        loop(width // 128, turn)
+        for q in range(3):
+            load_joint[q].wait()
+
+            def outer(j, q=q):
+                at = tile(j, step)
+                part = mm(turned[...], k["v_joint"][q, :, at]).astype(LOW)
+                grad[q, :, :, :, at] = part.reshape(4, 8, 32, step)
+
+            loop(width // step, outer)
+            pump(q)
+        pump(0)
+        next(small, None)
+        for made in load_qkv + [load_part]:
+            made.wait()
+        for i in range(items):
+            at_rows = pl.ds(i * half_len, half_len)
+            total = k["v_part"][at_rows, :]
+            for q in range(3):
+                total = total + mm(k["v_joint"][q, at_rows, :], k["v_qkv"][q].reshape(width, width), NT)
+            left[at_rows, :] = total.astype(LOW)
+            if i == 0:
+                pump(1)
+            if i == 1:
+                pump(2, 0)
+                next(small, None)
+        k.save(left, k["input_grad"])
+        pump(1, 2)
+        next(small, None)
+        pump(0, 1, 2)
+        for gen in gens + [small]:
+            run_out(gen)
+        k["totals"][...] = levels[stages]
+        if not by_hand:
+            for q in range(3):
+                k.save(grad.at[q], k["grad_qkv"].at[:, :, :, pl.ds(q * width, width)])
+        k.close()
+
+    ins = dict(
+        stream=fw["save_stream"],
+        joint_grad=ab["joint_grad"],
+        w_qkv=weights[0],
+        input_part=fb["input_part"],
+        sums_one=fw["sums"],
+        sums_two=fb["sums"],
+        sums_three=ab["sums"],
+    )
+    outs = dict(
+        input_grad=((rows, width), LOW, "hbm"),
+        totals=((24, width), F32, "vmem"),
+    )
+    if by_hand:
+        outs["grad_qkv"] = ((32, 3 * width), F32, "vmem")
+    else:
+        outs["grad_qkv"] = ((4, 8, 32, 3 * width), LOW, "hbm")
+    scratch = dict(
+        v_left=pltpu.VMEM((rows, width), LOW),
+        v_turned=pltpu.VMEM((width, rows), LOW),
+        v_joint=pltpu.VMEM((3, rows, width), LOW),
+        v_qkv=pltpu.VMEM((3, 4, 8, 32, width), LOW),
+        v_part=pltpu.VMEM((rows, width), F32),
+        grad=pltpu.VMEM((3, 4, 8, 32, width), LOW),
+        levels=pltpu.VMEM((stages + 1, 24, width), F32),
+        levels_taken=pltpu.VMEM((stages, 24, width), F32),
+    )
+    copies = stages
+    if by_hand:
+        copies += 3 * reduce_copies(nz)
+        for q in range(3):
+            for name, buffer in reduce_buffers(nz, 32, width).items():
+                scratch[f"{name}{q}"] = buffer
+    return call(body, ins, ("sums_one", "sums_two", "sums_three"), outs, scratch, copies, collective_id)
 
 
 def body(
@@ -785,17 +1274,18 @@
 ):
     items, half_len, width = block_input.shape
     rows = items * half_len
-    f32, low = jnp.float32, jnp.bfloat16
+    f32 = jnp.float32
     n = n_devices()
-    positions = lax.axis_index("ctx") * half_len + jnp.arange(half_len, dtype=jnp.int32)
-    other_positions = (1 - lax.axis_index("ctx")) * half_len + jnp.arange(half_len, dtype=jnp.int32)
-    key_pos = jnp.concatenate([positions, other_positions])
-    valid = (positions[None, :] < lengths[:, None]) & ((mask == 1) | (positions[None, :] == 0))
-    code_local = jnp.where(valid, blocks.astype(f32), code_absent)
     share = width // n
     b_count = b_in.shape[0]
-    share = width // n
-    b_count = b_in.shape[0]
+    positions = lax.axis_index("ctx") * half_len + jnp.arange(half_len, dtype=jnp.int32)
+    valid = (positions[None, :] < lengths[:, None]) & ((mask == 1) | (positions[None, :] == 0))
+    numbers = blocks.astype(f32)
+    key_codes = jnp.where(valid, numbers, code_absent)
+    codes = jnp.pad(jnp.concatenate([key_codes, numbers]), ((0, 8 - 2 * items), (0, 0)))
+    cols = jnp.concatenate([numbers, valid.astype(f32), key_codes]).T
+    cols = jnp.pad(cols, ((0, 0), (0, 128 - 3 * items)))
+    embed = jnp.pad(time_embed(timesteps, width), ((0, 8 - items), (0, 0)))
     small = jnp.concatenate([b_in, biases.reshape(-1), gains.reshape(-1), shifts.reshape(-1)])
     small_wide = -(-small.shape[0] // 128) * 128
     small = jnp.pad(small.astype(f32), (0, small_wide - small.shape[0]))
@@ -806,11 +1296,6 @@
         weights = [lax.all_gather(w, AXES, axis=0, tiled=True) for w in weights]
         weights = [w.reshape(4, 8, w.shape[0] // 32, w.shape[1]) for w in weights]
         small = lax.all_gather(small, AXES, axis=0).reshape(n // 8, 8, 8, small_wide)
-    embed = time_embed(timesteps, width)
-    embed_rows = jnp.pad(embed, ((0, 8 - items), (0, 0)))
-    codes = jnp.pad(code_local, ((0, 8 - items), (0, 0)))
-    cols = jnp.concatenate([blocks.astype(f32), valid.astype(f32)], axis=0).T
-    cols = jnp.pad(cols, ((0, 0), (0, 128 - 2 * items)))
     fw = forward(
         by_hand,
         items,
@@ -818,7 +1303,7 @@
         weights,
         small,
         block_input.reshape(rows, width),
-        embed_rows,
+        embed,
         codes,
         cols,
         cotangent.reshape(rows, width),
@@ -826,124 +1311,33 @@
     )
     if by_hand:
         weights = [fw["all_" + p] for p in ("w_qkv", "w_o", "w_in", "w_out")]
-    w_qkv_all, w_o_all, w_in_all, w_out_all = (w.reshape(-1, w.shape[-1]) for w in weights)
-    gain_full = fw["save_vectors"][4:6]
-    shift_full = fw["save_vectors"][6:8]
-    code_all = jnp.concatenate([code_local, swap(code_local, X)], axis=1)
-    stream = (block_input.astype(f32) + embed[:, None, :]).reshape(rows, width)
-    stream_low = stream.astype(low)
-    full_len = 2 * half_len
-    saved_heads = fw["save_heads"].reshape(5, items, half_len, width)
-    query_four = saved_heads[0].reshape(items, half_len, HEADS, HD)
-    key_four = jnp.concatenate([saved_heads[1], saved_heads[2]], axis=1).reshape(items, full_len, HEADS, HD)
-    value_four = jnp.concatenate([saved_heads[3], saved_heads[4]], axis=1).reshape(items, full_len, HEADS, HD)
-    query_block = blocks.astype(f32)
-    log_totals = fw["save_logs"][:, :, :HEADS].transpose(0, 2, 1)
-    mixed_low = fw["save_mixed"]
-    act_low = fw["act"].transpose(1, 0, 2).reshape(rows, -1)
-    slope = fw["save_slope"].transpose(1, 0, 2).reshape(rows, -1)
-    xhat_one = fw["save_xhat"]
-    rstd_one = fw["save_rstd"][:, :1]
-    hidden_low = (xhat_one * gain_full[0] + shift_full[0]).astype(low)
-    output = fw["output"].reshape(items, half_len, width)
-    dres_two = fw["save_back"]
-    branch_grad = fw["save_back_low"]
-    fsums = fw["sums"]
-    local_sums = jnp.concatenate([jnp.sum(fsums[:4], axis=1), jnp.sum(valid.astype(f32))[None]])
-    gain_two_grad, shift_two_grad = fsums[5], fsums[6]
-
-    grad_out_part = inner(act_low, branch_grad).astype(low)
-    act_grad = back_project(branch_grad, w_out_all)
-    pre_grad = (act_grad * slope.astype(f32)).astype(low)
-    grad_in_part = inner(hidden_low, pre_grad).astype(low)
-    dhidden = dres_two + back_project(pre_grad, w_in_all)
-    scaled = dhidden * gain_full[0]
-    dres_one = rstd_one * (
-        scaled
-        - jnp.mean(scaled, axis=-1, keepdims=True)
-        - xhat_one * jnp.mean(scaled * xhat_one, axis=-1, keepdims=True)
-    )
-    gain_one_grad = jnp.sum(dhidden * xhat_one, axis=0)
-    shift_one_grad = jnp.sum(dhidden, axis=0)
-    attn_grad = dres_one.astype(jnp.bfloat16)
-    grad_o_part = inner(mixed_low, attn_grad).astype(low)
-    mixed_grad = (
-        back_project(attn_grad, w_o_all).astype(jnp.bfloat16).reshape(items, half_len, HEADS, HD)
-    )
-
-    def attend_back(inputs):
-        query, keys, values, code_row, block_row, log_row, grad_row = inputs
-        scores = scores_of(query, keys, code_row, block_row, key_pos, positions)
-        probs = jnp.exp(scores - log_row[..., None])
-        value_part = jnp.einsum(
-            "hqk,qhd->khd", probs.astype(jnp.bfloat16), grad_row, preferred_element_type=jnp.float32
-        )
-        prob_grad = jnp.einsum("qhd,khd->hqk", grad_row, values, preferred_element_type=jnp.float32)
-        centre = jnp.sum(probs * prob_grad, axis=-1, keepdims=True)
-        score_grad = (probs * (prob_grad - centre)).astype(jnp.bfloat16)
-        query_part = jnp.einsum(
-            "hqk,khd->qhd", score_grad, keys, preferred_element_type=jnp.float32
-        ) * (1.0 / math.sqrt(HD))
-        key_part = jnp.einsum(
-            "hqk,qhd->khd", score_grad, query, preferred_element_type=jnp.float32
-        ) * (1.0 / math.sqrt(HD))
-        return (query_part, key_part, value_part)
-
-    query_part, key_part, value_part = lax.map(
-        attend_back,
-        (query_four, key_four, value_four, code_all, query_block, log_totals, mixed_grad),
-    )
-    key_part = key_part.reshape(items, full_len, width)
-    value_part = value_part.reshape(items, full_len, width)
-    away = jnp.stack([key_part[:, half_len:], value_part[:, half_len:]]).astype(low)
-    back = swap(away, X).astype(f32)
-    query_grad_low = query_part.reshape(rows, width).astype(jnp.bfloat16)
-    key_grad_low = (key_part[:, :half_len] + back[0]).reshape(rows, width).astype(jnp.bfloat16)
-    value_grad_low = (value_part[:, :half_len] + back[1]).reshape(rows, width).astype(jnp.bfloat16)
-    joint_grad = jnp.concatenate([query_grad_low, key_grad_low, value_grad_low], axis=1)
-    grad_qkv_part = inner(stream_low, joint_grad).astype(low)
-    if by_hand:
-        grad_out, grad_in = reduce_all([grad_out_part, grad_in_part], 2)
-        grad_qkv, grad_o = reduce_all([grad_qkv_part, grad_o_part], 3)
-    else:
-        grad_out, grad_in, grad_qkv, grad_o = (
-            lax.psum_scatter(part.astype(f32), AXES, scatter_dimension=0, tiled=True)
-            for part in (grad_out_part, grad_in_part, grad_qkv_part, grad_o_part)
-        )
-    input_grad = (
-        (dres_one + back_project(joint_grad, w_qkv_all))
-        .astype(jnp.bfloat16)
-        .reshape(items, half_len, width)
-    )
-    b_in_part = jnp.sum(pre_grad.astype(jnp.float32), axis=0)
-    parts = [
-        jnp.sum(query_grad_low.astype(jnp.float32), axis=0),
-        jnp.sum(value_grad_low.astype(jnp.float32), axis=0),
-        jnp.sum(attn_grad.astype(jnp.float32), axis=0),
-        fsums[4],
-        gain_one_grad,
-        gain_two_grad,
-        shift_one_grad,
-        shift_two_grad,
-    ]
-    sums = sum_small(jnp.concatenate([b_in_part] + parts + [local_sums]))
-    ff = b_in_part.shape[0]
+    fb = feed_back(by_hand, items, half_len, fw, weights, 2)
+    ab = attend_back(by_hand, items, half_len, fw, fb, 3)
+    pb = project_back(by_hand, items, half_len, fw, fb, ab, weights, 4)
+    grads = [pb["grad_qkv"], ab["grad_o"], ab["grad_in"], fb["grad_out"]]
+    if not by_hand:
+        grads = [
+            lax.psum_scatter(
+                part.astype(f32).reshape(-1, part.shape[-1]), AXES, scatter_dimension=0, tiled=True
+            )
+            for part in grads
+        ]
+    totals = pb["totals"]
     me = my_index()
-    grad_b_in = lax.dynamic_slice(sums, (me * b_count,), (b_count,))
-    grads = lax.dynamic_slice(sums[ff : ff + 8 * width].reshape(8, width), (0, me * share), (8, share))
-    totals = sums[ff + 8 * width :]
-    rms = jnp.sqrt(totals[:4] / (totals[4] * width))
+    grad_b_in = lax.dynamic_slice(totals[8:12].reshape(-1), (me * b_count,), (b_count,))
+    order = (16, 17, 14, 4, 12, 5, 13, 6)
+    mine = lax.dynamic_slice(totals, (0, me * share), (24, share))
+    mine = jnp.stack([mine[row] for row in order])
+    count = jnp.sum(totals[7, items : 2 * items])
+    rms = jnp.sqrt(jnp.sum(totals[:4], axis=1) / (count * width))
     return (
-        output,
-        input_grad,
-        grad_qkv,
-        grad_o,
-        grad_in,
-        grad_out,
+        fw["output"].reshape(block_input.shape),
+        pb["input_grad"].reshape(block_input.shape),
+        *grads,
         grad_b_in,
-        grads[:4],
-        grads[4:6],
-        grads[6:8],
+        mine[:4],
+        mine[4:6],
+        mine[6:8],
         rms,
     )
 

time: 730 us -> 473 us (0.65)
  matrix products: 125 us -> 0 us
  local copies, waits for them, and re-layouts: 129 us -> 12.8 us
  Pallas kernels: 357 us -> 441 us
  waiting for transfers between devices: 47.8 us -> 0 us
  other arithmetic: 42.6 us -> 8.88 us
  starting transfers between devices: 14.6 us -> 0 us
    dot_general x23 -> x0, matrix products: 125 us -> none  [the longest x4 41.3 us: back_project(): lax.dot_general(grad, weight, (((1,), (1,)), ((), ())), preferred_element...]
    pallas_call x2 -> x3, Pallas kernels: 163 us -> 240 us  [call(): pl.pallas_call(kernel, out_shape=[jax.ShapeDtypeStruct(s, d) for s, d, _...]
    ppermute x7 -> x0, waiting for transfers between devices: 47.8 us -> none  [swap(): lax.ppermute(array, AXES, [(i, i ^ bits) for i in range(n_devices())])]
    convert_element_type x7 -> x0, local copies, waits for them, and re-layouts: 35.2 us -> none  [the longest x2 25.5 us: body(): pre_grad = (act_grad * slope.astype(f32)).astype(low)]
    concatenate x6 -> x1, local copies, waits for them, and re-layouts: 21.3 us -> 0.12 us  [body(): cols = jnp.concatenate([numbers, valid.astype(f32), key_codes]).T]
    convert_element_type x8 -> x2, other arithmetic: 20.8 us -> 1.45 us  [the longest x1 0.77 us: body(): cols = jnp.concatenate([numbers, valid.astype(f32), key_codes]).T]
    unnamed x83 -> x17, local copies, waits for them, and re-layouts: 26 us -> 6.99 us
    ppermute x7 -> x0, starting transfers between devices: 14.6 us -> none  [swap(): lax.ppermute(array, AXES, [(i, i ^ bits) for i in range(n_devices())])]
  transfers between devices with their start and end apart: 7 -> 0, of which waited for: 1 -> 0; matrix products, arithmetic and copies ran while one was open for 30% -> 0% of each run, Pallas kernels for 50% -> 0%
where the time goes in v4:
time: 473 us; the launch traced here: 464 us
  Pallas kernels  441 us (93%)
  local copies, waits for them, and re-layouts  12.8 us (3%)
  other arithmetic  8.88 us (2%)
    pallas_call x3, Pallas kernels, call(): pl.pallas_call(kernel, out_shape=[jax.ShapeDtypeStruct(s, d) for s, d, _...  240 us
    pallas_call x1, Pallas kernels, forward(): pl.pallas_call(partial(forward_kernel, by_hand, items, half_len, list(ins...  200 us

profile of v4, /device:TPU:0, one launch (start us, length us, event | category | flops | bytes accessed | tf_op | source)
XLA Modules:
  0.0 464.4 jit_solution(9019790993093252442)
XLA Ops:
  0.7 0.8 fusion
  1.4 0.7 broadcast_select_fusion
  2.1 0.7 convert_element_type.24
  2.8 0.1 copy.30
  3.0 0.7 pad.14.refs_8_.refs_9_
  3.6 0.6 select_maximum_fusion.1.refs_7_
  4.2 0.7 convert_element_type.23
  4.9 0.1 multiply_sine_fusion
  5.0 0.6 select_maximum_fusion.refs_6_
  5.7 0.8 concatenate.25
  6.4 0.7 concatenate.26
  7.2 0.7 concatenate.27
  7.9 0.7 maximum_convert_fusion
  8.6 0.6 broadcast_in_dim.6.refs_1_
  9.2 200.4 %shard_map.221 = (bf16[4,8,32,3072]{3,2,1,0:T(8,128)(2,1)}, f32[4,8,8,384]{3,2,1,0:T(8,128)}, bf16[4,8,32,1024]{3,2,1,0:T(8,128)(2,1)}, bf16[4,8,32,4096]{3,2,1,...) custom-call(bf16[32,3072]{1,0:T(8,128)(2,1)} %refs_0_.1, ...), custom_call_target="tpu_custom_call" | custom-call | tf_op jit(solution)/shard_map/pallas_call | solution.py:691
  209.6 103.4 %shard_map.222 = (bf16[4,768,1024]{2,1,0:T(8,128)(2,1)}, f32[768,1024]{1,0:T(8,128)}, bf16[768,1024]{1,0:T(8,128)(2,1)}, bf16[768,1024]{1,0:T(8,128)(2,1)}, bf16...) custom-call(bf16[768,1024]{1,0:T(8,128)(2,1)} %get-tuple-element.49.refs_0_, ...), custom_call_target="tpu_custom_call" | custom-call | tf_op jit(solution)/shard_map/pallas_call | solution.py:743
  313.0 77.7 %shard_map.223 = (bf16[3,768,1024]{2,1,0:T(8,128)(2,1)}, f32[8,1024]{1,0:T(8,128)}, f32[32,4096]{1,0:T(8,128)}, f32[32,1024]{1,0:T(8,128)}) custom-call(bf16[768,1024]{1,0:T(8,128)(2,1)} %get-tuple-element.48.refs_0_, bf16[4,768,1024]{2,1,0:T(8,128)(2,1)} %get-tuple-element.59.refs_1_, bf16[768,1024]{1,0:T(8,128)(2,1)} %get-tuple-element.60.refs_2_, ...), custom_call_target="tpu_custom_call" | custom-call | tf_op jit(solution)/shard_map/pallas_call | solution.py:743
  390.8 59.4 %shard_map.224 = (bf16[768,1024]{1,0:T(8,128)(2,1)}, f32[24,1024]{1,0:T(8,128)}, f32[32,3072]{1,0:T(8,128)}) custom-call(bf16[768,1024]{1,0:T(8,128)(2,1)} %get-tuple-element.47.refs_0_, bf16[3,768,1024]{2,1,0:T(8,128)(2,1)} %get-tuple-element.69.refs_1_, bf16[4,8,32,3072]{3,2,1,0:T(8,128)(2,1)} %get-tuple-element.70.refs_2_, ...), custom_call_target="tpu_custom_call" | custom-call | tf_op jit(solution)/shard_map/pallas_call | solution.py:743
  450.2 0.9 slice_reduce_fusion
  451.1 1.3 slice_reduce_fusion.1
  453.1 0.5 divide_sqrt_fusion
  453.6 0.9 fusion.1
  454.5 0.6 pad_maximum_fusion.2
  455.1 0.8 dynamic-slice
  455.8 0.6 pad_maximum_fusion.1
  456.4 0.6 dynamic_slice.6
  457.0 0.0 copy-start
  457.0 2.8 copy.40
  459.8 0.0 copy-done
  459.8 0.0 copy-start.3
  459.8 0.0 copy-start.4
  459.8 0.0 copy-start.2
  459.8 1.1 copy.41
  460.9 0.1 copy-done.3
  461.0 0.0 copy-start.1
  461.0 0.7 copy.42
  461.7 0.0 copy-done.4
  461.7 0.7 copy.43
  462.4 0.0 copy-done.2
  462.4 0.8 copy.44
  463.2 0.0 copy-done.1
  463.2 0.8 copy.45
  (5 shorter events, 0.0 us)
Async XLA Ops:
  457.0 2.8 copy-start
  459.8 1.2 copy-start.3
  459.8 2.0 copy-start.4
  459.8 2.6 copy-start.2
  461.0 2.2 copy-start.1
